TPU v7x, 32 devices: a whole 2x2x4 slice. The times are simulated.
32 devices in a mesh: grp: 2 (over y), blk: 16 (over z, x, core).
Axes of the slice: x: 2, y: 2, z: 4, core: 2. Of those that a mesh axis runs over, the one named last changes fastest.
Arguments:
- activations: bfloat16 [2, 4096, 8192], P(None, ('grp', 'blk')), parts along dimension 1, may hold values from -6 to 6
- backprops: bfloat16 [2, 4096, 8192], P(None, ('grp', 'blk')), parts along dimension 1, may hold values from -6 to 6
- out_factors: bfloat16 [2, 384, 8192], P(None, 'blk'), may hold values from -1 to 1
- in_factors: bfloat16 [2, 384, 8192], P(None, 'blk'), may hold values from -1 to 1
- lengths: int32 [2], P('grp'), parts along dimension 0, may hold values from 512 to 2048, as said below
Outputs:
- layer_scores: float32 [2, 2, 12], P(None, 'grp'), parts along dimension 1
There are 2 independent parts, one for each index of `grp`. A program takes and returns all parts, laid end to end along the dimension named above; an argument that names none is the same for every part. Nothing has to cross between parts.
Inputs may be any that keep to these rules, and one draw needn't show every extreme that they name: `lengths`: some sequence has all 2048 tokens used in every draw.
All inputs are finite; a program needn't handle non-finite values.
Results may differ from a plain program's by a relative error of at most 0.0004.
Values may be sent and summed in bfloat16 or wider, within the bound.
No kernel may reach another device: no remote copies, remote signals or barrier semaphores. Data moves between devices by JAX's collectives and lax.ppermute only.
A program may use at most 128 MiB of HBM per device.

v0:
```python
import jax
import jax.numpy as jnp
from jax import lax
from jax.sharding import PartitionSpec as P

RANK = 32
LEN = 2048


def make_scorer(activations, backprops, in_use):
    width_out = backprops.shape[2]

    def scorer(fragment, column_start):
        out_part = fragment[:, :, :width_out]
        in_part = fragment[:, :, width_out:]
        proj_out = jnp.einsum(
            "ltd,lkd->ltk", backprops, out_part, preferred_element_type=jnp.float32
        )
        proj_in = jnp.einsum(
            "lte,lke->ltk", activations, in_part, preferred_element_type=jnp.float32
        )
        return jnp.einsum("ltk,t->lk", proj_out * proj_in, in_use)

    return scorer


def shards(activations, backprops, out_factors, in_factors, lengths):
    tokens_here = activations.shape[1]
    seq_count = lengths.shape[0]
    device = lax.axis_index("blk")
    first_token = device * tokens_here
    sequence = first_token // LEN
    position = first_token % LEN + jnp.arange(tokens_here, dtype=jnp.int32)
    select = jnp.arange(seq_count, dtype=jnp.int32) == sequence
    limit = jnp.sum(jnp.where(select, lengths, 0))
    in_use = (position < limit).astype(jnp.float32)
    select_rows = select.astype(jnp.float32)
    factors = jnp.concatenate([out_factors, in_factors], axis=2)
    scorer = make_scorer(activations, backprops, in_use)
    partial_value = scorer(lax.all_gather(factors, "blk", axis=1, tiled=True), jnp.int32(0))
    per_query = partial_value.reshape(partial_value.shape[0], -1, RANK).sum(axis=2)
    return lax.psum(per_query[:, None, :] * select_rows[None, :, None], "blk")


def solution(mesh):
    placed = (
        P(None, ("grp", "blk"), None),
        P(None, ("grp", "blk"), None),
        P(None, "blk", None),
        P(None, "blk", None),
        P("grp"),
    )
    return jax.shard_map(
        shards, mesh=mesh, in_specs=placed, out_specs=P(None, "grp", None), check_vma=False
    )
```

profile of v0, /device:TPU:0, one launch (start us, length us, event | category | flops | bytes accessed | tf_op | source)
XLA Modules:
  0.0 197.8 jit_solution(15061462229116488321)
XLA Ops:
  6.5 0.0 all-gather.2.cloned.1.call-start
  6.5 2.7 %pad_maximum_fusion = bf16[2,24,16384]{2,1,0:T(8,128)(2,1)} fusion(bf16[2,24,8192]{2,1,0:T(8,128)(2,1)} %param.8, bf16[2,24,8192]{2,1,0:T(8,128)(2,1)} %param.7), kind=kLoop, calls=%fused_computation.4 | loop fusion | flops 3145728 | bytes 3145728 | tf_op jit(solution)/shard_map/concatenate | solution.py:38
  9.2 0.0 all-gather.2.cloned.1.call-update
  9.9 130.7 %all-gather.2.cloned.1.call-done = bf16[2,384,16384]{2,1,0:T(8,128)(2,1)} async-done(((bf16[2,24,16384]{2,1,0:T(8,128)(2,1)}), bf16[2,384,16384]{2,1,0:T(8,128)(2,1)}) %all-gather.2.cloned.1.call-update) | async-done | bytes 25165840 | tf_op jit(solution)/shard_map/all_gather | solution.py:40
  140.7 7.6 %fusion = f32[2,384,128]{2,1,0:T(8,128)S(1)} fusion(bf16[2,128,8192]{2,1,0:T(8,128)(2,1)} %param.5, bf16[2,384,16384]{2,1,0:T(8,128)(2,1)} %all-gather.2.cloned.1.call-done), kind=kOutput, calls=%fused_computation | convolution fusion | flops 1610612736 | bytes 17170432 | tf_op jit(solution)/shard_map/lte,lke->ltk/dot_general | solution.py:19
  148.3 9.3 %fusion.11 = f32[1,2,384]{2,0,1:T(1,128)S(1)} fusion(f32[2,384,128]{2,1,0:T(8,128)S(1)} %fusion, bf16[2,128,8192]{2,1,0:T(8,128)(2,1)} %param.6, bf16[2,384,16384]{2,1,0:T(8,128)(2,1)} %all-gather.2.cloned.1.call-done, s32[]{:T(128)} %bitcast.2, s32[]{:T(128)S(6)} %select_n.15), kind=kOutput, calls=%fused_computation.7 | convolution fusion | flops 1610907904 | bytes 17174020 | tf_op jit(solution)/shard_map/ltk,t->lk/dot_general | solution.py:22
  157.6 0.1 reshape.21
  157.7 0.1 reduce_sum.16
  157.8 33.2 %psum.7 = f32[2,1,12]{2,0,1:T(2,128)} all-reduce(f32[2,1,12]{2,0,1:T(2,128)S(1)} %multiply_bitcast_fusion), channel_id=1, replica_groups=mesh['grp'=2,'blk'=16] {'blk'}, use_global_device_ids=true, to_apply=%region_1.2 | all-reduce | flops 24 | bytes 192 | tf_op jit(solution)/shard_map/psum | solution.py:42
  (2 shorter events, 0.0 us)
Async XLA Ops:
  6.5 134.1 %all-gather.2.cloned.1.call-start = ((), (), s32[]{:S(2)}) async-start(), calls=%async_computation | async-start | bytes 26738688 | tf_op jit(solution)/shard_map/all_gather | solution.py:40
Sparse Core Ops, SparseCore 0:
  9.4 131.2 all-gather.1
where the time goes:
time: 198 us
  waiting for transfers between devices  131 us (66%)
  blocking collectives  33.2 us (17%)
  matrix products  16.9 us (9%)
  between operations  14.1 us (7%)
  other arithmetic  2.8 us (1%)
    all_gather x1, waiting for transfers between devices, shards(): lax.all_gather(factors, 'blk', axis=1, tiled=True)  131 us
    psum x1, blocking collectives, shards(): return lax.psum(per_query[:, None, :] * select_rows[None, :, None], 'blk')  33.2 us
    dot_general x1, matrix products, scorer(): return jnp.einsum('ltk,t->lk', proj_out * proj_in, in_use)  9.29 us
    dot_general x1, matrix products, scorer(): jnp.einsum('lte,lke->ltk', activations, in_part, preferred_element_type=j...  7.61 us
  transfers between devices with their start and end apart: 1, of which 1 were waited for; matrix products, arithmetic and copies ran while one was open for 0% of the time, Pallas kernels for 0%

commit v1 on v0

v1 whole, which is shorter than its diff:
```python
import jax
import jax.numpy as jnp
from jax import lax
from jax.experimental import pallas as pl
from jax.experimental.pallas import tpu as pltpu
from jax.sharding import PartitionSpec as P

RANK = 32
LEN = 2048


def chip_ring(chips):
    return list(range(0, chips, 2)) + list(range(chips - 1, 0, -2))


def project(factors, tokens):
    return lax.dot_general(
        factors, tokens, (((1,), (1,)), ((), ())), preferred_element_type=jnp.float32
    )


def move(sources, targets, after=()):
    count = len(sources)
    moves, shapes = [], []
    for t, ranges in enumerate(targets):
        offset = 0
        for s, layer, start, stop in ranges:
            moves.append((t, s, layer, start, stop, offset))
            offset += stop - start
        lead = sources[s].shape[:2] if layer is None else sources[s].shape[1:2]
        shapes.append(jax.ShapeDtypeStruct((*lead, offset), sources[s].dtype))

    def kernel(*refs):
        ins, outs, sems = refs[:count], refs[count + len(after) : -1], refs[-1]
        me = lax.axis_index("grp")
        copies = []
        for k, (t, s, layer, start, stop, offset) in enumerate(moves):
            columns, place = pl.ds(start, stop - start), pl.ds(offset, stop - start)
            if layer is None:
                source, target = ins[s].at[:, :, columns], outs[t].at[:, :, place]
            else:
                row = me if layer == "mine" else 1 - me
                source, target = ins[s].at[row, :, columns], outs[t].at[:, place]
            copies.append(pltpu.make_async_copy(source, target, sems.at[k]))
            copies[-1].start()
        for copy in copies:
            copy.wait()

    anywhere = pl.BlockSpec(memory_space=pl.ANY)
    return pl.pallas_call(
        kernel,
        out_shape=shapes,
        in_specs=[anywhere] * (count + len(after)),
        out_specs=[pl.BlockSpec(memory_space=pltpu.VMEM)] * len(shapes),
        scratch_shapes=[pltpu.SemaphoreType.DMA((len(moves),))],
        compiler_params=pltpu.CompilerParams(vmem_limit_bytes=16 * 2**20),
    )(*sources, *after)


def cuts(total, parts):
    edges = [0]
    for k in range(1, parts):
        edges.append(total * 2 * k // (2 * parts - 1) // 128 * 128)
    return edges + [total]


def solution(mesh):
    blk = mesh.shape["blk"]
    chips = blk // 2
    full = (chips - 1) // 2
    order = chip_ring(chips)
    forward, backward = [], []
    for core in range(2):
        for k in range(chips):
            a = order[k] * 2 + core
            b = order[(k + 1) % chips] * 2 + core
            forward.append((a, b))
            backward.append((b, a))
    place = [0] * chips
    for k, chip in enumerate(order):
        place[chip] = k

    def swap_core(x):
        return lax.ppermute(x, "blk", [(i, i ^ 1) for i in range(blk)])

    def swap_grp(x):
        return lax.ppermute(x, "grp", [(0, 1), (1, 0)])

    def gather(piece, halves, chunks):
        ahead = back = piece
        got, tokens, swapped, state = [piece], [], [], ()
        for step in range(full + 1):
            send = (ahead, back) if step < full else halves(ahead, back)
            chunk = chunks(step)
            if chunk is not None:
                send = lax.optimization_barrier((*send, chunk, *state))
                chunk = send[2]
            ahead = lax.ppermute(send[0], "blk", forward)
            back = lax.ppermute(send[1], "blk", backward)
            state = (ahead, back)
            if chunk is not None:
                if tokens:
                    swapped.append(swap_core(tokens[-1]))
                tokens.append(swap_grp(chunk))
                state += (tokens[-1], *swapped[-1:])
            if step < full:
                got += [ahead, back]
            yield state
        swapped.append(swap_core(tokens[-1]))
        yield got, (ahead, back), tokens, swapped

    def shards(activations, backprops, out_factors, in_factors, lengths):
        tokens_here = activations.shape[1]
        width = backprops.shape[2]
        depth = activations.shape[2]
        cut = depth * 9 // 16
        packed = width + cut
        columns = out_factors.shape[1]
        seq_count = lengths.shape[0]
        me = lax.axis_index("grp")
        device = lax.axis_index("blk")

        def layer_of(x, layer):
            return lax.dynamic_index_in_dim(x, layer, 0, keepdims=False)

        home_rate, rate = 2 * (depth - cut), packed
        near = packed * rate // (rate + home_rate) // 128 * 128
        parts = min(full + 1, 4)
        near_edges = cuts(near, parts)
        far_edges = [near + e for e in cuts(packed - near, parts)]

        def packing(out_source, in_source, layer, start, stop):
            ranges = []
            if start < width:
                ranges.append((out_source, layer, start, min(stop, width)))
            if stop > width:
                ranges.append((in_source, layer, max(start - width, 0), stop - width))
            return ranges

        def away_part(edges, k):
            return packing(1, 0, "other", edges[k], edges[k + 1])

        tokens = (activations, backprops)
        home_piece, far_first = move(
            (activations, backprops, in_factors),
            [[(2, None, cut, depth)], away_part(far_edges, 0)],
        )
        piece, near_first, far_second = move(
            (*tokens, in_factors, out_factors),
            [
                packing(3, 2, "mine", 0, packed),
                away_part(near_edges, 0),
                away_part(far_edges, 1),
            ],
            after=(home_piece,),
        )
        later = {}
        home_ring = gather(
            home_piece,
            lambda a, b: (a[:1], b[1:]),
            lambda k: [far_first, far_second, *later.get("far", ())][k] if k < parts else None,
        )
        state = next(home_ring)
        rest = [away_part(near_edges, 1)]
        for k in range(2, parts):
            rest += [away_part(far_edges, k), away_part(near_edges, k)]
        rest += [packing(1, 0, "mine", 0, packed), [(0, None, cut, depth)]]
        moved = move(tokens, rest, after=state[:1])
        later["near"], later["far"] = moved[0:-2:2], moved[1:-2:2]
        mine, home_tokens = moved[-2:]
        for state in home_ring:
            pass
        home_got, home_last, far_away, far_sib = state
        home_got.append(jnp.concatenate(home_last, axis=0))
        middle = packed // 2
        for state in gather(
            piece,
            lambda a, b: (a[:, :middle], b[:, middle:]),
            lambda k: [near_first, *later["near"]][k] if k < parts else None,
        ):
            pass
        got, last, near_away, near_sib = state
        got.append(jnp.concatenate(last, axis=1))

        mine_sib = swap_core(mine)
        home_sib = swap_core(home_tokens)
        away = jnp.concatenate(near_away + far_away, axis=1)
        away_sib = jnp.concatenate(near_sib + far_sib, axis=1)
        other_lengths = swap_grp(lengths)

        home_factors = jnp.concatenate(home_got, axis=1)

        def home(tokens):
            return jnp.einsum(
                "lkd,ltd->lkt", home_factors, tokens, preferred_element_type=jnp.float32
            )

        home = jnp.concatenate([home(home_tokens), home(home_sib)], axis=2)
        home_mine = layer_of(home, me)
        home_away = swap_grp(layer_of(home, 1 - me))

        factors = jnp.concatenate(got, axis=0)
        first = (device // 2) * 2 * tokens_here
        sequence = first // LEN
        select = jnp.arange(seq_count, dtype=jnp.int32) == sequence
        odd = device % 2
        start = first % LEN

        def score(own, sib, beyond, limits):
            limit = jnp.sum(jnp.where(select, limits, 0))
            total = 0.0
            for k, tokens in enumerate((own, sib)):
                proj_out = project(factors[:, :width], tokens[:, :width])
                proj_in = project(factors[:, width:], tokens[:, width:])
                proj_in += beyond[:, k * tokens_here : (k + 1) * tokens_here]
                position = (
                    start
                    + (odd ^ k) * tokens_here
                    + jnp.arange(tokens_here, dtype=jnp.int32)
                )
                in_use = (position < limit).astype(jnp.float32)
                total += jnp.sum(proj_out * proj_in * in_use[None, :], axis=1)
            return total

        per_column = jnp.stack(
            [
                score(mine, mine_sib, home_mine, lengths),
                score(away, away_sib, home_away, other_lengths),
            ]
        )

        at = jnp.asarray(place, jnp.int32)[device // 2]
        steps = [0]
        for k in range(1, full + 1):
            steps += [-k, k]
        steps.append(chips // 2)
        shard_chip = jnp.asarray(order, jnp.int32)[
            (at + jnp.asarray(steps, jnp.int32)) % chips
        ]
        first_column = (shard_chip * 2 + odd) * columns
        column = first_column[:, None] + jnp.arange(columns, dtype=jnp.int32)[None, :]
        query = column.reshape(-1) // RANK
        queries = columns * blk // RANK
        hit = (query[:, None] == jnp.arange(queries)[None, :]).astype(jnp.float32)
        per_query = jnp.sum(per_column[:, :, None] * hit[None], axis=1)

        other = swap_grp(per_query[1])
        rows = jnp.arange(2)[:, None] == me
        value = jnp.where(rows, per_query[0][None], other[None])
        value = value[:, None, :] * select.astype(jnp.float32)[None, :, None]
        if blk & (blk - 1):
            return lax.psum(value, "blk")
        bit = 1
        while bit < blk:
            value = value + lax.ppermute(value, "blk", [(i, i ^ bit) for i in range(blk)])
            bit *= 2
        return value

    placed = (
        P(None, ("grp", "blk"), None),
        P(None, ("grp", "blk"), None),
        P(None, "blk", None),
        P(None, "blk", None),
        P("grp"),
    )
    return jax.shard_map(
        shards, mesh=mesh, in_specs=placed, out_specs=P(None, "grp", None), check_vma=False
    )
```

time: 198 us -> 148 us (0.75)
  waiting for transfers between devices: 131 us -> 83.1 us
  starting transfers between devices: 0.01 us -> 34.8 us
  blocking collectives: 33.2 us -> 0 us
  local copies, waits for them, and re-layouts: 0.08 us -> 15.4 us
  between operations: 14.1 us -> 1.7 us
  matrix products: 16.9 us -> 9.48 us
    all_gather x1 -> x0, waiting for transfers between devices: 131 us -> none  [shards(): lax.all_gather(factors, 'blk', axis=1, tiled=True)]
    ppermute x0 -> x41, waiting for transfers between devices: none -> 83.1 us  [the longest x8 32.9 us: gather(): ahead = lax.ppermute(send[0], 'blk', forward)]
    ppermute x0 -> x41, starting transfers between devices: none -> 34.8 us  [the longest x8 14.8 us: gather(): ahead = lax.ppermute(send[0], 'blk', forward)]
    psum x1 -> x0, blocking collectives: 33.2 us -> none  [shards(): return lax.psum(per_query[:, None, :] * select_rows[None, :, None], 'blk')]
    unnamed x0 -> x36, local copies, waits for them, and re-layouts: none -> 13.9 us
    dot_general x2 -> x10, matrix products: 16.9 us -> 9.48 us  [the longest x8 7.75 us: project(): lax.dot_general(factors, tokens, (((1,), (1,)), ((), ())), preferred_elem...]
    concatenate x1 -> x2, other arithmetic: 2.7 us -> 0.07 us  [the longest x1 0.04 us: shards(): factors = jnp.concatenate(got, axis=0)]
  transfers between devices with their start and end apart: 1 -> 41, of which waited for: 1 -> 23; matrix products, arithmetic and copies ran while one was open for 0% -> 9% of each run, Pallas kernels for 0% -> 1%
where the time goes in v1:
time: 148 us; the launch traced here: 147 us
  waiting for transfers between devices  83.1 us (56%)
  starting transfers between devices  34.8 us (24%)
  local copies, waits for them, and re-layouts  15.4 us (10%)
  matrix products  9.48 us (6%)
  other arithmetic  1.78 us (1%)
  between operations  1.7 us (1%)
    ppermute x8, waiting for transfers between devices, gather(): ahead = lax.ppermute(send[0], 'blk', forward)  32.9 us
    ppermute x11, waiting for transfers between devices, swap_grp(): return lax.ppermute(x, 'grp', [(0, 1), (1, 0)])  31.3 us
    ppermute x8, starting transfers between devices, gather(): ahead = lax.ppermute(send[0], 'blk', forward)  14.8 us
    unnamed x36, local copies, waits for them, and re-layouts  13.9 us
    ppermute x11, starting transfers between devices, swap_grp(): return lax.ppermute(x, 'grp', [(0, 1), (1, 0)])  12.3 us
    ppermute x8, waiting for transfers between devices, gather(): back = lax.ppermute(send[1], 'blk', backward)  10.1 us
    ppermute x4, waiting for transfers between devices, shards(): lax.ppermute(value, 'blk', [(i, i ^ bit) for i in range(blk)])  8.67 us
    dot_general x8, matrix products, project(): lax.dot_general(factors, tokens, (((1,), (1,)), ((), ())), preferred_elem...  7.75 us
  transfers between devices with their start and end apart: 41, of which 23 were waited for; matrix products, arithmetic and copies ran while one was open for 9% of the time, Pallas kernels for 1%

profile of v1, /device:TPU:0, one launch (start us, length us, event | category | flops | bytes accessed | tf_op | source)
XLA Modules:
  0.0 147.2 jit_solution(10518341853373369214)
XLA Ops:
  0.0 2.2 %copy-done = bf16[2,128,8192]{2,1,0:T(8,128)(2,1)S(1)} copy-done((bf16[2,128,8192]{2,1,0:T(8,128)(2,1)S(1)}, bf16[2,128,8192]{2,1,0:T(8,128)(2,1)}, u32[]{:S(2)}) %copy-start) | copy-done | bytes 4194328
  2.2 2.2 %copy-done.2 = bf16[2,128,8192]{2,1,0:T(8,128)(2,1)S(1)} copy-done((bf16[2,128,8192]{2,1,0:T(8,128)(2,1)S(1)}, bf16[2,128,8192]{2,1,0:T(8,128)(2,1)}, u32[]{:S(2)}) %copy-start.2) | copy-done | bytes 4194328
  4.4 1.1 copy-done.4
  5.6 3.1 %collective-permute-start.2 = (bf16[2,24,3584]{2,1,0:T(8,128)(2,1)S(1)}, bf16[2,24,3584]{2,1,0:T(8,128)(2,1)S(1)}, u32[]{:S(2)}, u32[]{:S(2)}) collective-permute-start(bf16[2,24,3584]{2,1,0:T(8,128)(2,1)S(1)} %get-tuple-element.61.refs_4_), channel_id=1, source_target_pairs={{0,4},{4,8},{8,12},{12,14},{14,10},{10,6},{6,2},{2,0},{1,5},{5,9},... | collective-permute-start | bytes 1032200 | tf_op jit(solution)/shard_map/ppermute | solution.py:98
  8.7 1.5 %collective-permute-start.15 = (bf16[128,1280]{1,0:T(8,128)(2,1)S(1)}, bf16[128,1280]{1,0:T(8,128)(2,1)}, u32[]{:S(2)}, u32[]{:S(2)}) collective-permute-start(bf16[128,1280]{1,0:T(8,128)(2,1)S(1)} %get-tuple-element.63), channel_id=1, source_target_pairs={{0,16},{16,0},{1,17},{17,1},{2,18},{18,2},{3,19},{19,3},{4,20},{20... | collective-permute-start | bytes 983048 | tf_op jit(solution)/shard_map/ppermute | solution.py:87
  11.1 2.0 %collective-permute-start.31 = (s32[1]{0:T(128)}, s32[1]{0:T(128)}, u32[]{:S(2)}, u32[]{:S(2)}) collective-permute-start(s32[1]{0:T(128)} %param.12), channel_id=1, source_target_pairs={{0,16},{16,0},{1,17},{17,1},{2,18},{18,2},{3,19},{19,3},{4,20},{20... | collective-permute-start | bytes 20 | tf_op jit(solution)/shard_map/ppermute | solution.py:87
  13.1 0.8 constant_dynamic-update-slice_fusion.13
  13.8 0.9 constant_dynamic-update-slice_fusion.6
  15.4 0.6 dynamic_slice.12
  16.0 0.6 compare_select_fusion
  16.7 0.6 gather_fusion
  17.5 13.1 %collective-permute-done.31 = s32[1]{0:T(128)} collective-permute-done((s32[1]{0:T(128)}, s32[1]{0:T(128)}, u32[]{:S(2)}, u32[]{:S(2)}) %collective-permute-start.31) | collective-permute-done | bytes 36 | tf_op jit(solution)/shard_map/ppermute | solution.py:87
  30.7 1.6 %collective-permute-start = (bf16[24,12800]{1,0:T(8,128)(2,1)S(1)}, bf16[24,12800]{1,0:T(8,128)(2,1)S(1)}, u32[]{:S(2)}, u32[]{:S(2)}) collective-permute-start(bf16[24,12800]{1,0:T(8,128)(2,1)S(1)} %get-tuple-element.45), channel_id=1, source_target_pairs={{0,4},{4,8},{8,12},{12,14},{14,10},{10,6},{6,2},{2,0},{1,5},{5,9},... | collective-permute-start | bytes 1843208 | tf_op jit(solution)/shard_map/ppermute | solution.py:98
  33.4 1.6 %collective-permute-start.18 = (bf16[128,1280]{1,0:T(8,128)(2,1)S(1)}, bf16[128,1280]{1,0:T(8,128)(2,1)S(1)}, u32[]{:S(2)}, u32[]{:S(2)}) collective-permute-start(bf16[128,1280]{1,0:T(8,128)(2,1)S(1)} %get-tuple-element.67), channel_id=1, source_target_pairs={{0,16},{16,0},{1,17},{17,1},{2,18},{18,2},{3,19},{19,3},{4,20},{20... | collective-permute-start | bytes 983048 | tf_op jit(solution)/shard_map/ppermute | solution.py:87
  35.0 0.8 constant_dynamic-update-slice_fusion.12
  35.7 2.2 %copy-done.1 = bf16[2,128,8192]{2,1,0:T(8,128)(2,1)S(1)} copy-done((bf16[2,128,8192]{2,1,0:T(8,128)(2,1)S(1)}, bf16[2,128,8192]{2,1,0:T(8,128)(2,1)}, u32[]{:S(2)}) %copy-start.1) | copy-done | bytes 4194328
  37.9 2.2 %copy-done.3 = bf16[2,128,8192]{2,1,0:T(8,128)(2,1)S(1)} copy-done((bf16[2,128,8192]{2,1,0:T(8,128)(2,1)S(1)}, bf16[2,128,8192]{2,1,0:T(8,128)(2,1)}, u32[]{:S(2)}) %copy-start.3) | copy-done | bytes 4194328
  40.1 0.6 shard_map.84
  40.8 1.1 copy-done.7
  41.9 3.0 %collective-permute-done = bf16[24,12800]{1,0:T(8,128)(2,1)S(1)} collective-permute-done((bf16[24,12800]{1,0:T(8,128)(2,1)S(1)}, bf16[24,12800]{1,0:T(8,128)(2,1)S(1)}, u32[]{:S(2)}, u32[]{:S(2)}) %collective-permute-start) | collective-permute-done | bytes 614432 | tf_op jit(solution)/shard_map/ppermute | solution.py:98
  44.9 1.6 %collective-permute-start.16 = (bf16[2,24,3584]{2,1,0:T(8,128)(2,1)S(1)}, bf16[2,24,3584]{2,1,0:T(8,128)(2,1)S(1)}, u32[]{:S(2)}, u32[]{:S(2)}) collective-permute-start(bf16[2,24,3584]{2,1,0:T(8,128)(2,1)S(1)} %collective-permute-done.2.refs_2_), channel_id=1, source_target_pairs={{0,4},{4,8},{8,12},{12,14},{14,10},{10,6},{6,2},{2,0},{1,5},{5,9},... | collective-permute-start | bytes 1032200 | tf_op jit(solution)/shard_map/ppermute | solution.py:98
  48.0 4.4 %collective-permute-done.16 = bf16[2,24,3584]{2,1,0:T(8,128)(2,1)S(1)} collective-permute-done((bf16[2,24,3584]{2,1,0:T(8,128)(2,1)S(1)}, bf16[2,24,3584]{2,1,0:T(8,128)(2,1)S(1)}, u32[]{:S(2)}, u32[]{:S(2)}) %collective-permute-start.16) | collective-permute-done | bytes 344096 | tf_op jit(solution)/shard_map/ppermute | solution.py:98
  52.4 1.8 %collective-permute-done.17 = bf16[2,24,3584]{2,1,0:T(8,128)(2,1)S(1)} collective-permute-done((bf16[2,24,3584]{2,1,0:T(8,128)(2,1)S(1)}, bf16[2,24,3584]{2,1,0:T(8,128)(2,1)S(1)}, u32[]{:S(2)}, u32[]{:S(2)}) %collective-permute-start.17) | collective-permute-done | bytes 344096 | tf_op jit(solution)/shard_map/ppermute | solution.py:99
  54.2 1.6 %collective-permute-start.20 = (bf16[2,24,3584]{2,1,0:T(8,128)(2,1)S(1)}, bf16[2,24,3584]{2,1,0:T(8,128)(2,1)S(1)}, u32[]{:S(2)}, u32[]{:S(2)}) collective-permute-start(bf16[2,24,3584]{2,1,0:T(8,128)(2,1)S(1)} %collective-permute-done.16), channel_id=1, source_target_pairs={{0,4},{4,8},{8,12},{12,14},{14,10},{10,6},{6,2},{2,0},{1,5},{5,9},... | collective-permute-start | bytes 1032200 | tf_op jit(solution)/shard_map/ppermute | solution.py:98
  56.3 1.5 %collective-permute-start.22 = (bf16[128,1280]{1,0:T(8,128)(2,1)S(1)}, bf16[128,1280]{1,0:T(8,128)(2,1)S(1)}, u32[]{:S(2)}, u32[]{:S(2)}) collective-permute-start(bf16[128,1280]{1,0:T(8,128)(2,1)S(1)} %get-tuple-element.71), channel_id=1, source_target_pairs={{0,16},{16,0},{1,17},{17,1},{2,18},{18,2},{3,19},{19,3},{4,20},{20... | collective-permute-start | bytes 983048 | tf_op jit(solution)/shard_map/ppermute | solution.py:87
  57.8 3.6 %collective-permute-done.20 = bf16[2,24,3584]{2,1,0:T(8,128)(2,1)S(1)} collective-permute-done((bf16[2,24,3584]{2,1,0:T(8,128)(2,1)S(1)}, bf16[2,24,3584]{2,1,0:T(8,128)(2,1)S(1)}, u32[]{:S(2)}, u32[]{:S(2)}) %collective-permute-start.20) | collective-permute-done | bytes 344096 | tf_op jit(solution)/shard_map/ppermute | solution.py:98
  61.5 1.6 %collective-permute-done.21 = bf16[2,24,3584]{2,1,0:T(8,128)(2,1)S(1)} collective-permute-done((bf16[2,24,3584]{2,1,0:T(8,128)(2,1)S(1)}, bf16[2,24,3584]{2,1,0:T(8,128)(2,1)S(1)}, u32[]{:S(2)}, u32[]{:S(2)}) %collective-permute-start.21) | collective-permute-done | bytes 344096 | tf_op jit(solution)/shard_map/ppermute | solution.py:99
  63.1 1.7 %collective-permute-start.6 = (bf16[128,2304]{1,0:T(8,128)(2,1)S(1)}, bf16[128,2304]{1,0:T(8,128)(2,1)S(1)}, u32[]{:S(2)}, u32[]{:S(2)}) collective-permute-start(bf16[128,2304]{1,0:T(8,128)(2,1)S(1)} %get-tuple-element.53), channel_id=1, source_target_pairs={{0,16},{16,0},{1,17},{17,1},{2,18},{18,2},{3,19},{19,3},{4,20},{20... | collective-permute-start | bytes 1769480 | tf_op jit(solution)/shard_map/ppermute | solution.py:87
  64.8 2.1 %collective-permute-start.24 = (bf16[1,24,3584]{2,1,0:T(8,128)(2,1)S(1)}, bf16[1,24,3584]{2,1,0:T(8,128)(2,1)S(1)}, u32[]{:S(2)}, u32[]{:S(2)}) collective-permute-start(bf16[1,24,3584]{2,1,0:T(8,128)(2,1)S(1)} %slice.87), channel_id=1, source_target_pairs={{0,4},{4,8},{8,12},{12,14},{14,10},{10,6},{6,2},{2,0},{1,5},{5,9},... | collective-permute-start | bytes 516104 | tf_op jit(solution)/shard_map/ppermute | solution.py:98
  66.9 3.3 %collective-permute-done.24 = bf16[1,24,3584]{2,1,0:T(8,128)(2,1)S(1)} collective-permute-done((bf16[1,24,3584]{2,1,0:T(8,128)(2,1)S(1)}, bf16[1,24,3584]{2,1,0:T(8,128)(2,1)S(1)}, u32[]{:S(2)}, u32[]{:S(2)}) %collective-permute-start.24) | collective-permute-done | bytes 172064 | tf_op jit(solution)/shard_map/ppermute | solution.py:98
  70.2 2.0 %collective-permute-start.4 = (bf16[24,12800]{1,0:T(8,128)(2,1)S(1)}, bf16[24,12800]{1,0:T(8,128)(2,1)S(1)}, u32[]{:S(2)}, u32[]{:S(2)}) collective-permute-start(bf16[24,12800]{1,0:T(8,128)(2,1)S(1)} %collective-permute-done), channel_id=1, source_target_pairs={{0,4},{4,8},{8,12},{12,14},{14,10},{10,6},{6,2},{2,0},{1,5},{5,9},... | collective-permute-start | bytes 1843208 | tf_op jit(solution)/shard_map/ppermute | solution.py:98
  72.3 5.1 %collective-permute-done.6 = bf16[128,2304]{1,0:T(8,128)(2,1)S(1)} collective-permute-done((bf16[128,2304]{1,0:T(8,128)(2,1)S(1)}, bf16[128,2304]{1,0:T(8,128)(2,1)S(1)}, u32[]{:S(2)}, u32[]{:S(2)}) %collective-permute-start.6) | collective-permute-done | bytes 589856 | tf_op jit(solution)/shard_map/ppermute | solution.py:87
  77.4 0.9 fusion.139
  78.2 5.5 %collective-permute-done.4 = bf16[24,12800]{1,0:T(8,128)(2,1)S(1)} collective-permute-done((bf16[24,12800]{1,0:T(8,128)(2,1)S(1)}, bf16[24,12800]{1,0:T(8,128)(2,1)S(1)}, u32[]{:S(2)}, u32[]{:S(2)}) %collective-permute-start.4) | collective-permute-done | bytes 614432 | tf_op jit(solution)/shard_map/ppermute | solution.py:98
  83.7 2.4 %collective-permute-done.5 = bf16[24,12800]{1,0:T(8,128)(2,1)S(1)} collective-permute-done((bf16[24,12800]{1,0:T(8,128)(2,1)S(1)}, bf16[24,12800]{1,0:T(8,128)(2,1)S(1)}, u32[]{:S(2)}, u32[]{:S(2)}) %collective-permute-start.5) | collective-permute-done | bytes 614432 | tf_op jit(solution)/shard_map/ppermute | solution.py:99
  86.1 1.7 %collective-permute-start.8 = (bf16[24,12800]{1,0:T(8,128)(2,1)S(1)}, bf16[24,12800]{1,0:T(8,128)(2,1)S(1)}, u32[]{:S(2)}, u32[]{:S(2)}) collective-permute-start(bf16[24,12800]{1,0:T(8,128)(2,1)S(1)} %collective-permute-done.4), channel_id=1, source_target_pairs={{0,4},{4,8},{8,12},{12,14},{14,10},{10,6},{6,2},{2,0},{1,5},{5,9},... | collective-permute-start | bytes 1843208 | tf_op jit(solution)/shard_map/ppermute | solution.py:98
  88.3 10.8 %collective-permute-done.8 = bf16[24,12800]{1,0:T(8,128)(2,1)S(1)} collective-permute-done((bf16[24,12800]{1,0:T(8,128)(2,1)S(1)}, bf16[24,12800]{1,0:T(8,128)(2,1)S(1)}, u32[]{:S(2)}, u32[]{:S(2)}) %collective-permute-start.8) | collective-permute-done | bytes 614432 | tf_op jit(solution)/shard_map/ppermute | solution.py:98
  99.1 2.0 %collective-permute-done.9 = bf16[24,12800]{1,0:T(8,128)(2,1)S(1)} collective-permute-done((bf16[24,12800]{1,0:T(8,128)(2,1)S(1)}, bf16[24,12800]{1,0:T(8,128)(2,1)S(1)}, u32[]{:S(2)}, u32[]{:S(2)}) %collective-permute-start.9) | collective-permute-done | bytes 614432 | tf_op jit(solution)/shard_map/ppermute | solution.py:99
  101.1 1.2 collective-permute-start.12
  102.3 0.9 collective-permute-start.13
  103.3 3.4 %collective-permute-done.29 = bf16[128,768]{1,0:T(8,128)(2,1)S(1)} collective-permute-done((bf16[128,768]{1,0:T(8,128)(2,1)S(1)}, bf16[128,768]{1,0:T(8,128)(2,1)S(1)}, u32[]{:S(2)}, u32[]{:S(2)}) %collective-permute-start.29) | collective-permute-done | bytes 196640 | tf_op jit(solution)/shard_map/ppermute | solution.py:87
  106.8 2.2 %collective-permute-done.12 = bf16[24,6400]{1,0:T(8,128)(2,1)S(1)} collective-permute-done((bf16[24,6400]{1,0:T(8,128)(2,1)S(1)}, bf16[24,6400]{1,0:T(8,128)(2,1)S(1)}, u32[]{:S(2)}, u32[]{:S(2)}) %collective-permute-start.12) | collective-permute-done | bytes 307232 | tf_op jit(solution)/shard_map/ppermute | solution.py:98
  109.0 2.0 %collective-permute-done.13 = bf16[24,6400]{1,0:T(8,128)(2,1)S(1)} collective-permute-done((bf16[24,6400]{1,0:T(8,128)(2,1)S(1)}, bf16[24,6400]{1,0:T(8,128)(2,1)S(1)}, u32[]{:S(2)}, u32[]{:S(2)}) %collective-permute-start.13) | collective-permute-done | bytes 307232 | tf_op jit(solution)/shard_map/ppermute | solution.py:99
  111.0 1.7 %collective-permute-start.28 = (bf16[128,1280]{1,0:T(8,128)(2,1)S(1)}, bf16[128,1280]{1,0:T(8,128)(2,1)S(1)}, u32[]{:S(2)}, u32[]{:S(2)}) collective-permute-start(bf16[128,1280]{1,0:T(8,128)(2,1)S(1)} %get-tuple-element.75), channel_id=1, source_target_pairs={{0,16},{16,0},{1,17},{17,1},{2,18},{18,2},{3,19},{19,3},{4,20},{20... | collective-permute-start | bytes 983048 | tf_op jit(solution)/shard_map/ppermute | solution.py:87
  112.8 0.9 fusion.140
  114.1 0.6 fusion.48
  114.7 1.1 fusion.108
  115.8 5.8 %collective-permute-done.28 = bf16[128,1280]{1,0:T(8,128)(2,1)S(1)} collective-permute-done((bf16[128,1280]{1,0:T(8,128)(2,1)S(1)}, bf16[128,1280]{1,0:T(8,128)(2,1)S(1)}, u32[]{:S(2)}, u32[]{:S(2)}) %collective-permute-start.28) | collective-permute-done | bytes 327712 | tf_op jit(solution)/shard_map/ppermute | solution.py:87
  121.5 2.1 %collective-permute-done.30 = f32[192,256]{1,0:T(8,128)S(1)} collective-permute-done((f32[192,256]{1,0:T(8,128)S(1)}, f32[192,256]{1,0:T(8,128)S(1)}, u32[]{:S(2)}, u32[]{:S(2)}) %collective-permute-start.30) | collective-permute-done | bytes 196640 | tf_op jit(solution)/shard_map/ppermute | solution.py:87
  123.6 1.6 %fusion.63 = f32[192,128]{1,0:T(8,128)S(1)} fusion(bf16[128,768]{1,0:T(8,128)(2,1)S(1)} %collective-permute-done.29, bf16[128,1280]{1,0:T(8,128)(2,1)S(1)} %collective-permute-done.22, bf16[128,1280]{1,0:T(8,128)(2,1)S(1)} %collective-permute-done.18, bf16[128,1280]{1,0:T(8,128)(2,1)} %collective-permute-done.15, ...), kind=kOutput, calls=%fused_computation.52 | convolution fusion | flops 231235584 | bytes 3145728 | tf_op jit(solution)/shard_map/dot_general | solution.py:17
  125.2 1.1 fusion.118
  126.3 0.6 fusion.58
  127.0 1.1 fusion.113
  128.1 0.6 fusion.53
  128.7 1.1 fusion.123
  130.1 1.8 %collective-permute-start.36 = (f32[12]{0:T(128)S(1)}, f32[12]{0:T(128)S(1)}, u32[]{:S(2)}, u32[]{:S(2)}) collective-permute-start(f32[12]{0:T(128)S(1)} %get-tuple-element.78), channel_id=1, source_target_pairs={{0,16},{16,0},{1,17},{17,1},{2,18},{18,2},{3,19},{19,3},{4,20},{20... | collective-permute-start | bytes 152 | tf_op jit(solution)/shard_map/ppermute | solution.py:87
  131.9 1.8 %collective-permute-done.36 = f32[12]{0:T(128)S(1)} collective-permute-done((f32[12]{0:T(128)S(1)}, f32[12]{0:T(128)S(1)}, u32[]{:S(2)}, u32[]{:S(2)}) %collective-permute-start.36) | collective-permute-done | bytes 80 | tf_op jit(solution)/shard_map/ppermute | solution.py:87
  133.8 1.1 collective-permute-done.37
  135.0 3.6 %collective-permute-done.38 = f32[2,1,12]{2,1,0:T(1,128)S(1)} collective-permute-done((f32[2,1,12]{2,1,0:T(1,128)S(1)}, f32[2,1,12]{2,1,0:T(1,128)S(1)}, u32[]{:S(2)}, u32[]{:S(2)}) %collective-permute-start.38) | collective-permute-done | bytes 128 | tf_op jit(solution)/shard_map/ppermute | solution.py:255
  138.6 2.0 %collective-permute-start.39 = (f32[2,1,12]{2,1,0:T(1,128)S(1)}, f32[2,1,12]{2,1,0:T(1,128)S(1)}, u32[]{:S(2)}, u32[]{:S(2)}) collective-permute-start(f32[2,1,12]{2,1,0:T(1,128)S(1)} %fusion.146), channel_id=1, source_target_pairs={{0,4},{1,5},{2,6},{3,7},{4,0},{5,1},{6,2},{7,3},{8,12},{9,13},{10,... | collective-permute-start | bytes 296 | tf_op jit(solution)/shard_map/ppermute | solution.py:255
  140.6 1.6 %collective-permute-done.39 = f32[2,1,12]{2,1,0:T(1,128)S(1)} collective-permute-done((f32[2,1,12]{2,1,0:T(1,128)S(1)}, f32[2,1,12]{2,1,0:T(1,128)S(1)}, u32[]{:S(2)}, u32[]{:S(2)}) %collective-permute-start.39) | collective-permute-done | bytes 128 | tf_op jit(solution)/shard_map/ppermute | solution.py:255
  142.2 2.1 %collective-permute-start.40 = (f32[2,1,12]{2,1,0:T(1,128)S(1)}, f32[2,1,12]{2,1,0:T(1,128)S(1)}, u32[]{:S(2)}, u32[]{:S(2)}) collective-permute-start(f32[2,1,12]{2,1,0:T(1,128)S(1)} %add.190), channel_id=1, source_target_pairs={{0,8},{1,9},{2,10},{3,11},{4,12},{5,13},{6,14},{7,15},{8,0},{9,1},... | collective-permute-start | bytes 296 | tf_op jit(solution)/shard_map/ppermute | solution.py:255
  144.3 2.4 %collective-permute-done.40 = f32[2,1,12]{2,1,0:T(1,128)S(1)} collective-permute-done((f32[2,1,12]{2,1,0:T(1,128)S(1)}, f32[2,1,12]{2,1,0:T(1,128)S(1)}, u32[]{:S(2)}, u32[]{:S(2)}) %collective-permute-start.40) | collective-permute-done | bytes 128 | tf_op jit(solution)/shard_map/ppermute | solution.py:255
  146.7 0.6 add.191
  (96 shorter events, 5.3 us)
Async XLA Ops:
  0.0 2.2 %copy-start = (bf16[2,128,8192]{2,1,0:T(8,128)(2,1)S(1)}, bf16[2,128,8192]{2,1,0:T(8,128)(2,1)}, u32[]{:S(2)}) copy-start(bf16[2,128,8192]{2,1,0:T(8,128)(2,1)} %refs_0_.5) | copy-start | bytes 12582916
  2.2 2.2 %copy-start.2 = (bf16[2,128,8192]{2,1,0:T(8,128)(2,1)S(1)}, bf16[2,128,8192]{2,1,0:T(8,128)(2,1)}, u32[]{:S(2)}) copy-start(bf16[2,128,8192]{2,1,0:T(8,128)(2,1)} %refs_1_.5) | copy-start | bytes 12582916
  4.4 1.1 copy-start.4
  5.5 5.2 %copy-start.5 = (bf16[2,24,8192]{2,1,0:T(8,128)(2,1)S(1)}, bf16[2,24,8192]{2,1,0:T(8,128)(2,1)}, u32[]{:S(2)}) copy-start(bf16[2,24,8192]{2,1,0:T(8,128)(2,1)} %refs_3_.1) | copy-start | bytes 2359300
  5.6 9.8 %copy-start.10 = (s32[8]{0:T(128)S(1)}, s32[8]{0:T(128)}, u32[]{:S(2)}) copy-start(s32[8]{0:T(128)} %constant.112.clone) | copy-start | bytes 100
  5.6 10.4 %copy-start.9 = (s32[8]{0:T(128)S(1)}, s32[8]{0:T(128)}, u32[]{:S(2)}) copy-start(s32[8]{0:T(128)} %constant.114.clone) | copy-start | bytes 100
  5.6 11.0 %copy-start.6 = (s32[8]{0:T(128)S(1)}, s32[8]{0:T(128)}, u32[]{:S(2)}) copy-start(s32[8]{0:T(128)} %constant.113.clone) | copy-start | bytes 100
  5.6 27.7 %collective-permute-start.2 = (bf16[2,24,3584]{2,1,0:T(8,128)(2,1)S(1)}, bf16[2,24,3584]{2,1,0:T(8,128)(2,1)S(1)}, u32[]{:S(2)}, u32[]{:S(2)}) collective-permute-start(bf16[2,24,3584]{2,1,0:T(8,128)(2,1)S(1)} %get-tuple-element.61.refs_4_), channel_id=1, source_target_pairs={{0,4},{4,8},{8,12},{12,14},{14,10},{10,6},{6,2},{2,0},{1,5},{5,9},... | collective-permute-start | bytes 1032200 | tf_op jit(solution)/shard_map/ppermute | solution.py:98
  8.7 24.1 %collective-permute-start.15 = (bf16[128,1280]{1,0:T(8,128)(2,1)S(1)}, bf16[128,1280]{1,0:T(8,128)(2,1)}, u32[]{:S(2)}, u32[]{:S(2)}) collective-permute-start(bf16[128,1280]{1,0:T(8,128)(2,1)S(1)} %get-tuple-element.63), channel_id=1, source_target_pairs={{0,16},{16,0},{1,17},{17,1},{2,18},{18,2},{3,19},{19,3},{4,20},{20... | collective-permute-start | bytes 983048 | tf_op jit(solution)/shard_map/ppermute | solution.py:87
  10.2 23.1 %collective-permute-start.14 = (bf16[2,24,3584]{2,1,0:T(8,128)(2,1)S(1)}, bf16[2,24,3584]{2,1,0:T(8,128)(2,1)S(1)}, u32[]{:S(2)}, u32[]{:S(2)}) collective-permute-start(bf16[2,24,3584]{2,1,0:T(8,128)(2,1)S(1)} %get-tuple-element.61.refs_4_), channel_id=1, source_target_pairs={{4,0},{8,4},{12,8},{14,12},{10,14},{6,10},{2,6},{0,2},{5,1},{9,5},... | collective-permute-start | bytes 1032200 | tf_op jit(solution)/shard_map/ppermute | solution.py:99
  11.0 36.5 %collective-permute-start.3 = (bf16[128,2304]{1,0:T(8,128)(2,1)S(1)}, bf16[128,2304]{1,0:T(8,128)(2,1)S(1)}, u32[]{:S(2)}, u32[]{:S(2)}) collective-permute-start(bf16[128,2304]{1,0:T(8,128)(2,1)S(1)} %get-tuple-element.49), channel_id=1, source_target_pairs={{0,16},{16,0},{1,17},{17,1},{2,18},{18,2},{3,19},{19,3},{4,20},{20... | collective-permute-start | bytes 1769480 | tf_op jit(solution)/shard_map/ppermute | solution.py:87
  11.1 19.6 %collective-permute-start.31 = (s32[1]{0:T(128)}, s32[1]{0:T(128)}, u32[]{:S(2)}, u32[]{:S(2)}) collective-permute-start(s32[1]{0:T(128)} %param.12), channel_id=1, source_target_pairs={{0,16},{16,0},{1,17},{17,1},{2,18},{18,2},{3,19},{19,3},{4,20},{20... | collective-permute-start | bytes 20 | tf_op jit(solution)/shard_map/ppermute | solution.py:87
  30.7 14.2 %collective-permute-start = (bf16[24,12800]{1,0:T(8,128)(2,1)S(1)}, bf16[24,12800]{1,0:T(8,128)(2,1)S(1)}, u32[]{:S(2)}, u32[]{:S(2)}) collective-permute-start(bf16[24,12800]{1,0:T(8,128)(2,1)S(1)} %get-tuple-element.45), channel_id=1, source_target_pairs={{0,4},{4,8},{8,12},{12,14},{14,10},{10,6},{6,2},{2,0},{1,5},{5,9},... | collective-permute-start | bytes 1843208 | tf_op jit(solution)/shard_map/ppermute | solution.py:98
  32.9 14.1 %collective-permute-start.1 = (bf16[24,12800]{1,0:T(8,128)(2,1)S(1)}, bf16[24,12800]{1,0:T(8,128)(2,1)S(1)}, u32[]{:S(2)}, u32[]{:S(2)}) collective-permute-start(bf16[24,12800]{1,0:T(8,128)(2,1)S(1)} %get-tuple-element.45), channel_id=1, source_target_pairs={{4,0},{8,4},{12,8},{14,12},{10,14},{6,10},{2,6},{0,2},{5,1},{9,5},... | collective-permute-start | bytes 1843208 | tf_op jit(solution)/shard_map/ppermute | solution.py:99
  33.4 14.7 %collective-permute-start.19 = (bf16[128,1280]{1,0:T(8,128)(2,1)}, bf16[128,1280]{1,0:T(8,128)(2,1)S(1)}, u32[]{:S(2)}, u32[]{:S(2)}) collective-permute-start(bf16[128,1280]{1,0:T(8,128)(2,1)} %collective-permute-done.15), channel_id=1, source_target_pairs={{0,1},{1,0},{2,3},{3,2},{4,5},{5,4},{6,7},{7,6},{8,9},{9,8},{10,11... | collective-permute-start | bytes 983048 | tf_op jit(solution)/shard_map/ppermute | solution.py:84
  33.4 14.1 %collective-permute-start.18 = (bf16[128,1280]{1,0:T(8,128)(2,1)S(1)}, bf16[128,1280]{1,0:T(8,128)(2,1)S(1)}, u32[]{:S(2)}, u32[]{:S(2)}) collective-permute-start(bf16[128,1280]{1,0:T(8,128)(2,1)S(1)} %get-tuple-element.67), channel_id=1, source_target_pairs={{0,16},{16,0},{1,17},{17,1},{2,18},{18,2},{3,19},{19,3},{4,20},{20... | collective-permute-start | bytes 983048 | tf_op jit(solution)/shard_map/ppermute | solution.py:87
  35.7 2.2 %copy-start.1 = (bf16[2,128,8192]{2,1,0:T(8,128)(2,1)S(1)}, bf16[2,128,8192]{2,1,0:T(8,128)(2,1)}, u32[]{:S(2)}) copy-start(bf16[2,128,8192]{2,1,0:T(8,128)(2,1)} %refs_0_.5) | copy-start | bytes 12582916
  37.9 2.2 %copy-start.3 = (bf16[2,128,8192]{2,1,0:T(8,128)(2,1)S(1)}, bf16[2,128,8192]{2,1,0:T(8,128)(2,1)}, u32[]{:S(2)}) copy-start(bf16[2,128,8192]{2,1,0:T(8,128)(2,1)} %refs_1_.5) | copy-start | bytes 12582916
  40.1 1.8 %copy-start.7 = (bf16[2,192,3584]{2,1,0:T(8,128)(2,1)S(1)}, bf16[2,192,3584]{2,1,0:T(8,128)(2,1)}, u32[]{:S(2)}) copy-start(bf16[2,192,3584]{2,1,0:T(8,128)(2,1)} %constant_dynamic-update-slice_fusion.12) | copy-start | bytes 8257540
  40.1 6.4 %copy-start.8 = (bf16[192,12800]{1,0:T(8,128)(2,1)S(1)}, bf16[192,12800]{1,0:T(8,128)(2,1)}, u32[]{:S(2)}) copy-start(bf16[192,12800]{1,0:T(8,128)(2,1)} %constant_dynamic-update-slice_fusion.6) | copy-start | bytes 14745604
  44.9 7.5 %collective-permute-start.16 = (bf16[2,24,3584]{2,1,0:T(8,128)(2,1)S(1)}, bf16[2,24,3584]{2,1,0:T(8,128)(2,1)S(1)}, u32[]{:S(2)}, u32[]{:S(2)}) collective-permute-start(bf16[2,24,3584]{2,1,0:T(8,128)(2,1)S(1)} %collective-permute-done.2.refs_2_), channel_id=1, source_target_pairs={{0,4},{4,8},{8,12},{12,14},{14,10},{10,6},{6,2},{2,0},{1,5},{5,9},... | collective-permute-start | bytes 1032200 | tf_op jit(solution)/shard_map/ppermute | solution.py:98
  46.9 7.3 %collective-permute-start.17 = (bf16[2,24,3584]{2,1,0:T(8,128)(2,1)S(1)}, bf16[2,24,3584]{2,1,0:T(8,128)(2,1)S(1)}, u32[]{:S(2)}, u32[]{:S(2)}) collective-permute-start(bf16[2,24,3584]{2,1,0:T(8,128)(2,1)S(1)} %collective-permute-done.14), channel_id=1, source_target_pairs={{4,0},{8,4},{12,8},{14,12},{10,14},{6,10},{2,6},{0,2},{5,1},{9,5},... | collective-permute-start | bytes 1032200 | tf_op jit(solution)/shard_map/ppermute | solution.py:99
  47.4 65.3 %collective-permute-start.26 = (bf16[2,128,3584]{2,1,0:T(8,128)(2,1)S(1)}, bf16[2,128,3584]{2,1,0:T(8,128)(2,1)S(1)}, u32[]{:S(2)}, u32[]{:S(2)}) collective-permute-start(bf16[2,128,3584]{2,1,0:T(8,128)(2,1)S(1)} %get-tuple-element.74), channel_id=1, source_target_pairs={{0,1},{1,0},{2,3},{3,2},{4,5},{5,4},{6,7},{7,6},{8,9},{9,8},{10,11... | collective-permute-start | bytes 5505032 | tf_op jit(solution)/shard_map/ppermute | solution.py:84
  47.5 17.2 %collective-permute-start.23 = (bf16[128,1280]{1,0:T(8,128)(2,1)S(1)}, bf16[128,1280]{1,0:T(8,128)(2,1)S(1)}, u32[]{:S(2)}, u32[]{:S(2)}) collective-permute-start(bf16[128,1280]{1,0:T(8,128)(2,1)S(1)} %collective-permute-done.18), channel_id=1, source_target_pairs={{0,1},{1,0},{2,3},{3,2},{4,5},{5,4},{6,7},{7,6},{8,9},{9,8},{10,11... | collective-permute-start | bytes 983048 | tf_op jit(solution)/shard_map/ppermute | solution.py:84
  54.2 7.2 %collective-permute-start.20 = (bf16[2,24,3584]{2,1,0:T(8,128)(2,1)S(1)}, bf16[2,24,3584]{2,1,0:T(8,128)(2,1)S(1)}, u32[]{:S(2)}, u32[]{:S(2)}) collective-permute-start(bf16[2,24,3584]{2,1,0:T(8,128)(2,1)S(1)} %collective-permute-done.16), channel_id=1, source_target_pairs={{0,4},{4,8},{8,12},{12,14},{14,10},{10,6},{6,2},{2,0},{1,5},{5,9},... | collective-permute-start | bytes 1032200 | tf_op jit(solution)/shard_map/ppermute | solution.py:98
  55.8 7.2 %collective-permute-start.21 = (bf16[2,24,3584]{2,1,0:T(8,128)(2,1)S(1)}, bf16[2,24,3584]{2,1,0:T(8,128)(2,1)S(1)}, u32[]{:S(2)}, u32[]{:S(2)}) collective-permute-start(bf16[2,24,3584]{2,1,0:T(8,128)(2,1)S(1)} %collective-permute-done.17), channel_id=1, source_target_pairs={{4,0},{8,4},{12,8},{14,12},{10,14},{6,10},{2,6},{0,2},{5,1},{9,5},... | collective-permute-start | bytes 1032200 | tf_op jit(solution)/shard_map/ppermute | solution.py:99
  56.3 8.5 %collective-permute-start.22 = (bf16[128,1280]{1,0:T(8,128)(2,1)S(1)}, bf16[128,1280]{1,0:T(8,128)(2,1)S(1)}, u32[]{:S(2)}, u32[]{:S(2)}) collective-permute-start(bf16[128,1280]{1,0:T(8,128)(2,1)S(1)} %get-tuple-element.71), channel_id=1, source_target_pairs={{0,16},{16,0},{1,17},{17,1},{2,18},{18,2},{3,19},{19,3},{4,20},{20... | collective-permute-start | bytes 983048 | tf_op jit(solution)/shard_map/ppermute | solution.py:87
  61.5 16.7 %collective-permute-start.7 = (bf16[128,2304]{1,0:T(8,128)(2,1)S(1)}, bf16[128,2304]{1,0:T(8,128)(2,1)S(1)}, u32[]{:S(2)}, u32[]{:S(2)}) collective-permute-start(bf16[128,2304]{1,0:T(8,128)(2,1)S(1)} %collective-permute-done.3), channel_id=1, source_target_pairs={{0,1},{1,0},{2,3},{3,2},{4,5},{5,4},{6,7},{7,6},{8,9},{9,8},{10,11... | collective-permute-start | bytes 1769480 | tf_op jit(solution)/shard_map/ppermute | solution.py:84
  63.1 14.3 %collective-permute-start.6 = (bf16[128,2304]{1,0:T(8,128)(2,1)S(1)}, bf16[128,2304]{1,0:T(8,128)(2,1)S(1)}, u32[]{:S(2)}, u32[]{:S(2)}) collective-permute-start(bf16[128,2304]{1,0:T(8,128)(2,1)S(1)} %get-tuple-element.53), channel_id=1, source_target_pairs={{0,16},{16,0},{1,17},{17,1},{2,18},{18,2},{3,19},{19,3},{4,20},{20... | collective-permute-start | bytes 1769480 | tf_op jit(solution)/shard_map/ppermute | solution.py:87
  64.8 5.5 %collective-permute-start.24 = (bf16[1,24,3584]{2,1,0:T(8,128)(2,1)S(1)}, bf16[1,24,3584]{2,1,0:T(8,128)(2,1)S(1)}, u32[]{:S(2)}, u32[]{:S(2)}) collective-permute-start(bf16[1,24,3584]{2,1,0:T(8,128)(2,1)S(1)} %slice.87), channel_id=1, source_target_pairs={{0,4},{4,8},{8,12},{12,14},{14,10},{10,6},{6,2},{2,0},{1,5},{5,9},... | collective-permute-start | bytes 516104 | tf_op jit(solution)/shard_map/ppermute | solution.py:98
  66.9 5.4 %collective-permute-start.25 = (bf16[1,24,3584]{2,1,0:T(8,128)(2,1)S(1)}, bf16[1,24,3584]{2,1,0:T(8,128)(2,1)S(1)}, u32[]{:S(2)}, u32[]{:S(2)}) collective-permute-start(bf16[1,24,3584]{2,1,0:T(8,128)(2,1)S(1)} %slice.88), channel_id=1, source_target_pairs={{4,0},{8,4},{12,8},{14,12},{10,14},{6,10},{2,6},{0,2},{5,1},{9,5},... | collective-permute-start | bytes 516104 | tf_op jit(solution)/shard_map/ppermute | solution.py:99
  70.2 13.5 %collective-permute-start.4 = (bf16[24,12800]{1,0:T(8,128)(2,1)S(1)}, bf16[24,12800]{1,0:T(8,128)(2,1)S(1)}, u32[]{:S(2)}, u32[]{:S(2)}) collective-permute-start(bf16[24,12800]{1,0:T(8,128)(2,1)S(1)} %collective-permute-done), channel_id=1, source_target_pairs={{0,4},{4,8},{8,12},{12,14},{14,10},{10,6},{6,2},{2,0},{1,5},{5,9},... | collective-permute-start | bytes 1843208 | tf_op jit(solution)/shard_map/ppermute | solution.py:98
  72.3 13.9 %collective-permute-start.5 = (bf16[24,12800]{1,0:T(8,128)(2,1)S(1)}, bf16[24,12800]{1,0:T(8,128)(2,1)S(1)}, u32[]{:S(2)}, u32[]{:S(2)}) collective-permute-start(bf16[24,12800]{1,0:T(8,128)(2,1)S(1)} %collective-permute-done.1), channel_id=1, source_target_pairs={{4,0},{8,4},{12,8},{14,12},{10,14},{6,10},{2,6},{0,2},{5,1},{9,5},... | collective-permute-start | bytes 1843208 | tf_op jit(solution)/shard_map/ppermute | solution.py:99
  77.3 23.8 %collective-permute-start.11 = (bf16[128,2304]{1,0:T(8,128)(2,1)S(1)}, bf16[128,2304]{1,0:T(8,128)(2,1)S(1)}, u32[]{:S(2)}, u32[]{:S(2)}) collective-permute-start(bf16[128,2304]{1,0:T(8,128)(2,1)S(1)} %collective-permute-done.6), channel_id=1, source_target_pairs={{0,1},{1,0},{2,3},{3,2},{4,5},{5,4},{6,7},{7,6},{8,9},{9,8},{10,11... | collective-permute-start | bytes 1769480 | tf_op jit(solution)/shard_map/ppermute | solution.py:84
  86.1 13.0 %collective-permute-start.8 = (bf16[24,12800]{1,0:T(8,128)(2,1)S(1)}, bf16[24,12800]{1,0:T(8,128)(2,1)S(1)}, u32[]{:S(2)}, u32[]{:S(2)}) collective-permute-start(bf16[24,12800]{1,0:T(8,128)(2,1)S(1)} %collective-permute-done.4), channel_id=1, source_target_pairs={{0,4},{4,8},{8,12},{12,14},{14,10},{10,6},{6,2},{2,0},{1,5},{5,9},... | collective-permute-start | bytes 1843208 | tf_op jit(solution)/shard_map/ppermute | solution.py:98
  87.9 13.2 %collective-permute-start.9 = (bf16[24,12800]{1,0:T(8,128)(2,1)S(1)}, bf16[24,12800]{1,0:T(8,128)(2,1)S(1)}, u32[]{:S(2)}, u32[]{:S(2)}) collective-permute-start(bf16[24,12800]{1,0:T(8,128)(2,1)S(1)} %collective-permute-done.5), channel_id=1, source_target_pairs={{4,0},{8,4},{12,8},{14,12},{10,14},{6,10},{2,6},{0,2},{5,1},{9,5},... | collective-permute-start | bytes 1843208 | tf_op jit(solution)/shard_map/ppermute | solution.py:99
  88.2 13.0 %collective-permute-start.10 = (bf16[128,2304]{1,0:T(8,128)(2,1)S(1)}, bf16[128,2304]{1,0:T(8,128)(2,1)S(1)}, u32[]{:S(2)}, u32[]{:S(2)}) collective-permute-start(bf16[128,2304]{1,0:T(8,128)(2,1)S(1)} %get-tuple-element.57), channel_id=1, source_target_pairs={{0,16},{16,0},{1,17},{17,1},{2,18},{18,2},{3,19},{19,3},{4,20},{20... | collective-permute-start | bytes 1769480 | tf_op jit(solution)/shard_map/ppermute | solution.py:87
  99.1 29.0 %collective-permute-start.27 = (bf16[128,12800]{1,0:T(8,128)(2,1)S(1)}, bf16[128,12800]{1,0:T(8,128)(2,1)S(1)}, u32[]{:S(2)}, u32[]{:S(2)}) collective-permute-start(bf16[128,12800]{1,0:T(8,128)(2,1)S(1)} %get-tuple-element.60), channel_id=1, source_target_pairs={{0,1},{1,0},{2,3},{3,2},{4,5},{5,4},{6,7},{7,6},{8,9},{9,8},{10,11... | collective-permute-start | bytes 9830408 | tf_op jit(solution)/shard_map/ppermute | solution.py:84
  101.1 5.7 %collective-permute-start.29 = (bf16[128,768]{1,0:T(8,128)(2,1)S(1)}, bf16[128,768]{1,0:T(8,128)(2,1)S(1)}, u32[]{:S(2)}, u32[]{:S(2)}) collective-permute-start(bf16[128,768]{1,0:T(8,128)(2,1)S(1)} %get-tuple-element.76), channel_id=1, source_target_pairs={{0,16},{16,0},{1,17},{17,1},{2,18},{18,2},{3,19},{19,3},{4,20},{20... | collective-permute-start | bytes 589832 | tf_op jit(solution)/shard_map/ppermute | solution.py:87
  101.1 7.8 %collective-permute-start.12 = (bf16[24,6400]{1,0:T(8,128)(2,1)S(1)}, bf16[24,6400]{1,0:T(8,128)(2,1)S(1)}, u32[]{:S(2)}, u32[]{:S(2)}) collective-permute-start(bf16[24,6400]{1,0:T(8,128)(2,1)S(1)} %slice.83), channel_id=1, source_target_pairs={{0,4},{4,8},{8,12},{12,14},{14,10},{10,6},{6,2},{2,0},{1,5},{5,9},... | collective-permute-start | bytes 921608 | tf_op jit(solution)/shard_map/ppermute | solution.py:98
  102.3 8.7 %collective-permute-start.13 = (bf16[24,6400]{1,0:T(8,128)(2,1)S(1)}, bf16[24,6400]{1,0:T(8,128)(2,1)S(1)}, u32[]{:S(2)}, u32[]{:S(2)}) collective-permute-start(bf16[24,6400]{1,0:T(8,128)(2,1)S(1)} %slice.84), channel_id=1, source_target_pairs={{4,0},{8,4},{12,8},{14,12},{10,14},{6,10},{2,6},{0,2},{5,1},{9,5},... | collective-permute-start | bytes 921608 | tf_op jit(solution)/shard_map/ppermute | solution.py:99
  106.8 19.5 %collective-permute-start.34 = (bf16[128,1280]{1,0:T(8,128)(2,1)S(1)}, bf16[128,1280]{1,0:T(8,128)(2,1)S(1)}, u32[]{:S(2)}, u32[]{:S(2)}) collective-permute-start(bf16[128,1280]{1,0:T(8,128)(2,1)S(1)} %collective-permute-done.22), channel_id=1, source_target_pairs={{0,1},{1,0},{2,3},{3,2},{4,5},{5,4},{6,7},{7,6},{8,9},{9,8},{10,11... | collective-permute-start | bytes 983048 | tf_op jit(solution)/shard_map/ppermute | solution.py:84
  109.0 17.3 %collective-permute-start.35 = (bf16[128,768]{1,0:T(8,128)(2,1)S(1)}, bf16[128,768]{1,0:T(8,128)(2,1)S(1)}, u32[]{:S(2)}, u32[]{:S(2)}) collective-permute-start(bf16[128,768]{1,0:T(8,128)(2,1)S(1)} %collective-permute-done.29), channel_id=1, source_target_pairs={{0,1},{1,0},{2,3},{3,2},{4,5},{5,4},{6,7},{7,6},{8,9},{9,8},{10,11... | collective-permute-start | bytes 589832 | tf_op jit(solution)/shard_map/ppermute | solution.py:84
  111.0 10.5 %collective-permute-start.28 = (bf16[128,1280]{1,0:T(8,128)(2,1)S(1)}, bf16[128,1280]{1,0:T(8,128)(2,1)S(1)}, u32[]{:S(2)}, u32[]{:S(2)}) collective-permute-start(bf16[128,1280]{1,0:T(8,128)(2,1)S(1)} %get-tuple-element.75), channel_id=1, source_target_pairs={{0,16},{16,0},{1,17},{17,1},{2,18},{18,2},{3,19},{19,3},{4,20},{20... | collective-permute-start | bytes 983048 | tf_op jit(solution)/shard_map/ppermute | solution.py:87
  113.7 9.9 %collective-permute-start.30 = (f32[192,256]{1,0:T(8,128)S(1)}, f32[192,256]{1,0:T(8,128)S(1)}, u32[]{:S(2)}, u32[]{:S(2)}) collective-permute-start(f32[192,256]{1,0:T(8,128)S(1)} %get-tuple-element.80), channel_id=1, source_target_pairs={{0,16},{16,0},{1,17},{17,1},{2,18},{18,2},{3,19},{19,3},{4,20},{20... | collective-permute-start | bytes 589832 | tf_op jit(solution)/shard_map/ppermute | solution.py:87
  121.5 5.4 %collective-permute-start.32 = (bf16[128,2304]{1,0:T(8,128)(2,1)S(1)}, bf16[128,2304]{1,0:T(8,128)(2,1)S(1)}, u32[]{:S(2)}, u32[]{:S(2)}) collective-permute-start(bf16[128,2304]{1,0:T(8,128)(2,1)S(1)} %collective-permute-done.10), channel_id=1, source_target_pairs={{0,1},{1,0},{2,3},{3,2},{4,5},{5,4},{6,7},{7,6},{8,9},{9,8},{10,11... | collective-permute-start | bytes 1769480 | tf_op jit(solution)/shard_map/ppermute | solution.py:84
  123.6 3.3 %collective-permute-start.33 = (bf16[128,1280]{1,0:T(8,128)(2,1)S(1)}, bf16[128,1280]{1,0:T(8,128)(2,1)S(1)}, u32[]{:S(2)}, u32[]{:S(2)}) collective-permute-start(bf16[128,1280]{1,0:T(8,128)(2,1)S(1)} %collective-permute-done.28), channel_id=1, source_target_pairs={{0,1},{1,0},{2,3},{3,2},{4,5},{5,4},{6,7},{7,6},{8,9},{9,8},{10,11... | collective-permute-start | bytes 983048 | tf_op jit(solution)/shard_map/ppermute | solution.py:84
  130.1 3.6 %collective-permute-start.36 = (f32[12]{0:T(128)S(1)}, f32[12]{0:T(128)S(1)}, u32[]{:S(2)}, u32[]{:S(2)}) collective-permute-start(f32[12]{0:T(128)S(1)} %get-tuple-element.78), channel_id=1, source_target_pairs={{0,16},{16,0},{1,17},{17,1},{2,18},{18,2},{3,19},{19,3},{4,20},{20... | collective-permute-start | bytes 152 | tf_op jit(solution)/shard_map/ppermute | solution.py:87
  133.8 1.1 collective-permute-start.37
  135.0 3.6 %collective-permute-start.38 = (f32[2,1,12]{2,1,0:T(1,128)S(1)}, f32[2,1,12]{2,1,0:T(1,128)S(1)}, u32[]{:S(2)}, u32[]{:S(2)}) collective-permute-start(f32[2,1,12]{2,1,0:T(1,128)S(1)} %fusion.145), channel_id=1, source_target_pairs={{0,2},{1,3},{2,0},{3,1},{4,6},{5,7},{6,4},{7,5},{8,10},{9,11},{10,... | collective-permute-start | bytes 296 | tf_op jit(solution)/shard_map/ppermute | solution.py:255
  138.6 3.6 %collective-permute-start.39 = (f32[2,1,12]{2,1,0:T(1,128)S(1)}, f32[2,1,12]{2,1,0:T(1,128)S(1)}, u32[]{:S(2)}, u32[]{:S(2)}) collective-permute-start(f32[2,1,12]{2,1,0:T(1,128)S(1)} %fusion.146), channel_id=1, source_target_pairs={{0,4},{1,5},{2,6},{3,7},{4,0},{5,1},{6,2},{7,3},{8,12},{9,13},{10,... | collective-permute-start | bytes 296 | tf_op jit(solution)/shard_map/ppermute | solution.py:255
  142.2 4.5 %collective-permute-start.40 = (f32[2,1,12]{2,1,0:T(1,128)S(1)}, f32[2,1,12]{2,1,0:T(1,128)S(1)}, u32[]{:S(2)}, u32[]{:S(2)}) collective-permute-start(f32[2,1,12]{2,1,0:T(1,128)S(1)} %add.190), channel_id=1, source_target_pairs={{0,8},{1,9},{2,10},{3,11},{4,12},{5,13},{6,14},{7,15},{8,0},{9,1},... | collective-permute-start | bytes 296 | tf_op jit(solution)/shard_map/ppermute | solution.py:255

commit v2 on v0

v2 whole, which is shorter than its diff:
```python
import math

import jax
import jax.numpy as jnp
from jax import lax
from jax.experimental import pallas as pl
from jax.experimental.pallas import tpu as pltpu
from jax.sharding import PartitionSpec as P

RANK = 32
LEN = 2048
MIB = 2**20
SPAN = 512
LOAD = 2048
OUTER = 52
ANYWHERE = pl.BlockSpec(memory_space=pl.ANY)
CHIP = pl.BlockSpec(memory_space=pltpu.VMEM)


def chip_ring(chips):
    return list(range(0, chips, 2)) + list(range(chips - 1, 0, -2))


def contract(factors, tokens):
    return lax.dot_general(
        factors, tokens, (((1,), (1,)), ((), ())), preferred_element_type=jnp.float32
    )


def rows_of(pieces):
    return jnp.concatenate(pieces, axis=0) if len(pieces) > 1 else pieces[0]


def move(sources, targets, after=()):
    count = len(sources)
    moves, shapes = [], []
    for t, ranges in enumerate(targets):
        offset = 0
        for s, layer, start, stop in ranges:
            moves.append((t, s, layer, start, stop, offset))
            offset += stop - start
        lead = sources[s].shape[:2] if layer is None else sources[s].shape[1:2]
        shapes.append(jax.ShapeDtypeStruct((*lead, offset), sources[s].dtype))

    def kernel(*refs):
        ins, outs, sems = refs[:count], refs[count + len(after) : -1], refs[-1]
        me = lax.axis_index("grp")
        copies = []
        for k, (t, s, layer, start, stop, offset) in enumerate(moves):
            columns, place = pl.ds(start, stop - start), pl.ds(offset, stop - start)
            if layer is None:
                source, target = ins[s].at[:, :, columns], outs[t].at[:, :, place]
            else:
                row = {"mine": me, "other": 1 - me}.get(layer, layer)
                source, target = ins[s].at[row, :, columns], outs[t].at[:, place]
            copies.append(pltpu.make_async_copy(source, target, sems.at[k]))
            copies[-1].start()
        for copy in copies:
            copy.wait()

    return pl.pallas_call(
        kernel,
        out_shape=shapes,
        in_specs=[ANYWHERE] * (count + len(after)),
        out_specs=[CHIP] * len(shapes),
        scratch_shapes=[pltpu.SemaphoreType.DMA((len(moves),))],
        compiler_params=pltpu.CompilerParams(vmem_limit_bytes=62 * MIB),
        cost_estimate=pl.CostEstimate(
            flops=0,
            transcendentals=0,
            bytes_accessed=4 * sum(math.prod(x.shape) * 2 for x in shapes),
        ),
    )(*sources, *after)


def cost(flops):
    return pl.CostEstimate(flops=flops, transcendentals=0, bytes_accessed=flops // 64)


class Loads:

    def __init__(self):
        self.arrays, self.keys, self.targets = [], [], []

    def add(self, array, lead, first, width, target=None):
        for k, known in enumerate(self.arrays):
            if known is array:
                break
        else:
            k = len(self.arrays)
            self.arrays.append(array)
        self.keys.append((k, lead, first, width))
        self.targets.append(target)
        return len(self.keys) - 1

    def scratch(self):
        buffers = [
            pltpu.VMEM((self.arrays[k].shape[-2], width), self.arrays[k].dtype)
            for (k, _, _, width), target in zip(self.keys, self.targets)
            if target is None
        ]
        return [*buffers, pltpu.SemaphoreType.DMA((len(self.keys),))]

    def start(self, ins, outs, buffers):
        free = iter(buffers[:-1])
        self.copies, self.refs = [], []
        for i, ((k, lead, first, width), target) in enumerate(zip(self.keys, self.targets)):
            columns = pl.ds(first, width)
            row = lax.axis_index("grp") if lead == "mine" else lead
            source = ins[k].at[:, columns] if lead is None else ins[k].at[row, :, columns]
            if target is None:
                ref = next(free)
            else:
                out, down, across = target
                rows = self.arrays[k].shape[-2]
                ref = outs[out].at[pl.ds(down, rows), pl.ds(across, width)]
            self.refs.append(ref)
            self.copies.append(pltpu.make_async_copy(source, ref, buffers[-1].at[i]))
            self.copies[-1].start()

    def wait(self, wanted=None):
        for i in sorted(set(range(len(self.keys)) if wanted is None else wanted)):
            if self.copies[i] is not None:
                self.copies[i].wait()
                self.copies[i] = None


def products(total, factors, tokens, width):
    for a in range(0, width, SPAN):
        span = min(SPAN, width - a)
        left = rows_of([ref[:, first + a : first + a + span] for ref, first in factors])
        right = rows_of([ref[:, first + a : first + a + span] for ref, first in tokens])
        product = contract(left, right)
        total = product if total is None else total + product
    return total


def solution(mesh):
    blk = mesh.shape["blk"]
    chips = blk // 2
    full = (chips - 1) // 2
    order = chip_ring(chips)
    forward, backward = [], []
    for core in range(2):
        for k in range(chips):
            a = order[k] * 2 + core
            b = order[(k + 1) % chips] * 2 + core
            forward.append((a, b))
            backward.append((b, a))
    place = [0] * chips
    for k, chip in enumerate(order):
        place[chip] = k

    def swap_core(x):
        return lax.ppermute(x, "blk", [(i, i ^ 1) for i in range(blk)])

    def swap_grp(x):
        return lax.ppermute(x, "grp", [(0, 1), (1, 0)])

    def ahead_of(x):
        return lax.ppermute(x, "blk", forward)

    def back_of(x):
        return lax.ppermute(x, "blk", backward)

    def after(values, *others):
        return lax.optimization_barrier((*values, *others))[: len(values)]

    def shards(activations, backprops, out_factors, in_factors, lengths):
        tokens_here = activations.shape[1]
        width = backprops.shape[2]
        depth = activations.shape[2]
        cut = depth * 7 // 16
        packed = width + cut
        beyond = depth - cut
        columns = out_factors.shape[1]
        seq_count = lengths.shape[0]
        me = lax.axis_index("grp")
        device = lax.axis_index("blk")

        def packing(out_source, in_source, layer, start, stop):
            ranges = []
            if start < width:
                ranges.append((out_source, layer, start, min(stop, width)))
            if stop > width:
                ranges.append((in_source, layer, max(start - width, 0), stop - width))
            return ranges

        share = -(-packed // 3 // 128) * 128
        edges = [0, share, 2 * share, packed]

        def away_part(k):
            return packing(1, 0, "other", edges[k], edges[k + 1])

        acts_sib, backs_sib = swap_core(activations), swap_core(backprops)

        sources = (activations, backprops)
        piece, *chunks = move(
            (*sources, out_factors, in_factors),
            [
                packing(2, 3, "mine", 0, packed) + [(3, k, cut, depth) for k in range(2)],
                away_part(0),
            ],
        )
        chunks += move(sources, [away_part(1), away_part(2)], after=(piece,))

        got = [piece]
        ahead = back = piece
        away, away_sib = [], []
        for step in range(full):
            given = [ahead, back]
            if step < 3:
                given.append(chunks[step])
            if step == 1:
                given = after(given, away[0], *chunks[1:], backs_sib)
            if step == 2:
                given = after(given, away[1], acts_sib)
                away_sib = [swap_core(x) for x in away]
            ahead, back = ahead_of(given[0]), back_of(given[1])
            if step < 3:
                away.append(swap_grp(given[2]))
            got += [ahead, back]
        ahead, back = after((ahead, back), away[2], *away_sib)
        away_sib.append(swap_core(away[2]))
        last_home = (
            ahead_of(ahead[:, packed : packed + beyond]),
            back_of(back[:, packed + beyond :]),
        )
        middle = packed // 2
        rest = after((ahead[:, :middle], back[:, middle:packed]), *last_home)
        last = ahead_of(rest[0]), back_of(rest[1])
        if chips > 8:
            got = [jnp.concatenate(got, axis=0)]

        shard_rows = chips * columns
        chip_tokens = 2 * tokens_here

        home_loads = Loads()
        home_shards = [home_loads.add(g, None, packed, 2 * beyond) for g in got]
        home_sides = []
        for k in range(2):
            home_sides.append(
                (
                    home_loads.add(last_home[k], None, 0, beyond),
                    [home_loads.add(x, k, cut, beyond) for x in (activations, acts_sib)],
                )
            )
        count_home = len(home_loads.arrays)

        def home_kernel(*refs):
            lengths_ref, mine_ref, other_ref, *scratch = refs[count_home:]
            home_loads.start(refs[:count_home], (), scratch)
            at = home_loads.refs
            me = lax.axis_index("grp")
            first = lax.axis_index("blk") // 2 * chip_tokens
            limit = lengths_ref[first // LEN].astype(jnp.float32)
            for ref in (mine_ref, other_ref):
                ref[shard_rows:, :] = jnp.full((8, chip_tokens), limit)
            for k, (tail, tokens) in enumerate(home_sides):
                home_loads.wait([*home_shards, tail, *tokens])
                factors = [(at[i], k * beyond) for i in home_shards] + [(at[tail], 0)]
                value = products(None, factors, [(at[i], 0) for i in tokens], beyond)

                @pl.when(me == k)
                def _():
                    mine_ref[:shard_rows, :] = value

                @pl.when(me != k)
                def _():
                    other_ref[:shard_rows, :] = value

        extra = jax.ShapeDtypeStruct((shard_rows + 8, chip_tokens), jnp.float32)
        home_mine, home_away = pl.pallas_call(
            home_kernel,
            out_shape=[extra] * 2,
            in_specs=[ANYWHERE] * count_home + [pl.BlockSpec(memory_space=pltpu.SMEM)],
            out_specs=[CHIP] * 2,
            scratch_shapes=home_loads.scratch(),
            compiler_params=pltpu.CompilerParams(vmem_limit_bytes=62 * MIB),
            cost_estimate=cost(2 * shard_rows * chip_tokens * 2 * beyond),
        )(*home_loads.arrays, lengths)
        home_away = swap_grp(home_away)

        points = sorted({*range(0, packed, LOAD), width, middle, *edges})
        loads = Loads()
        plan, shard_loads = [], {}
        for a, b in zip(points[:-1], points[1:]):
            k = max(i for i in range(3) if edges[i] <= a)
            if a >= width:
                break
            base = 0 if a < width // 2 else width // 2
            if base not in shard_loads:
                shard_loads[base] = [loads.add(g, None, base, width // 2) for g in got]
            if a < middle:
                tail = loads.add(last[0], None, a, b - a)
            else:
                tail = loads.add(last[1], None, a - middle, b - a)
            tokens = [loads.add(x, "mine", a, b - a) for x in (backprops, backs_sib)]
            tokens += [loads.add(x[k], None, a - edges[k], b - a) for x in (away, away_sib)]
            plan.append((base, a, b, tail, tokens))
        for i, x in enumerate((activations, acts_sib)):
            loads.add(x, "mine", 0, cut, (1, i * tokens_here, 0))
        for k in range(3):
            a, b = max(edges[k], width), edges[k + 1]
            if a < b:
                for i, x in enumerate((away, away_sib)):
                    loads.add(
                        x[k], None, a - edges[k], b - a, (1, (2 + i) * tokens_here, a - width)
                    )
        for i, g in enumerate(got):
            loads.add(g, None, width, cut, (2 + i, 0, 0))
        count = len(loads.arrays)
        outs = 2 + len(got)

        def out_kernel(*refs):
            out_refs = refs[count : count + outs]
            loads.start(refs[:count], out_refs, refs[count + outs :])
            at, total = loads.refs, None
            for base, a, b, tail, tokens in plan:
                loads.wait([*shard_loads[base], tail, *tokens])
                factors = [(at[i], a - base) for i in shard_loads[base]] + [(at[tail], 0)]
                total = products(total, factors, [(at[i], 0) for i in tokens], b - a)
            out_refs[0][...] = total
            loads.wait()

        proj_out, in_tokens, *in_shards = pl.pallas_call(
            out_kernel,
            out_shape=[
                jax.ShapeDtypeStruct((shard_rows, 2 * chip_tokens), jnp.float32),
                jax.ShapeDtypeStruct((2 * chip_tokens, cut), activations.dtype),
                *(jax.ShapeDtypeStruct((g.shape[0], cut), g.dtype) for g in got),
            ],
            in_specs=[ANYWHERE] * count,
            out_specs=[CHIP] * outs,
            scratch_shapes=loads.scratch(),
            compiler_params=pltpu.CompilerParams(vmem_limit_bytes=OUTER * MIB),
            cost_estimate=cost(2 * shard_rows * 2 * chip_tokens * width),
        )(*loads.arrays)

        odd = device % 2
        at = jnp.asarray(place, jnp.int32)[device // 2]
        steps = [0]
        for k in range(1, full + 1):
            steps += [-k, k]
        steps.append(chips // 2)
        shard_chip = jnp.asarray(order, jnp.int32)[
            (at + jnp.asarray(steps, jnp.int32)) % chips
        ]
        first_column = (shard_chip * 2 + odd) * columns
        column = first_column[:, None] + jnp.arange(columns, dtype=jnp.int32)[None, :]
        query = column.reshape(-1) // RANK
        queries = columns * blk // RANK
        hit = (query[:, None] == jnp.arange(128)[None, :]).astype(jnp.float32)

        shards_in = len(in_shards)
        tail_in = last[1] if middle <= width else None
        assert tail_in is not None

        def score_kernel(*refs):
            token_ref, tail_ref = refs[shards_in : shards_in + 2]
            out_ref, mine_ref, other_ref, hit_ref, *scores = refs[shards_in + 2 :]
            factors = [(ref, 0) for ref in refs[:shards_in]] + [(tail_ref, width - middle)]
            proj_in = products(None, factors, [(token_ref, 0)], cut)
            first = lax.axis_index("blk") // 2 * chip_tokens
            flip = lax.axis_index("blk") % 2
            lane = lax.broadcasted_iota(jnp.int32, (1, chip_tokens), 1)
            swapped = jnp.where(lane < tokens_here, lane + tokens_here, lane - tokens_here)
            position = (first % LEN + jnp.where(flip == 1, swapped, lane)).astype(jnp.float32)

            for k, extra_ref in enumerate((mine_ref, other_ref)):
                span = slice(k * chip_tokens, (k + 1) * chip_tokens)
                in_use = position < extra_ref[shard_rows : shard_rows + 1, :]
                product = out_ref[:, span] * (proj_in[:, span] + extra_ref[:shard_rows, :])
                product = jnp.where(in_use, product, 0.0)
                per_column = jnp.sum(product, axis=1, keepdims=True)
                scores[k][...] = jnp.sum(per_column * hit_ref[...], axis=0, keepdims=True)

        own, other = pl.pallas_call(
            score_kernel,
            out_shape=[jax.ShapeDtypeStruct((1, 128), jnp.float32)] * 2,
            in_specs=[CHIP] * (shards_in + 6),
            out_specs=[CHIP] * 2,
            compiler_params=pltpu.CompilerParams(vmem_limit_bytes=OUTER * MIB),
            cost_estimate=cost(2 * shard_rows * 2 * chip_tokens * cut),
        )(*in_shards, in_tokens, last[1], proj_out, home_mine, home_away, hit)

        other = swap_grp(other)
        sequence = device // 2 * chip_tokens // LEN
        select = jnp.arange(seq_count, dtype=jnp.int32) == sequence
        rows = jnp.arange(2)[:, None] == me
        value = jnp.where(rows, own, other)
        value = value[:, None, :] * select.astype(jnp.float32)[None, :, None]
        if blk & (blk - 1):
            return lax.psum(value, "blk")[:, :, :queries]
        bit = 1
        while bit < blk:
            value = value + lax.ppermute(value, "blk", [(i, i ^ bit) for i in range(blk)])
            bit *= 2
        return value[:, :, :queries]

    placed = (
        P(None, ("grp", "blk"), None),
        P(None, ("grp", "blk"), None),
        P(None, "blk", None),
        P(None, "blk", None),
        P("grp"),
    )
    return jax.shard_map(
        shards, mesh=mesh, in_specs=placed, out_specs=P(None, "grp", None), check_vma=False
    )
```

time: 198 us -> 131 us (0.66)
  waiting for transfers between devices: 131 us -> 81.4 us
  blocking collectives: 33.2 us -> 0 us
  Pallas kernels: 0 us -> 24 us
  starting transfers between devices: 0.01 us -> 20.6 us
  matrix products: 16.9 us -> 0 us
  between operations: 14.1 us -> 0.83 us
  local copies, waits for them, and re-layouts: 0.08 us -> 2.15 us
    all_gather x1 -> x0, waiting for transfers between devices: 131 us -> none  [shards(): lax.all_gather(factors, 'blk', axis=1, tiled=True)]
    ppermute x0 -> x24, waiting for transfers between devices: none -> 81.4 us  [the longest x5 48.3 us: ahead_of(): return lax.ppermute(x, 'blk', forward)]
    psum x1 -> x0, blocking collectives: 33.2 us -> none  [shards(): return lax.psum(per_query[:, None, :] * select_rows[None, :, None], 'blk')]
    pallas_call x0 -> x5, Pallas kernels: none -> 24 us  [the longest x1 8.24 us: shards(): pl.pallas_call(out_kernel, out_shape=[jax.ShapeDtypeStruct((shard_rows, 2...]
    ppermute x0 -> x24, starting transfers between devices: none -> 20.6 us  [the longest x5 7.18 us: swap_grp(): return lax.ppermute(x, 'grp', [(0, 1), (1, 0)])]
    dot_general x2 -> x0, matrix products: 16.9 us -> none  [the longest x1 9.29 us: scorer(): return jnp.einsum('ltk,t->lk', proj_out * proj_in, in_use)]
    concatenate x1 -> x0, other arithmetic: 2.7 us -> none  [shards(): factors = jnp.concatenate([out_factors, in_factors], axis=2)]
  transfers between devices with their start and end apart: 1 -> 24, of which waited for: 1 -> 14; matrix products, arithmetic and copies ran while one was open for 0% -> 2% of each run, Pallas kernels for 0% -> 16%
where the time goes in v2:
time: 131 us
  waiting for transfers between devices  81.4 us (62%)
  Pallas kernels  24 us (18%)
  starting transfers between devices  20.6 us (16%)
  local copies, waits for them, and re-layouts  2.15 us (2%)
  other arithmetic  1.63 us (1%)
    ppermute x5, waiting for transfers between devices, ahead_of(): return lax.ppermute(x, 'blk', forward)  48.3 us
    ppermute x5, waiting for transfers between devices, swap_grp(): return lax.ppermute(x, 'grp', [(0, 1), (1, 0)])  17.4 us
    ppermute x4, waiting for transfers between devices, shards(): lax.ppermute(value, 'blk', [(i, i ^ bit) for i in range(blk)])  10.6 us
    pallas_call x1, Pallas kernels, shards(): pl.pallas_call(out_kernel, out_shape=[jax.ShapeDtypeStruct((shard_rows, 2...  8.24 us
    ppermute x5, starting transfers between devices, swap_grp(): return lax.ppermute(x, 'grp', [(0, 1), (1, 0)])  7.18 us
    ppermute x5, starting transfers between devices, ahead_of(): return lax.ppermute(x, 'blk', forward)  6.98 us
    pallas_call x1, Pallas kernels, shards(): pl.pallas_call(home_kernel, out_shape=[extra] * 2, in_specs=[ANYWHERE] *...  6.36 us
    pallas_call x2, Pallas kernels, move(): pl.pallas_call(kernel, out_shape=shapes, in_specs=[ANYWHERE] * (count + l...  5.83 us
  transfers between devices with their start and end apart: 24, of which 14 were waited for; matrix products, arithmetic and copies ran while one was open for 2% of the time, Pallas kernels for 16%

profile of v2, /device:TPU:0, one launch (start us, length us, event | category | flops | bytes accessed | tf_op | source)
XLA Modules:
  0.0 130.6 jit_solution(7974695657145557982)
XLA Ops:
  0.0 0.5 collective-permute-start.3
  0.5 0.1 collective-permute-start.7
  0.5 3.0 %shard_map.82 = (bf16[24,20992]{1,0:T(8,128)(2,1)}, bf16[128,3968]{1,0:T(8,128)(2,1)}) custom-call(bf16[2,128,8192]{2,1,0:T(8,128)(2,1)} %refs_8_.3, bf16[2,128,8192]{2,1,0:T(8,128)(2,1)} %refs_8_.2, bf16[2,24,8192]{2,1,0:T(8,128)(2,1)} %refs_2_.1, bf16[2,24,8192]{2,1,0:T(8,128)(2,1)} %refs_3_.1), custom_call_target="tpu_custom_call" | custom-call | bytes 8093696 | tf_op jit(solution)/shard_map/pallas_call | solution.py:61
  3.5 3.0 %collective-permute-start.2 = (bf16[128,3968]{1,0:T(8,128)(2,1)}, bf16[128,3968]{1,0:T(8,128)(2,1)}, u32[]{:S(2)}, u32[]{:S(2)}) collective-permute-start(bf16[128,3968]{1,0:T(8,128)(2,1)} %get-tuple-element.34), channel_id=1, source_target_pairs={{0,16},{16,0},{1,17},{17,1},{2,18},{18,2},{3,19},{19,3},{4,20},{20... | collective-permute-start | bytes 3047432 | tf_op jit(solution)/shard_map/ppermute | solution.py:158
  6.5 1.6 %collective-permute-start = (bf16[24,20992]{1,0:T(8,128)(2,1)}, bf16[24,20992]{1,0:T(8,128)(2,1)S(1)}, u32[]{:S(2)}, u32[]{:S(2)}) collective-permute-start(bf16[24,20992]{1,0:T(8,128)(2,1)} %get-tuple-element.32.refs_2_.refs_0_), channel_id=1, source_target_pairs={{0,4},{4,8},{8,12},{12,14},{14,10},{10,6},{6,2},{2,0},{1,5},{5,9},... | collective-permute-start | bytes 3022856 | tf_op jit(solution)/shard_map/ppermute | solution.py:161
  8.1 0.4 collective-permute-start.1
  8.6 2.9 %shard_map.83 = (bf16[128,3968]{1,0:T(8,128)(2,1)}, bf16[128,3840]{1,0:T(8,128)(2,1)}) custom-call(bf16[2,128,8192]{2,1,0:T(8,128)(2,1)} %refs_8_.3, bf16[2,128,8192]{2,1,0:T(8,128)(2,1)} %refs_8_.2, bf16[24,20992]{1,0:T(8,128)(2,1)} %get-tuple-element.32.refs_2_.refs_0_), custom_call_target="tpu_custom_call" | custom-call | bytes 7995392 | tf_op jit(solution)/shard_map/pallas_call | solution.py:61
  11.4 19.2 %collective-permute-done.refs_1_ = bf16[24,20992]{1,0:T(8,128)(2,1)S(1)} collective-permute-done((bf16[24,20992]{1,0:T(8,128)(2,1)}, bf16[24,20992]{1,0:T(8,128)(2,1)S(1)}, u32[]{:S(2)}, u32[]{:S(2)}) %collective-permute-start) | collective-permute-done | bytes 1007648 | tf_op jit(solution)/shard_map/ppermute | solution.py:161
  30.6 1.3 collective-permute-done.1.refs_2_
  31.9 0.0 collective-permute-done.2.refs_10_
  31.9 0.0 collective-permute-done.3.refs_9_
  32.0 0.6 collective-permute-start.6
  32.5 1.6 %collective-permute-start.4 = (bf16[24,20992]{1,0:T(8,128)(2,1)S(1)}, bf16[24,20992]{1,0:T(8,128)(2,1)}, u32[]{:S(2)}, u32[]{:S(2)}) collective-permute-start(bf16[24,20992]{1,0:T(8,128)(2,1)S(1)} %collective-permute-done.refs_1_), channel_id=1, source_target_pairs={{0,4},{4,8},{8,12},{12,14},{14,10},{10,6},{6,2},{2,0},{1,5},{5,9},... | collective-permute-start | bytes 3022856 | tf_op jit(solution)/shard_map/ppermute | solution.py:161
  34.1 0.4 collective-permute-start.5
  34.6 0.0 collective-permute-done.7.refs_18_.refs_9_
  34.6 20.6 %collective-permute-done.4.refs_3_ = bf16[24,20992]{1,0:T(8,128)(2,1)} collective-permute-done((bf16[24,20992]{1,0:T(8,128)(2,1)S(1)}, bf16[24,20992]{1,0:T(8,128)(2,1)}, u32[]{:S(2)}, u32[]{:S(2)}) %collective-permute-start.4) | collective-permute-done | bytes 1007648 | tf_op jit(solution)/shard_map/ppermute | solution.py:161
  55.2 1.3 collective-permute-done.5.refs_4_
  56.5 0.0 collective-permute-done.6.refs_12_
  56.5 1.4 %collective-permute-start.10 = (bf16[128,3840]{1,0:T(8,128)(2,1)}, bf16[128,3840]{1,0:T(8,128)(2,1)}, u32[]{:S(2)}, u32[]{:S(2)}) collective-permute-start(bf16[128,3840]{1,0:T(8,128)(2,1)} %get-tuple-element.41), channel_id=1, source_target_pairs={{0,16},{16,0},{1,17},{17,1},{2,18},{18,2},{3,19},{19,3},{4,20},{20... | collective-permute-start | bytes 2949128 | tf_op jit(solution)/shard_map/ppermute | solution.py:158
  57.9 0.0 collective-permute-start.11
  57.9 0.5 collective-permute-start.12
  58.4 1.6 %collective-permute-start.8 = (bf16[24,20992]{1,0:T(8,128)(2,1)}, bf16[24,20992]{1,0:T(8,128)(2,1)S(1)}, u32[]{:S(2)}, u32[]{:S(2)}) collective-permute-start(bf16[24,20992]{1,0:T(8,128)(2,1)} %collective-permute-done.4.refs_3_), channel_id=1, source_target_pairs={{0,4},{4,8},{8,12},{12,14},{14,10},{10,6},{6,2},{2,0},{1,5},{5,9},... | collective-permute-start | bytes 3022856 | tf_op jit(solution)/shard_map/ppermute | solution.py:161
  60.0 0.4 collective-permute-start.9
  60.4 0.6 dynamic_slice.3
  61.0 0.7 compare_select_fusion
  61.7 0.6 gather_fusion
  62.3 15.2 %collective-permute-done.10.refs_15_ = bf16[128,3840]{1,0:T(8,128)(2,1)} collective-permute-done((bf16[128,3840]{1,0:T(8,128)(2,1)}, bf16[128,3840]{1,0:T(8,128)(2,1)}, u32[]{:S(2)}, u32[]{:S(2)}) %collective-permute-start.10) | collective-permute-done | bytes 983072 | tf_op jit(solution)/shard_map/ppermute | solution.py:158
  77.6 0.0 collective-permute-start.17
  77.6 0.1 iota_add_fusion
  77.7 0.1 add.83
  77.7 0.0 collective-permute-done.11.refs_11_
  77.8 5.1 %collective-permute-done.8.refs_5_ = bf16[24,20992]{1,0:T(8,128)(2,1)S(1)} collective-permute-done((bf16[24,20992]{1,0:T(8,128)(2,1)}, bf16[24,20992]{1,0:T(8,128)(2,1)S(1)}, u32[]{:S(2)}, u32[]{:S(2)}) %collective-permute-start.8) | collective-permute-done | bytes 1007648 | tf_op jit(solution)/shard_map/ppermute | solution.py:161
  82.9 1.3 collective-permute-done.9.refs_6_
  84.2 0.0 collective-permute-done.12.refs_13_
  84.2 1.5 %collective-permute-start.13 = (bf16[24,4608]{1,0:T(8,128)(2,1)S(1)}, bf16[24,4608]{1,0:T(8,128)(2,1)S(1)}, u32[]{:S(2)}, u32[]{:S(2)}) collective-permute-start(bf16[24,4608]{1,0:T(8,128)(2,1)S(1)} %slice.17), channel_id=1, source_target_pairs={{0,4},{4,8},{8,12},{12,14},{14,10},{10,6},{6,2},{2,0},{1,5},{5,9},... | collective-permute-start | bytes 663560 | tf_op jit(solution)/shard_map/ppermute | solution.py:161
  85.7 0.6 collective-permute-start.14
  86.3 0.8 slice.15
  87.1 3.4 %collective-permute-done.13.refs_7_ = bf16[24,4608]{1,0:T(8,128)(2,1)S(1)} collective-permute-done((bf16[24,4608]{1,0:T(8,128)(2,1)S(1)}, bf16[24,4608]{1,0:T(8,128)(2,1)S(1)}, u32[]{:S(2)}, u32[]{:S(2)}) %collective-permute-start.13) | collective-permute-done | bytes 221216 | tf_op jit(solution)/shard_map/ppermute | solution.py:161
  90.5 1.3 collective-permute-done.14.refs_10_
  91.8 0.7 collective-permute-start.15
  92.5 1.3 %collective-permute-start.16 = (bf16[24,5888]{1,0:T(8,128)(2,1)S(1)}, bf16[24,5888]{1,0:T(8,128)(2,1)S(1)}, u32[]{:S(2)}, u32[]{:S(2)}) collective-permute-start(bf16[24,5888]{1,0:T(8,128)(2,1)S(1)} %slice.16), channel_id=1, source_target_pairs={{4,0},{8,4},{12,8},{14,12},{10,14},{6,10},{2,6},{0,2},{5,1},{9,5},... | collective-permute-start | bytes 847880 | tf_op jit(solution)/shard_map/ppermute | solution.py:164
  93.8 0.1 fusion.refs_12_
  94.6 6.4 %shard_map.85 = (f32[200,256]{1,0:T(8,128)}, f32[200,256]{1,0:T(8,128)}) custom-call(bf16[24,20992]{1,0:T(8,128)(2,1)} %get-tuple-element.32.refs_2_.refs_0_, bf16[24,20992]{1,0:T(8,128)(2,1)} %copy-done.4, bf16[24,20992]{1,0:T(8,128)(2,1)} %copy-done.5, bf16[24,20992]{1,0:T(8,128)(2,1)} %collective-permute-done.4.refs_3_, ...), custom_call_target="tpu_custom_call" | custom-call | flops 905969664 | bytes 14155776 | tf_op jit(solution)/shard_map/pallas_call | solution.py:273
  100.9 0.7 collective-permute-start.18
  101.6 0.0 collective-permute-done.15.refs_7_
  101.6 0.0 collective-permute-done.16.refs_14_.refs_8_
  101.6 0.0 collective-permute-done.17.refs_16_
  101.6 8.2 %shard_map.84 = (f32[192,512]{1,0:T(8,128)}, bf16[512,3584]{1,0:T(8,128)(2,1)}, bf16[24,3584]{1,0:T(8,128)(2,1)S(1)}, bf16[24,3584]{1,0:T(8,128)(2,1)S(1)}, bf16...) custom-call(bf16[24,20992]{1,0:T(8,128)(2,1)} %get-tuple-element.32., ...), custom_call_target="tpu_custom_call" | custom-call | flops 1610612736 | bytes 25165824 | tf_op jit(solution)/shard_map/pallas_call | solution.py:326
  109.9 0.0 collective-permute-done.18.refs_11_
  109.9 3.5 %shard_map.86 = (f32[1,128]{1,0:T(1,128)S(1)}, f32[1,128]{1,0:T(1,128)S(1)}) custom-call(bf16[24,3584]{1,0:T(8,128)(2,1)S(1)} %get-tuple-element.46.refs_0_, bf16[24,3584]{1,0:T(8,128)(2,1)S(1)} %get-tuple-element.47.refs_1_, bf16[24,3584]{1,0:T(8,128)(2,1)S(1)} %get-tuple-element.48.refs_2_, bf16[24,3584]{1,0:T(8,128)(2,1)S(1)} %get-tuple-element.49.refs_3_, ...), custom_call_target="tpu_custom_call" | custom-call | flops 704643072 | bytes 11010048 | tf_op jit(solution)/shard_map/pallas_call | solution.py:378
  113.4 1.5 %collective-permute-start.19 = (f32[1,128]{1,0:T(1,128)S(1)}, f32[1,128]{1,0:T(1,128)S(1)}, u32[]{:S(2)}, u32[]{:S(2)}) collective-permute-start(f32[1,128]{1,0:T(1,128)S(1)} %get-tuple-element.58), channel_id=1, source_target_pairs={{0,16},{16,0},{1,17},{17,1},{2,18},{18,2},{3,19},{19,3},{4,20},{20... | collective-permute-start | bytes 1544 | tf_op jit(solution)/shard_map/ppermute | solution.py:158
  114.9 2.1 %collective-permute-done.19 = f32[1,128]{1,0:T(1,128)S(1)} collective-permute-done((f32[1,128]{1,0:T(1,128)S(1)}, f32[1,128]{1,0:T(1,128)S(1)}, u32[]{:S(2)}, u32[]{:S(2)}) %collective-permute-start.19) | collective-permute-done | bytes 544 | tf_op jit(solution)/shard_map/ppermute | solution.py:158
  117.1 0.1 fusion.1
  117.1 0.0 collective-permute-start.20
  117.1 1.1 collective-permute-done.20
  118.3 0.1 fusion.3
  118.3 0.5 collective-permute-start.21
  118.9 3.0 %collective-permute-done.21 = f32[2,1,128]{2,1,0:T(1,128)S(1)} collective-permute-done((f32[2,1,128]{2,1,0:T(1,128)S(1)}, f32[2,1,128]{2,1,0:T(1,128)S(1)}, u32[]{:S(2)}, u32[]{:S(2)}) %collective-permute-start.21) | collective-permute-done | bytes 1056 | tf_op jit(solution)/shard_map/ppermute | solution.py:397
  121.9 0.1 fusion.4
  122.0 0.8 collective-permute-start.22
  122.8 2.8 %collective-permute-done.22 = f32[2,1,128]{2,1,0:T(1,128)S(1)} collective-permute-done((f32[2,1,128]{2,1,0:T(1,128)S(1)}, f32[2,1,128]{2,1,0:T(1,128)S(1)}, u32[]{:S(2)}, u32[]{:S(2)}) %collective-permute-start.22) | collective-permute-done | bytes 1056 | tf_op jit(solution)/shard_map/ppermute | solution.py:397
  125.6 0.8 collective-permute-start.23
  126.4 3.6 %collective-permute-done.23 = f32[2,1,128]{2,1,0:T(1,128)S(1)} collective-permute-done((f32[2,1,128]{2,1,0:T(1,128)S(1)}, f32[2,1,128]{2,1,0:T(1,128)S(1)}, u32[]{:S(2)}, u32[]{:S(2)}) %collective-permute-start.23) | collective-permute-done | bytes 1056 | tf_op jit(solution)/shard_map/ppermute | solution.py:397
  130.0 0.6 slice_add_fusion
  (28 shorter events, 0.1 us)
Async XLA Ops:
  0.0 32.0 %collective-permute-start.3 = (bf16[2,128,8192]{2,1,0:T(8,128)(2,1)}, bf16[2,128,8192]{2,1,0:T(8,128)(2,1)}, u32[]{:S(2)}, u32[]{:S(2)}) collective-permute-start(bf16[2,128,8192]{2,1,0:T(8,128)(2,1)} %refs_8_.2), channel_id=1, source_target_pairs={{0,1},{1,0},{2,3},{3,2},{4,5},{5,4},{6,7},{7,6},{8,9},{9,8},{10,11... | collective-permute-start | bytes 12582920 | tf_op jit(solution)/shard_map/ppermute | solution.py:155
  0.5 34.1 %collective-permute-start.7 = (bf16[2,128,8192]{2,1,0:T(8,128)(2,1)}, bf16[2,128,8192]{2,1,0:T(8,128)(2,1)}, u32[]{:S(2)}, u32[]{:S(2)}) collective-permute-start(bf16[2,128,8192]{2,1,0:T(8,128)(2,1)} %refs_8_.3), channel_id=1, source_target_pairs={{0,1},{1,0},{2,3},{3,2},{4,5},{5,4},{6,7},{7,6},{8,9},{9,8},{10,11... | collective-permute-start | bytes 12582920 | tf_op jit(solution)/shard_map/ppermute | solution.py:155
  3.5 28.5 %collective-permute-start.2 = (bf16[128,3968]{1,0:T(8,128)(2,1)}, bf16[128,3968]{1,0:T(8,128)(2,1)}, u32[]{:S(2)}, u32[]{:S(2)}) collective-permute-start(bf16[128,3968]{1,0:T(8,128)(2,1)} %get-tuple-element.34), channel_id=1, source_target_pairs={{0,16},{16,0},{1,17},{17,1},{2,18},{18,2},{3,19},{19,3},{4,20},{20... | collective-permute-start | bytes 3047432 | tf_op jit(solution)/shard_map/ppermute | solution.py:158
  6.5 53.9 %copy-start.9 = (s32[8]{0:T(128)S(1)}, s32[8]{0:T(128)}, u32[]{:S(2)}) copy-start(s32[8]{0:T(128)} %constant.89.clone) | copy-start | bytes 100
  6.5 54.5 %copy-start.8 = (s32[8]{0:T(128)S(1)}, s32[8]{0:T(128)}, u32[]{:S(2)}) copy-start(s32[8]{0:T(128)} %constant.91.clone) | copy-start | bytes 100
  6.5 55.2 %copy-start.1 = (s32[8]{0:T(128)S(1)}, s32[8]{0:T(128)}, u32[]{:S(2)}) copy-start(s32[8]{0:T(128)} %constant.90.clone) | copy-start | bytes 100
  6.5 24.1 %collective-permute-start = (bf16[24,20992]{1,0:T(8,128)(2,1)}, bf16[24,20992]{1,0:T(8,128)(2,1)S(1)}, u32[]{:S(2)}, u32[]{:S(2)}) collective-permute-start(bf16[24,20992]{1,0:T(8,128)(2,1)} %get-tuple-element.32.refs_2_.refs_0_), channel_id=1, source_target_pairs={{0,4},{4,8},{8,12},{12,14},{14,10},{10,6},{6,2},{2,0},{1,5},{5,9},... | collective-permute-start | bytes 3022856 | tf_op jit(solution)/shard_map/ppermute | solution.py:161
  8.1 23.8 %collective-permute-start.1 = (bf16[24,20992]{1,0:T(8,128)(2,1)}, bf16[24,20992]{1,0:T(8,128)(2,1)S(1)}, u32[]{:S(2)}, u32[]{:S(2)}) collective-permute-start(bf16[24,20992]{1,0:T(8,128)(2,1)} %get-tuple-element.32.refs_2_.refs_0_), channel_id=1, source_target_pairs={{4,0},{8,4},{12,8},{14,12},{10,14},{6,10},{2,6},{0,2},{5,1},{9,5},... | collective-permute-start | bytes 3022856 | tf_op jit(solution)/shard_map/ppermute | solution.py:164
  30.6 27.2 %copy-start.4 = (bf16[24,20992]{1,0:T(8,128)(2,1)}, bf16[24,20992]{1,0:T(8,128)(2,1)S(1)}, u32[]{:S(2)}) copy-start(bf16[24,20992]{1,0:T(8,128)(2,1)S(1)} %collective-permute-done.refs_1_) | copy-start | bytes 3022852
  31.9 25.9 %copy-start.5 = (bf16[24,20992]{1,0:T(8,128)(2,1)}, bf16[24,20992]{1,0:T(8,128)(2,1)S(1)}, u32[]{:S(2)}) copy-start(bf16[24,20992]{1,0:T(8,128)(2,1)S(1)} %collective-permute-done.1.refs_2_) | copy-start | bytes 3022852
  32.0 24.5 %collective-permute-start.6 = (bf16[128,3968]{1,0:T(8,128)(2,1)}, bf16[128,3968]{1,0:T(8,128)(2,1)}, u32[]{:S(2)}, u32[]{:S(2)}) collective-permute-start(bf16[128,3968]{1,0:T(8,128)(2,1)} %get-tuple-element.38), channel_id=1, source_target_pairs={{0,16},{16,0},{1,17},{17,1},{2,18},{18,2},{3,19},{19,3},{4,20},{20... | collective-permute-start | bytes 3047432 | tf_op jit(solution)/shard_map/ppermute | solution.py:158
  32.5 22.6 %collective-permute-start.4 = (bf16[24,20992]{1,0:T(8,128)(2,1)S(1)}, bf16[24,20992]{1,0:T(8,128)(2,1)}, u32[]{:S(2)}, u32[]{:S(2)}) collective-permute-start(bf16[24,20992]{1,0:T(8,128)(2,1)S(1)} %collective-permute-done.refs_1_), channel_id=1, source_target_pairs={{0,4},{4,8},{8,12},{12,14},{14,10},{10,6},{6,2},{2,0},{1,5},{5,9},... | collective-permute-start | bytes 3022856 | tf_op jit(solution)/shard_map/ppermute | solution.py:161
  34.1 22.4 %collective-permute-start.5 = (bf16[24,20992]{1,0:T(8,128)(2,1)S(1)}, bf16[24,20992]{1,0:T(8,128)(2,1)}, u32[]{:S(2)}, u32[]{:S(2)}) collective-permute-start(bf16[24,20992]{1,0:T(8,128)(2,1)S(1)} %collective-permute-done.1.refs_2_), channel_id=1, source_target_pairs={{4,0},{8,4},{12,8},{14,12},{10,14},{6,10},{2,6},{0,2},{5,1},{9,5},... | collective-permute-start | bytes 3022856 | tf_op jit(solution)/shard_map/ppermute | solution.py:164
  56.5 21.1 %collective-permute-start.10 = (bf16[128,3840]{1,0:T(8,128)(2,1)}, bf16[128,3840]{1,0:T(8,128)(2,1)}, u32[]{:S(2)}, u32[]{:S(2)}) collective-permute-start(bf16[128,3840]{1,0:T(8,128)(2,1)} %get-tuple-element.41), channel_id=1, source_target_pairs={{0,16},{16,0},{1,17},{17,1},{2,18},{18,2},{3,19},{19,3},{4,20},{20... | collective-permute-start | bytes 2949128 | tf_op jit(solution)/shard_map/ppermute | solution.py:158
  57.9 19.9 %collective-permute-start.11 = (bf16[128,3968]{1,0:T(8,128)(2,1)}, bf16[128,3968]{1,0:T(8,128)(2,1)}, u32[]{:S(2)}, u32[]{:S(2)}) collective-permute-start(bf16[128,3968]{1,0:T(8,128)(2,1)} %collective-permute-done.2.refs_10_), channel_id=1, source_target_pairs={{0,1},{1,0},{2,3},{3,2},{4,5},{5,4},{6,7},{7,6},{8,9},{9,8},{10,11... | collective-permute-start | bytes 3047432 | tf_op jit(solution)/shard_map/ppermute | solution.py:155
  57.9 26.3 %collective-permute-start.12 = (bf16[128,3968]{1,0:T(8,128)(2,1)}, bf16[128,3968]{1,0:T(8,128)(2,1)}, u32[]{:S(2)}, u32[]{:S(2)}) collective-permute-start(bf16[128,3968]{1,0:T(8,128)(2,1)} %collective-permute-done.6.refs_12_), channel_id=1, source_target_pairs={{0,1},{1,0},{2,3},{3,2},{4,5},{5,4},{6,7},{7,6},{8,9},{9,8},{10,11... | collective-permute-start | bytes 3047432 | tf_op jit(solution)/shard_map/ppermute | solution.py:155
  58.4 24.5 %collective-permute-start.8 = (bf16[24,20992]{1,0:T(8,128)(2,1)}, bf16[24,20992]{1,0:T(8,128)(2,1)S(1)}, u32[]{:S(2)}, u32[]{:S(2)}) collective-permute-start(bf16[24,20992]{1,0:T(8,128)(2,1)} %collective-permute-done.4.refs_3_), channel_id=1, source_target_pairs={{0,4},{4,8},{8,12},{12,14},{14,10},{10,6},{6,2},{2,0},{1,5},{5,9},... | collective-permute-start | bytes 3022856 | tf_op jit(solution)/shard_map/ppermute | solution.py:161
  60.0 24.2 %collective-permute-start.9 = (bf16[24,20992]{1,0:T(8,128)(2,1)}, bf16[24,20992]{1,0:T(8,128)(2,1)S(1)}, u32[]{:S(2)}, u32[]{:S(2)}) collective-permute-start(bf16[24,20992]{1,0:T(8,128)(2,1)} %collective-permute-done.5.refs_4_), channel_id=1, source_target_pairs={{4,0},{8,4},{12,8},{14,12},{10,14},{6,10},{2,6},{0,2},{5,1},{9,5},... | collective-permute-start | bytes 3022856 | tf_op jit(solution)/shard_map/ppermute | solution.py:164
  77.6 24.0 %collective-permute-start.17 = (bf16[128,3840]{1,0:T(8,128)(2,1)}, bf16[128,3840]{1,0:T(8,128)(2,1)}, u32[]{:S(2)}, u32[]{:S(2)}) collective-permute-start(bf16[128,3840]{1,0:T(8,128)(2,1)} %collective-permute-done.10.refs_15_), channel_id=1, source_target_pairs={{0,1},{1,0},{2,3},{3,2},{4,5},{5,4},{6,7},{7,6},{8,9},{9,8},{10,11... | collective-permute-start | bytes 2949128 | tf_op jit(solution)/shard_map/ppermute | solution.py:155
  82.9 11.7 %copy-start.2 = (bf16[24,20992]{1,0:T(8,128)(2,1)}, bf16[24,20992]{1,0:T(8,128)(2,1)S(1)}, u32[]{:S(2)}) copy-start(bf16[24,20992]{1,0:T(8,128)(2,1)S(1)} %collective-permute-done.8.refs_5_) | copy-start | bytes 3022852
  84.2 8.3 %copy-start.3 = (bf16[24,20992]{1,0:T(8,128)(2,1)}, bf16[24,20992]{1,0:T(8,128)(2,1)S(1)}, u32[]{:S(2)}) copy-start(bf16[24,20992]{1,0:T(8,128)(2,1)S(1)} %collective-permute-done.9.refs_6_) | copy-start | bytes 3022852
  84.2 6.3 %collective-permute-start.13 = (bf16[24,4608]{1,0:T(8,128)(2,1)S(1)}, bf16[24,4608]{1,0:T(8,128)(2,1)S(1)}, u32[]{:S(2)}, u32[]{:S(2)}) collective-permute-start(bf16[24,4608]{1,0:T(8,128)(2,1)S(1)} %slice.17), channel_id=1, source_target_pairs={{0,4},{4,8},{8,12},{12,14},{14,10},{10,6},{6,2},{2,0},{1,5},{5,9},... | collective-permute-start | bytes 663560 | tf_op jit(solution)/shard_map/ppermute | solution.py:161
  85.7 6.0 %collective-permute-start.14 = (bf16[24,4608]{1,0:T(8,128)(2,1)S(1)}, bf16[24,4608]{1,0:T(8,128)(2,1)S(1)}, u32[]{:S(2)}, u32[]{:S(2)}) collective-permute-start(bf16[24,4608]{1,0:T(8,128)(2,1)S(1)} %slice.18), channel_id=1, source_target_pairs={{4,0},{8,4},{12,8},{14,12},{10,14},{6,10},{2,6},{0,2},{5,1},{9,5},... | collective-permute-start | bytes 663560 | tf_op jit(solution)/shard_map/ppermute | solution.py:164
  90.5 3.3 %copy-start.6 = (bf16[24,4608]{1,0:T(8,128)(2,1)}, bf16[24,4608]{1,0:T(8,128)(2,1)S(1)}, u32[]{:S(2)}) copy-start(bf16[24,4608]{1,0:T(8,128)(2,1)S(1)} %collective-permute-done.13.refs_7_) | copy-start | bytes 663556
  91.8 2.1 %copy-start.7 = (bf16[24,4608]{1,0:T(8,128)(2,1)}, bf16[24,4608]{1,0:T(8,128)(2,1)S(1)}, u32[]{:S(2)}) copy-start(bf16[24,4608]{1,0:T(8,128)(2,1)S(1)} %collective-permute-done.14.refs_10_) | copy-start | bytes 663556
  91.8 9.8 %collective-permute-start.15 = (bf16[24,5888]{1,0:T(8,128)(2,1)}, bf16[24,5888]{1,0:T(8,128)(2,1)S(1)}, u32[]{:S(2)}, u32[]{:S(2)}) collective-permute-start(bf16[24,5888]{1,0:T(8,128)(2,1)} %slice.15), channel_id=1, source_target_pairs={{0,4},{4,8},{8,12},{12,14},{14,10},{10,6},{6,2},{2,0},{1,5},{5,9},... | collective-permute-start | bytes 847880 | tf_op jit(solution)/shard_map/ppermute | solution.py:161
  92.5 9.1 %collective-permute-start.16 = (bf16[24,5888]{1,0:T(8,128)(2,1)S(1)}, bf16[24,5888]{1,0:T(8,128)(2,1)S(1)}, u32[]{:S(2)}, u32[]{:S(2)}) collective-permute-start(bf16[24,5888]{1,0:T(8,128)(2,1)S(1)} %slice.16), channel_id=1, source_target_pairs={{4,0},{8,4},{12,8},{14,12},{10,14},{6,10},{2,6},{0,2},{5,1},{9,5},... | collective-permute-start | bytes 847880 | tf_op jit(solution)/shard_map/ppermute | solution.py:164
  100.9 9.0 %collective-permute-start.18 = (f32[200,256]{1,0:T(8,128)}, f32[200,256]{1,0:T(8,128)S(1)}, u32[]{:S(2)}, u32[]{:S(2)}) collective-permute-start(f32[200,256]{1,0:T(8,128)} %get-tuple-element.56), channel_id=1, source_target_pairs={{0,16},{16,0},{1,17},{17,1},{2,18},{18,2},{3,19},{19,3},{4,20},{20... | collective-permute-start | bytes 614408 | tf_op jit(solution)/shard_map/ppermute | solution.py:158
  101.6 8.3 %copy-start = (f32[200,256]{1,0:T(8,128)S(1)}, f32[200,256]{1,0:T(8,128)}, u32[]{:S(2)}) copy-start(f32[200,256]{1,0:T(8,128)} %get-tuple-element.55.refs_10_) | copy-start | bytes 614404
  113.4 3.6 %collective-permute-start.19 = (f32[1,128]{1,0:T(1,128)S(1)}, f32[1,128]{1,0:T(1,128)S(1)}, u32[]{:S(2)}, u32[]{:S(2)}) collective-permute-start(f32[1,128]{1,0:T(1,128)S(1)} %get-tuple-element.58), channel_id=1, source_target_pairs={{0,16},{16,0},{1,17},{17,1},{2,18},{18,2},{3,19},{19,3},{4,20},{20... | collective-permute-start | bytes 1544 | tf_op jit(solution)/shard_map/ppermute | solution.py:158
  117.1 1.1 collective-permute-start.20
  118.3 3.6 %collective-permute-start.21 = (f32[2,1,128]{2,1,0:T(1,128)S(1)}, f32[2,1,128]{2,1,0:T(1,128)S(1)}, u32[]{:S(2)}, u32[]{:S(2)}) collective-permute-start(f32[2,1,128]{2,1,0:T(1,128)S(1)} %fusion.3), channel_id=1, source_target_pairs={{0,2},{1,3},{2,0},{3,1},{4,6},{5,7},{6,4},{7,5},{8,10},{9,11},{10,... | collective-permute-start | bytes 3080 | tf_op jit(solution)/shard_map/ppermute | solution.py:397
  122.0 3.6 %collective-permute-start.22 = (f32[2,1,128]{2,1,0:T(1,128)S(1)}, f32[2,1,128]{2,1,0:T(1,128)S(1)}, u32[]{:S(2)}, u32[]{:S(2)}) collective-permute-start(f32[2,1,128]{2,1,0:T(1,128)S(1)} %fusion.4), channel_id=1, source_target_pairs={{0,4},{1,5},{2,6},{3,7},{4,0},{5,1},{6,2},{7,3},{8,12},{9,13},{10,... | collective-permute-start | bytes 3080 | tf_op jit(solution)/shard_map/ppermute | solution.py:397
  125.6 4.5 %collective-permute-start.23 = (f32[2,1,128]{2,1,0:T(1,128)S(1)}, f32[2,1,128]{2,1,0:T(1,128)S(1)}, u32[]{:S(2)}, u32[]{:S(2)}) collective-permute-start(f32[2,1,128]{2,1,0:T(1,128)S(1)} %add.86), channel_id=1, source_target_pairs={{0,8},{1,9},{2,10},{3,11},{4,12},{5,13},{6,14},{7,15},{8,0},{9,1},... | collective-permute-start | bytes 3080 | tf_op jit(solution)/shard_map/ppermute | solution.py:397

commit v3 on v2

v3 whole, which is shorter than its diff:
```python
import math

import jax
import jax.numpy as jnp
from jax import lax
from jax.experimental import pallas as pl
from jax.experimental.pallas import tpu as pltpu
from jax.sharding import PartitionSpec as P

RANK = 32
LEN = 2048
MIB = 2**20
SPAN = 512
RESERVE = 8
OUTER = 50
ANYWHERE = pl.BlockSpec(memory_space=pl.ANY)
CHIP = pl.BlockSpec(memory_space=pltpu.VMEM)


def chip_ring(chips):
    return list(range(0, chips, 2)) + list(range(chips - 1, 0, -2))


def contract(left, right):
    return lax.dot_general(
        left, right, (((1,), (1,)), ((), ())), preferred_element_type=jnp.float32
    )


def rows_of(pieces):
    return jnp.concatenate(pieces, axis=0) if len(pieces) > 1 else pieces[0]


def move(sources, targets, after=()):
    count = len(sources)
    moves, shapes = [], []
    for t, ranges in enumerate(targets):
        offset = 0
        for s, layer, start, stop in ranges:
            moves.append((t, s, layer, start, stop, offset))
            offset += stop - start
        lead = sources[s].shape[:2] if layer is None else sources[s].shape[1:2]
        shapes.append(jax.ShapeDtypeStruct((*lead, offset), sources[s].dtype))

    def kernel(*refs):
        ins, outs, sems = refs[:count], refs[count + len(after) : -1], refs[-1]
        me = lax.axis_index("grp")
        copies = []
        for k, (t, s, layer, start, stop, offset) in enumerate(moves):
            columns, place = pl.ds(start, stop - start), pl.ds(offset, stop - start)
            if layer is None:
                source, target = ins[s].at[:, :, columns], outs[t].at[:, :, place]
            else:
                row = {"mine": me, "other": 1 - me}.get(layer, layer)
                source, target = ins[s].at[row, :, columns], outs[t].at[:, place]
            copies.append(pltpu.make_async_copy(source, target, sems.at[k]))
            copies[-1].start()
        for copy in copies:
            copy.wait()

    return pl.pallas_call(
        kernel,
        out_shape=shapes,
        in_specs=[ANYWHERE] * (count + len(after)),
        out_specs=[CHIP] * len(shapes),
        scratch_shapes=[pltpu.SemaphoreType.DMA((len(moves),))],
        compiler_params=pltpu.CompilerParams(vmem_limit_bytes=62 * MIB),
        cost_estimate=pl.CostEstimate(
            flops=0,
            transcendentals=0,
            bytes_accessed=4 * sum(math.prod(x.shape) * 2 for x in shapes),
        ),
    )(*sources, *after)


def cost(flops):
    return pl.CostEstimate(flops=flops, transcendentals=0, bytes_accessed=flops // 64)


class Loads:

    def __init__(self):
        self.arrays, self.keys = [], []

    def add(self, array, lead, first, width):
        for k, known in enumerate(self.arrays):
            if known is array:
                break
        else:
            k = len(self.arrays)
            self.arrays.append(array)
        self.keys.append((k, lead, first, width))
        return len(self.keys) - 1

    def scratch(self):
        buffers = [
            pltpu.VMEM((self.arrays[k].shape[-2], width), self.arrays[k].dtype)
            for k, _, _, width in self.keys
        ]
        return [*buffers, pltpu.SemaphoreType.DMA((len(self.keys),))]

    def start(self, ins, buffers):
        self.copies, self.refs = [], buffers[:-1]
        for i, (k, lead, first, width) in enumerate(self.keys):
            columns = pl.ds(first, width)
            row = lax.axis_index("grp") if lead == "mine" else lead
            source = ins[k].at[:, columns] if lead is None else ins[k].at[row, :, columns]
            self.copies.append(pltpu.make_async_copy(source, buffers[i], buffers[-1].at[i]))
            self.copies[-1].start()

    def wait(self, wanted):
        for i in sorted(set(wanted)):
            if self.copies[i] is not None:
                self.copies[i].wait()
                self.copies[i] = None


def products(total, tokens, factors, width):
    for a in range(0, width, SPAN):
        span = min(SPAN, width - a)
        left = rows_of([ref[:, first + a : first + a + span] for ref, first in tokens])
        right = rows_of([ref[:, first + a : first + a + span] for ref, first in factors])
        product = contract(left, right)
        total = product if total is None else total + product
    return total


def solution(mesh):
    blk = mesh.shape["blk"]
    chips = blk // 2
    full = (chips - 1) // 2
    order = chip_ring(chips)
    forward, backward = [], []
    for core in range(2):
        for k in range(chips):
            a = order[k] * 2 + core
            b = order[(k + 1) % chips] * 2 + core
            forward.append((a, b))
            backward.append((b, a))
    def swap_core(x):
        return lax.ppermute(x, "blk", [(i, i ^ 1) for i in range(blk)])

    def swap_grp(x):
        return lax.ppermute(x, "grp", [(0, 1), (1, 0)])

    def ahead_of(x):
        return lax.ppermute(x, "blk", forward)

    def back_of(x):
        return lax.ppermute(x, "blk", backward)

    def after(values, *others):
        return lax.optimization_barrier((*values, *others))[: len(values)]

    def shards(activations, backprops, out_factors, in_factors, lengths):
        tokens_here = activations.shape[1]
        width = backprops.shape[2]
        depth = activations.shape[2]
        cut = depth * 5 // 8
        packed = width + cut
        beyond = depth - cut
        columns = out_factors.shape[1]
        seq_count = lengths.shape[0]
        me = lax.axis_index("grp")
        device = lax.axis_index("blk")

        def packing(out_source, in_source, layer, start, stop):
            ranges = []
            if start < width:
                ranges.append((out_source, layer, start, min(stop, width)))
            if stop > width:
                ranges.append((in_source, layer, max(start - width, 0), stop - width))
            return ranges

        edges = [0, width // 2, width, packed]

        def away_part(k):
            return packing(1, 0, "other", edges[k], edges[k + 1])

        acts_sib, backs_sib = swap_core(activations), swap_core(backprops)

        sources = (activations, backprops)
        piece, *chunks = move(
            (*sources, out_factors, in_factors),
            [
                packing(2, 3, "mine", 0, packed) + [(3, k, cut, depth) for k in range(2)],
                away_part(0),
            ],
        )
        chunks += move(sources, [away_part(1), away_part(2)], after=(piece,))

        got = [piece]
        ahead = back = piece
        away, away_sib = [], []
        for step in range(full):
            given = [ahead, back]
            if step < 3:
                given.append(chunks[step])
            if step == 1:
                given = after(given, away[0], *chunks[1:], backs_sib)
            if step == 2:
                given = after(given, away[1], acts_sib)
                away_sib = [swap_core(x) for x in away]
            ahead, back = ahead_of(given[0]), back_of(given[1])
            if step < 3:
                away.append(swap_grp(given[2]))
            got += [ahead, back]
        total = packed + 2 * beyond
        middle = total // 2
        chip_tokens = 2 * tokens_here
        shard_rows = chips * columns
        if chips > 8:
            got = [jnp.concatenate(got, axis=0)]
        queries = columns * blk // RANK
        steps = [0]
        for k in range(1, full + 1):
            steps += [-k, k]
        steps.append(chips // 2)

        last = ahead_of(ahead[:, :middle]), back_of(back[:, middle:])
        away_sib.append(swap_core(after((away[2],), *last)[0]))
        own = ((backprops, backs_sib), (activations, acts_sib))
        lanes = -(-(shard_rows + 1) // 128) * 128

        def shard_pieces(loads, first, width):
            pieces = [loads.add(g, None, first, width) for g in got]
            if first < middle:
                return [*pieces, loads.add(last[0], None, first, width)]
            return [*pieces, loads.add(last[1], None, first - middle, width)]

        home_loads = Loads()
        home_plan = []
        for k in range(2):
            tokens = [home_loads.add(x, k, cut, beyond) for x in own[1]]
            home_plan.append((tokens, shard_pieces(home_loads, packed + k * beyond, beyond)))
        count_home = len(home_loads.arrays)

        def home_kernel(*refs):
            lengths_ref, mine_ref, other_ref, *scratch = refs[count_home:]
            home_loads.start(refs[:count_home], scratch)
            me = lax.axis_index("grp")
            first = lax.axis_index("blk") // 2 * chip_tokens
            limit = lengths_ref[first // LEN].astype(jnp.float32)
            for ref in (mine_ref, other_ref):
                ref[:, shard_rows:] = jnp.full((chip_tokens, lanes - shard_rows), limit)
            for k, sides in enumerate(home_plan):
                for side in sides:
                    home_loads.wait(side)
                tokens, factors = ([(home_loads.refs[i], 0) for i in side] for side in sides)
                value = products(None, tokens, factors, beyond)

                @pl.when(me == k)
                def _():
                    mine_ref[:, :shard_rows] = value

                @pl.when(me != k)
                def _():
                    other_ref[:, :shard_rows] = value

        extra = jax.ShapeDtypeStruct((chip_tokens, lanes), jnp.float32)
        home_mine, home_away = pl.pallas_call(
            home_kernel,
            out_shape=[extra] * 2,
            in_specs=[ANYWHERE] * count_home + [pl.BlockSpec(memory_space=pltpu.SMEM)],
            out_specs=[CHIP] * 2,
            scratch_shapes=home_loads.scratch(),
            compiler_params=pltpu.CompilerParams(vmem_limit_bytes=OUTER * MIB),
            cost_estimate=cost(2 * shard_rows * chip_tokens * 2 * beyond),
        )(*home_loads.arrays, lengths)
        home_away = swap_grp(home_away)

        main_loads = Loads()
        main_plan = []
        points = sorted({0, width // 2, width, middle, packed, *edges[1:]})
        for a, b in zip(points[:-1], points[1:]):
            k = max(i for i in range(3) if edges[i] <= a)
            side = int(a >= width)
            factors = shard_pieces(main_loads, a, b - a)
            tokens = [main_loads.add(x, "mine", a - side * width, b - a) for x in own[side]]
            tokens += [main_loads.add(x[k], None, a - edges[k], b - a) for x in (away, away_sib)]
            main_plan.append((side, tokens, factors, b - a))
        count_main = len(main_loads.arrays)

        def main_kernel(*refs):
            out_refs, scratch = refs[count_main : count_main + 2], refs[count_main + 2 :]
            main_loads.start(refs[:count_main], scratch)
            totals = [None, None]
            for side, tokens, factors, span in main_plan:
                main_loads.wait([*tokens, *factors])
                pieces = ([(main_loads.refs[i], 0) for i in x] for x in (tokens, factors))
                totals[side] = products(totals[side], *pieces, span)
            for ref, total in zip(out_refs, totals):
                ref[...] = total

        proj = jax.ShapeDtypeStruct((2 * chip_tokens, shard_rows), jnp.float32)
        proj_out, proj_in = pl.pallas_call(
            main_kernel,
            out_shape=[proj] * 2,
            in_specs=[ANYWHERE] * count_main,
            out_specs=[CHIP] * 2,
            scratch_shapes=main_loads.scratch(),
            compiler_params=pltpu.CompilerParams(vmem_limit_bytes=OUTER * MIB),
            cost_estimate=cost(2 * shard_rows * 2 * chip_tokens * packed),
        )(*main_loads.arrays)

        def score_kernel(*refs):
            out_ref, in_ref, mine_ref, other_ref, *scores = refs
            chip, odd = lax.axis_index("blk") // 2, lax.axis_index("blk") % 2
            at = jnp.where(chip % 2 == 0, chip // 2, chips - (chip + 1) // 2)
            within = lax.broadcasted_iota(jnp.int32, (columns, 128), 0)
            lowest = lax.broadcasted_iota(jnp.int32, (columns, 128), 1) * RANK
            hits = []
            for step in steps:
                p = (at + step + chips) % chips
                there = jnp.where(p < chips // 2, 2 * p, 2 * (chips - 1 - p) + 1)
                column = (there * 2 + odd) * columns + within
                hits.append(((column >= lowest) & (column < lowest + RANK)).astype(jnp.float32))
            hit = rows_of(hits)
            first = lax.axis_index("blk") // 2 * chip_tokens
            flip = lax.axis_index("blk") % 2
            row = lax.broadcasted_iota(jnp.int32, (chip_tokens, 1), 0)
            swapped = jnp.where(row < tokens_here, row + tokens_here, row - tokens_here)
            position = (first % LEN + jnp.where(flip == 1, swapped, row)).astype(jnp.float32)
            for k, extra_ref in enumerate((mine_ref, other_ref)):
                span = slice(k * chip_tokens, (k + 1) * chip_tokens)
                in_use = position < extra_ref[:, shard_rows : shard_rows + 1]
                product = out_ref[span, :] * (in_ref[span, :] + extra_ref[:, :shard_rows])
                product = jnp.where(in_use, product, 0.0)
                per_column = jnp.sum(product, axis=0, keepdims=True)
                scores[k][...] = lax.dot_general(
                    per_column,
                    hit,
                    (((1,), (0,)), ((), ())),
                    precision=lax.Precision.HIGHEST,
                    preferred_element_type=jnp.float32,
                )

        scored, other = pl.pallas_call(
            score_kernel,
            out_shape=[jax.ShapeDtypeStruct((1, 128), jnp.float32)] * 2,
            in_specs=[CHIP] * 4,
            out_specs=[CHIP] * 2,
            compiler_params=pltpu.CompilerParams(vmem_limit_bytes=RESERVE * MIB),
        )(proj_out, proj_in, home_mine, home_away)

        other = swap_grp(other)
        sequence = device // 2 * chip_tokens // LEN
        select = jnp.arange(seq_count, dtype=jnp.int32) == sequence
        rows = jnp.arange(2)[:, None] == me
        value = jnp.where(rows, scored, other)
        value = value[:, None, :] * select.astype(jnp.float32)[None, :, None]
        if blk & (blk - 1):
            return lax.psum(value, "blk")[:, :, :queries]
        bit = 1
        while bit < blk:
            value = value + lax.ppermute(value, "blk", [(i, i ^ bit) for i in range(blk)])
            bit *= 2
        return value[:, :, :queries]

    placed = (
        P(None, ("grp", "blk"), None),
        P(None, ("grp", "blk"), None),
        P(None, "blk", None),
        P(None, "blk", None),
        P("grp"),
    )
    return jax.shard_map(
        shards, mesh=mesh, in_specs=placed, out_specs=P(None, "grp", None), check_vma=False
    )
```

time: 131 us -> 124 us (0.947)
  waiting for transfers between devices: 81.4 us -> 77.7 us
  Pallas kernels: 24 us -> 21.9 us
  local copies, waits for them, and re-layouts: 2.15 us -> 0.8 us
    ppermute x5, waiting for transfers between devices: 17.4 us -> 11 us  [swap_grp(): return lax.ppermute(x, 'grp', [(0, 1), (1, 0)])]
    ppermute x5 -> x4, waiting for transfers between devices: 48.3 us -> 54.6 us  [ahead_of(): return lax.ppermute(x, 'blk', forward)]
    ppermute x4, starting transfers between devices: 2.17 us -> 4.64 us  [shards(): lax.ppermute(value, 'blk', [(i, i ^ bit) for i in range(blk)])]
    ppermute x4, waiting for transfers between devices: 10.6 us -> 8.11 us  [shards(): lax.ppermute(value, 'blk', [(i, i ^ bit) for i in range(blk)])]
    pallas_call x1, Pallas kernels: 3.53 us -> 1.4 us  [shards(): pl.pallas_call(score_kernel, out_shape=[jax.ShapeDtypeStruct((1, 128), jn...]
    pallas_call x1, Pallas kernels: 6.36 us -> 4.45 us  [shards(): pl.pallas_call(home_kernel, out_shape=[extra] * 2, in_specs=[ANYWHERE] *...]
    pallas_call x1, Pallas kernels: 8.24 us -> 10.1 us  [shards(): pl.pallas_call(main_kernel, out_shape=[proj] * 2, in_specs=[ANYWHERE] * c...]
    ppermute x5 -> x4, waiting for transfers between devices: 5.17 us -> 4 us  [back_of(): return lax.ppermute(x, 'blk', backward)]
  transfers between devices with their start and end apart: 24 -> 22, of which waited for: 14 -> 14; matrix products, arithmetic and copies ran while one was open for 2% -> 0% of each run, Pallas kernels for 16% -> 17%
where the time goes in v3:
time: 124 us
  waiting for transfers between devices  77.7 us (63%)
  starting transfers between devices  21.9 us (18%)
  Pallas kernels  21.9 us (18%)
    ppermute x4, waiting for transfers between devices, ahead_of(): return lax.ppermute(x, 'blk', forward)  54.6 us
    ppermute x5, waiting for transfers between devices, swap_grp(): return lax.ppermute(x, 'grp', [(0, 1), (1, 0)])  11 us
    pallas_call x1, Pallas kernels, shards(): pl.pallas_call(main_kernel, out_shape=[proj] * 2, in_specs=[ANYWHERE] * c...  10.1 us
    ppermute x4, waiting for transfers between devices, shards(): lax.ppermute(value, 'blk', [(i, i ^ bit) for i in range(blk)])  8.11 us
    ppermute x5, starting transfers between devices, swap_grp(): return lax.ppermute(x, 'grp', [(0, 1), (1, 0)])  7.92 us
    ppermute x4, starting transfers between devices, ahead_of(): return lax.ppermute(x, 'blk', forward)  6.06 us
    pallas_call x2, Pallas kernels, move(): pl.pallas_call(kernel, out_shape=shapes, in_specs=[ANYWHERE] * (count + l...  6 us
    ppermute x4, starting transfers between devices, shards(): lax.ppermute(value, 'blk', [(i, i ^ bit) for i in range(blk)])  4.64 us
  transfers between devices with their start and end apart: 22, of which 14 were waited for; matrix products, arithmetic and copies ran while one was open for 0% of the time, Pallas kernels for 17%

profile of v3, /device:TPU:0, one launch (start us, length us, event | category | flops | bytes accessed | tf_op | source)
XLA Modules:
  0.0 123.9 jit_solution(4896408019518357733)
XLA Ops:
  0.0 0.5 collective-permute-start.3
  0.5 0.1 collective-permute-start.7
  0.5 3.0 %shard_map.55 = (bf16[24,19456]{1,0:T(8,128)(2,1)}, bf16[128,4096]{1,0:T(8,128)(2,1)}) custom-call(bf16[2,128,8192]{2,1,0:T(8,128)(2,1)} %refs_0_.5, bf16[2,128,8192]{2,1,0:T(8,128)(2,1)} %refs_8_.1, bf16[2,24,8192]{2,1,0:T(8,128)(2,1)} %refs_2_.1, bf16[2,24,8192]{2,1,0:T(8,128)(2,1)} %refs_3_.1), custom_call_target="tpu_custom_call" | custom-call | bytes 7929856 | tf_op jit(solution)/shard_map/pallas_call | solution.py:61
  3.5 3.0 %collective-permute-start.2 = (bf16[128,4096]{1,0:T(8,128)(2,1)}, bf16[128,4096]{1,0:T(8,128)(2,1)}, u32[]{:S(2)}, u32[]{:S(2)}) collective-permute-start(bf16[128,4096]{1,0:T(8,128)(2,1)} %get-tuple-element.24), channel_id=1, source_target_pairs={{0,16},{16,0},{1,17},{17,1},{2,18},{18,2},{3,19},{19,3},{4,20},{20... | collective-permute-start | bytes 3145736 | tf_op jit(solution)/shard_map/ppermute | solution.py:144
  6.5 0.0 copy-start
  6.5 1.6 %collective-permute-start = (bf16[24,19456]{1,0:T(8,128)(2,1)}, bf16[24,19456]{1,0:T(8,128)(2,1)S(1)}, u32[]{:S(2)}, u32[]{:S(2)}) collective-permute-start(bf16[24,19456]{1,0:T(8,128)(2,1)} %get-tuple-element.22.refs_2_.refs_0_), channel_id=1, source_target_pairs={{0,4},{4,8},{8,12},{12,14},{14,10},{10,6},{6,2},{2,0},{1,5},{5,9},... | collective-permute-start | bytes 2801672 | tf_op jit(solution)/shard_map/ppermute | solution.py:147
  8.1 0.4 collective-permute-start.1
  8.6 3.0 %shard_map.56 = (bf16[128,4096]{1,0:T(8,128)(2,1)}, bf16[128,5120]{1,0:T(8,128)(2,1)}) custom-call(bf16[2,128,8192]{2,1,0:T(8,128)(2,1)} %refs_0_.5, bf16[2,128,8192]{2,1,0:T(8,128)(2,1)} %refs_8_.1, bf16[24,19456]{1,0:T(8,128)(2,1)} %get-tuple-element.22.refs_2_.refs_0_), custom_call_target="tpu_custom_call" | custom-call | bytes 9437184 | tf_op jit(solution)/shard_map/pallas_call | solution.py:61
  11.6 17.5 %collective-permute-done.refs_1_.refs_3_ = bf16[24,19456]{1,0:T(8,128)(2,1)S(1)} collective-permute-done((bf16[24,19456]{1,0:T(8,128)(2,1)}, bf16[24,19456]{1,0:T(8,128)(2,1)S(1)}, u32[]{:S(2)}, u32[]{:S(2)}) %collective-permute-start) | collective-permute-done | bytes 933920 | tf_op jit(solution)/shard_map/ppermute | solution.py:147
  29.1 1.4 %collective-permute-done.1.refs_2_.refs_4_ = bf16[24,19456]{1,0:T(8,128)(2,1)} collective-permute-done((bf16[24,19456]{1,0:T(8,128)(2,1)}, bf16[24,19456]{1,0:T(8,128)(2,1)}, u32[]{:S(2)}, u32[]{:S(2)}) %collective-permute-start.1) | collective-permute-done | bytes 933920 | tf_op jit(solution)/shard_map/ppermute | solution.py:150
  30.5 0.0 collective-permute-done.2.refs_10_
  30.5 0.0 collective-permute-done.3.refs_9_
  30.5 1.4 %collective-permute-start.6 = (bf16[128,4096]{1,0:T(8,128)(2,1)}, bf16[128,4096]{1,0:T(8,128)(2,1)}, u32[]{:S(2)}, u32[]{:S(2)}) collective-permute-start(bf16[128,4096]{1,0:T(8,128)(2,1)} %get-tuple-element.28), channel_id=1, source_target_pairs={{0,16},{16,0},{1,17},{17,1},{2,18},{18,2},{3,19},{19,3},{4,20},{20... | collective-permute-start | bytes 3145736 | tf_op jit(solution)/shard_map/ppermute | solution.py:144
  31.9 1.6 %collective-permute-start.4 = (bf16[24,19456]{1,0:T(8,128)(2,1)S(1)}, bf16[24,19456]{1,0:T(8,128)(2,1)S(1)}, u32[]{:S(2)}, u32[]{:S(2)}) collective-permute-start(bf16[24,19456]{1,0:T(8,128)(2,1)S(1)} %collective-permute-done.refs_1_.refs_3_), channel_id=1, source_target_pairs={{0,4},{4,8},{8,12},{12,14},{14,10},{10,6},{6,2},{2,0},{1,5},{5,9},... | collective-permute-start | bytes 2801672 | tf_op jit(solution)/shard_map/ppermute | solution.py:147
  33.5 0.4 collective-permute-start.5
  33.9 0.0 collective-permute-done.7.refs_15_.refs_1_
  33.9 19.4 %collective-permute-done.4.refs_3_.refs_5_ = bf16[24,19456]{1,0:T(8,128)(2,1)S(1)} collective-permute-done((bf16[24,19456]{1,0:T(8,128)(2,1)S(1)}, bf16[24,19456]{1,0:T(8,128)(2,1)S(1)}, u32[]{:S(2)}, u32[]{:S(2)}) %collective-permute-start.4) | collective-permute-done | bytes 933920 | tf_op jit(solution)/shard_map/ppermute | solution.py:147
  53.4 1.5 %collective-permute-done.5.refs_4_.refs_6_ = bf16[24,19456]{1,0:T(8,128)(2,1)S(1)} collective-permute-done((bf16[24,19456]{1,0:T(8,128)(2,1)}, bf16[24,19456]{1,0:T(8,128)(2,1)S(1)}, u32[]{:S(2)}, u32[]{:S(2)}) %collective-permute-start.5) | collective-permute-done | bytes 933920 | tf_op jit(solution)/shard_map/ppermute | solution.py:150
  54.9 0.0 copy-start.6
  54.9 0.1 collective-permute-done.6.refs_12_
  55.0 1.5 %collective-permute-start.8 = (bf16[24,19456]{1,0:T(8,128)(2,1)S(1)}, bf16[24,19456]{1,0:T(8,128)(2,1)S(1)}, u32[]{:S(2)}, u32[]{:S(2)}) collective-permute-start(bf16[24,19456]{1,0:T(8,128)(2,1)S(1)} %collective-permute-done.4.refs_3_.refs_5_), channel_id=1, source_target_pairs={{0,4},{4,8},{8,12},{12,14},{14,10},{10,6},{6,2},{2,0},{1,5},{5,9},... | collective-permute-start | bytes 2801672 | tf_op jit(solution)/shard_map/ppermute | solution.py:147
  56.5 0.5 collective-permute-start.9
  57.1 0.0 copy-done.5
  57.1 1.4 %collective-permute-start.13 = (bf16[128,5120]{1,0:T(8,128)(2,1)}, bf16[128,5120]{1,0:T(8,128)(2,1)}, u32[]{:S(2)}, u32[]{:S(2)}) collective-permute-start(bf16[128,5120]{1,0:T(8,128)(2,1)} %get-tuple-element.31), channel_id=1, source_target_pairs={{0,16},{16,0},{1,17},{17,1},{2,18},{18,2},{3,19},{19,3},{4,20},{20... | collective-permute-start | bytes 3932168 | tf_op jit(solution)/shard_map/ppermute | solution.py:144
  58.5 17.4 %collective-permute-done.8.refs_5_.refs_7_ = bf16[24,19456]{1,0:T(8,128)(2,1)S(1)} collective-permute-done((bf16[24,19456]{1,0:T(8,128)(2,1)S(1)}, bf16[24,19456]{1,0:T(8,128)(2,1)S(1)}, u32[]{:S(2)}, u32[]{:S(2)}) %collective-permute-start.8) | collective-permute-done | bytes 933920 | tf_op jit(solution)/shard_map/ppermute | solution.py:147
  75.9 0.0 copy-start.3
  75.9 1.4 %collective-permute-start.10 = (bf16[24,9728]{1,0:T(8,128)(2,1)S(1)}, bf16[24,9728]{1,0:T(8,128)(2,1)S(1)}, u32[]{:S(2)}, u32[]{:S(2)}) collective-permute-start(bf16[24,9728]{1,0:T(8,128)(2,1)S(1)} %slice.12), channel_id=1, source_target_pairs={{0,4},{4,8},{8,12},{12,14},{14,10},{10,6},{6,2},{2,0},{1,5},{5,9},... | collective-permute-start | bytes 1400840 | tf_op jit(solution)/shard_map/ppermute | solution.py:147
  77.3 0.0 collective-permute-done.9.refs_6_.refs_8_
  77.4 0.7 collective-permute-start.14
  78.1 7.7 %collective-permute-done.13.refs_16_ = bf16[128,5120]{1,0:T(8,128)(2,1)} collective-permute-done((bf16[128,5120]{1,0:T(8,128)(2,1)}, bf16[128,5120]{1,0:T(8,128)(2,1)}, u32[]{:S(2)}, u32[]{:S(2)}) %collective-permute-start.13) | collective-permute-done | bytes 1310752 | tf_op jit(solution)/shard_map/ppermute | solution.py:144
  85.7 0.3 collective-permute-done.10.refs_7_
  86.0 1.1 collective-permute-done.14.refs_18_.refs_9_
  87.1 0.0 copy-done.3
  87.1 0.0 collective-permute-start.15
  87.1 0.0 copy-done.4
  87.1 0.5 collective-permute-start.11
  87.6 0.0 copy-done.6
  87.6 0.1 collective-permute-start.12
  88.3 0.0 copy-done
  88.3 4.5 %shard_map.58 = (f32[256,256]{1,0:T(8,128)S(1)}, f32[256,256]{1,0:T(8,128)}) custom-call(bf16[2,128,8192]{2,1,0:T(8,128)(2,1)} %refs_0_.5, bf16[2,128,8192]{2,1,0:T(8,128)(2,1)} %collective-permute-done.7.refs_15_.refs_1_, bf16[24,19456]{1,0:T(8,128)(2,1)S(1)} %copy-done, bf16[24,19456]{1,0:T(8,128)(2,1)S(1)} %collective-permute-done.refs_1_.refs_3_, ...), custom_call_target="tpu_custom_call" | custom-call | flops 603979776 | bytes 9437184 | tf_op jit(solution)/shard_map/pallas_call | solution.py:261
  92.8 0.0 copy-start.1
  92.8 0.7 copy-done.1
  93.5 1.7 %collective-permute-start.16 = (f32[256,256]{1,0:T(8,128)}, f32[256,256]{1,0:T(8,128)}, u32[]{:S(2)}, u32[]{:S(2)}) collective-permute-start(f32[256,256]{1,0:T(8,128)} %get-tuple-element.36), channel_id=1, source_target_pairs={{0,16},{16,0},{1,17},{17,1},{2,18},{18,2},{3,19},{19,3},{4,20},{20... | collective-permute-start | bytes 786440 | tf_op jit(solution)/shard_map/ppermute | solution.py:144
  95.2 0.0 collective-permute-done.11.refs_11_
  95.2 0.0 collective-permute-done.12.refs_13_
  95.2 0.0 collective-permute-done.15.refs_17_
  95.2 10.1 %shard_map.57 = (f32[512,192]{1,0:T(8,128)S(1)}, f32[512,192]{1,0:T(8,128)S(1)}) custom-call(bf16[24,19456]{1,0:T(8,128)(2,1)S(1)} %copy-done, bf16[24,19456]{1,0:T(8,128)(2,1)S(1)} %collective-permute-done.refs_1_.refs_3_, bf16[24,19456]{1,0:T(8,128)(2,1)} %collective-permute-done.1.refs_2_.refs_4_, bf16[24,19456]{1,0:T(8,128)(2,1)} %copy-done.5, ...), custom_call_target="tpu_custom_call" | custom-call | flops 2617245696 | bytes 40894464 | tf_op jit(solution)/shard_map/pallas_call | solution.py:296
  105.3 0.0 collective-permute-done.16.refs_3_
  105.4 0.0 copy-done.2
  105.4 1.4 %shard_map.59 = (f32[1,128]{1,0:T(1,128)S(1)}, f32[1,128]{1,0:T(1,128)S(1)}) custom-call(f32[512,192]{1,0:T(8,128)S(1)} %get-tuple-element.33.refs_0_, f32[512,192]{1,0:T(8,128)S(1)} %get-tuple-element.34.refs_1_, f32[256,256]{1,0:T(8,128)S(1)} %copy-done.2, f32[256,256]{1,0:T(8,128)} %collective-permute-done.16.refs_3_), custom_call_target="tpu_custom_call" | custom-call | tf_op jit(solution)/shard_map/pallas_call | solution.py:338
  106.8 0.3 collective-permute-start.17
  107.1 3.2 %collective-permute-done.17 = f32[1,128]{1,0:T(1,128)S(1)} collective-permute-done((f32[1,128]{1,0:T(1,128)S(1)}, f32[1,128]{1,0:T(1,128)S(1)}, u32[]{:S(2)}, u32[]{:S(2)}) %collective-permute-start.17) | collective-permute-done | bytes 544 | tf_op jit(solution)/shard_map/ppermute | solution.py:144
  110.3 0.1 fusion
  110.4 0.0 collective-permute-start.18
  110.4 1.1 collective-permute-done.18
  111.5 0.1 fusion.1
  111.6 0.5 collective-permute-start.19
  112.1 3.1 %collective-permute-done.19 = f32[2,1,128]{2,1,0:T(1,128)S(1)} collective-permute-done((f32[2,1,128]{2,1,0:T(1,128)S(1)}, f32[2,1,128]{2,1,0:T(1,128)S(1)}, u32[]{:S(2)}, u32[]{:S(2)}) %collective-permute-start.19) | collective-permute-done | bytes 1056 | tf_op jit(solution)/shard_map/ppermute | solution.py:356
  115.2 0.1 fusion.2
  115.2 1.6 %collective-permute-start.20 = (f32[2,1,128]{2,1,0:T(1,128)S(1)}, f32[2,1,128]{2,1,0:T(1,128)S(1)}, u32[]{:S(2)}, u32[]{:S(2)}) collective-permute-start(f32[2,1,128]{2,1,0:T(1,128)S(1)} %fusion.2), channel_id=1, source_target_pairs={{0,4},{1,5},{2,6},{3,7},{4,0},{5,1},{6,2},{7,3},{8,12},{9,13},{10,... | collective-permute-start | bytes 3080 | tf_op jit(solution)/shard_map/ppermute | solution.py:356
  116.8 2.0 %collective-permute-done.20 = f32[2,1,128]{2,1,0:T(1,128)S(1)} collective-permute-done((f32[2,1,128]{2,1,0:T(1,128)S(1)}, f32[2,1,128]{2,1,0:T(1,128)S(1)}, u32[]{:S(2)}, u32[]{:S(2)}) %collective-permute-start.20) | collective-permute-done | bytes 1056 | tf_op jit(solution)/shard_map/ppermute | solution.py:356
  118.8 2.6 %collective-permute-start.21 = (f32[2,1,128]{2,1,0:T(1,128)S(1)}, f32[2,1,128]{2,1,0:T(1,128)S(1)}, u32[]{:S(2)}, u32[]{:S(2)}) collective-permute-start(f32[2,1,128]{2,1,0:T(1,128)S(1)} %add.16), channel_id=1, source_target_pairs={{0,8},{1,9},{2,10},{3,11},{4,12},{5,13},{6,14},{7,15},{8,0},{9,1},... | collective-permute-start | bytes 3080 | tf_op jit(solution)/shard_map/ppermute | solution.py:356
  121.4 1.9 %collective-permute-done.21 = f32[2,1,128]{2,1,0:T(1,128)S(1)} collective-permute-done((f32[2,1,128]{2,1,0:T(1,128)S(1)}, f32[2,1,128]{2,1,0:T(1,128)S(1)}, u32[]{:S(2)}, u32[]{:S(2)}) %collective-permute-start.21) | collective-permute-done | bytes 1056 | tf_op jit(solution)/shard_map/ppermute | solution.py:356
  123.3 0.6 slice_add_fusion
  (7 shorter events, 0.1 us)
Async XLA Ops:
  0.0 30.5 %collective-permute-start.3 = (bf16[2,128,8192]{2,1,0:T(8,128)(2,1)}, bf16[2,128,8192]{2,1,0:T(8,128)(2,1)}, u32[]{:S(2)}, u32[]{:S(2)}) collective-permute-start(bf16[2,128,8192]{2,1,0:T(8,128)(2,1)} %refs_8_.1), channel_id=1, source_target_pairs={{0,1},{1,0},{2,3},{3,2},{4,5},{5,4},{6,7},{7,6},{8,9},{9,8},{10,11... | collective-permute-start | bytes 12582920 | tf_op jit(solution)/shard_map/ppermute | solution.py:141
  0.5 33.5 %collective-permute-start.7 = (bf16[2,128,8192]{2,1,0:T(8,128)(2,1)}, bf16[2,128,8192]{2,1,0:T(8,128)(2,1)}, u32[]{:S(2)}, u32[]{:S(2)}) collective-permute-start(bf16[2,128,8192]{2,1,0:T(8,128)(2,1)} %refs_0_.5), channel_id=1, source_target_pairs={{0,1},{1,0},{2,3},{3,2},{4,5},{5,4},{6,7},{7,6},{8,9},{9,8},{10,11... | collective-permute-start | bytes 12582920 | tf_op jit(solution)/shard_map/ppermute | solution.py:141
  3.5 27.0 %collective-permute-start.2 = (bf16[128,4096]{1,0:T(8,128)(2,1)}, bf16[128,4096]{1,0:T(8,128)(2,1)}, u32[]{:S(2)}, u32[]{:S(2)}) collective-permute-start(bf16[128,4096]{1,0:T(8,128)(2,1)} %get-tuple-element.24), channel_id=1, source_target_pairs={{0,16},{16,0},{1,17},{17,1},{2,18},{18,2},{3,19},{19,3},{4,20},{20... | collective-permute-start | bytes 3145736 | tf_op jit(solution)/shard_map/ppermute | solution.py:144
  6.5 81.8 %copy-start = (bf16[24,19456]{1,0:T(8,128)(2,1)S(1)}, bf16[24,19456]{1,0:T(8,128)(2,1)}, u32[]{:S(2)}) copy-start(bf16[24,19456]{1,0:T(8,128)(2,1)} %get-tuple-element.22.refs_2_.refs_0_) | copy-start | bytes 2801668
  6.5 22.5 %collective-permute-start = (bf16[24,19456]{1,0:T(8,128)(2,1)}, bf16[24,19456]{1,0:T(8,128)(2,1)S(1)}, u32[]{:S(2)}, u32[]{:S(2)}) collective-permute-start(bf16[24,19456]{1,0:T(8,128)(2,1)} %get-tuple-element.22.refs_2_.refs_0_), channel_id=1, source_target_pairs={{0,4},{4,8},{8,12},{12,14},{14,10},{10,6},{6,2},{2,0},{1,5},{5,9},... | collective-permute-start | bytes 2801672 | tf_op jit(solution)/shard_map/ppermute | solution.py:147
  8.1 22.4 %collective-permute-start.1 = (bf16[24,19456]{1,0:T(8,128)(2,1)}, bf16[24,19456]{1,0:T(8,128)(2,1)}, u32[]{:S(2)}, u32[]{:S(2)}) collective-permute-start(bf16[24,19456]{1,0:T(8,128)(2,1)} %get-tuple-element.22.refs_2_.refs_0_), channel_id=1, source_target_pairs={{4,0},{8,4},{12,8},{14,12},{10,14},{6,10},{2,6},{0,2},{5,1},{9,5},... | collective-permute-start | bytes 2801672 | tf_op jit(solution)/shard_map/ppermute | solution.py:150
  30.5 24.5 %collective-permute-start.6 = (bf16[128,4096]{1,0:T(8,128)(2,1)}, bf16[128,4096]{1,0:T(8,128)(2,1)}, u32[]{:S(2)}, u32[]{:S(2)}) collective-permute-start(bf16[128,4096]{1,0:T(8,128)(2,1)} %get-tuple-element.28), channel_id=1, source_target_pairs={{0,16},{16,0},{1,17},{17,1},{2,18},{18,2},{3,19},{19,3},{4,20},{20... | collective-permute-start | bytes 3145736 | tf_op jit(solution)/shard_map/ppermute | solution.py:144
  31.9 21.5 %collective-permute-start.4 = (bf16[24,19456]{1,0:T(8,128)(2,1)S(1)}, bf16[24,19456]{1,0:T(8,128)(2,1)S(1)}, u32[]{:S(2)}, u32[]{:S(2)}) collective-permute-start(bf16[24,19456]{1,0:T(8,128)(2,1)S(1)} %collective-permute-done.refs_1_.refs_3_), channel_id=1, source_target_pairs={{0,4},{4,8},{8,12},{12,14},{14,10},{10,6},{6,2},{2,0},{1,5},{5,9},... | collective-permute-start | bytes 2801672 | tf_op jit(solution)/shard_map/ppermute | solution.py:147
  33.5 21.4 %collective-permute-start.5 = (bf16[24,19456]{1,0:T(8,128)(2,1)}, bf16[24,19456]{1,0:T(8,128)(2,1)S(1)}, u32[]{:S(2)}, u32[]{:S(2)}) collective-permute-start(bf16[24,19456]{1,0:T(8,128)(2,1)} %collective-permute-done.1.refs_2_.refs_4_), channel_id=1, source_target_pairs={{4,0},{8,4},{12,8},{14,12},{10,14},{6,10},{2,6},{0,2},{5,1},{9,5},... | collective-permute-start | bytes 2801672 | tf_op jit(solution)/shard_map/ppermute | solution.py:150
  53.4 3.7 %copy-start.5 = (bf16[24,19456]{1,0:T(8,128)(2,1)}, bf16[24,19456]{1,0:T(8,128)(2,1)S(1)}, u32[]{:S(2)}) copy-start(bf16[24,19456]{1,0:T(8,128)(2,1)S(1)} %collective-permute-done.4.refs_3_.refs_5_) | copy-start | bytes 2801668
  54.9 32.7 %copy-start.6 = (bf16[24,19456]{1,0:T(8,128)(2,1)}, bf16[24,19456]{1,0:T(8,128)(2,1)S(1)}, u32[]{:S(2)}) copy-start(bf16[24,19456]{1,0:T(8,128)(2,1)S(1)} %collective-permute-done.5.refs_4_.refs_6_) | copy-start | bytes 2801668
  55.0 20.8 %collective-permute-start.8 = (bf16[24,19456]{1,0:T(8,128)(2,1)S(1)}, bf16[24,19456]{1,0:T(8,128)(2,1)S(1)}, u32[]{:S(2)}, u32[]{:S(2)}) collective-permute-start(bf16[24,19456]{1,0:T(8,128)(2,1)S(1)} %collective-permute-done.4.refs_3_.refs_5_), channel_id=1, source_target_pairs={{0,4},{4,8},{8,12},{12,14},{14,10},{10,6},{6,2},{2,0},{1,5},{5,9},... | collective-permute-start | bytes 2801672 | tf_op jit(solution)/shard_map/ppermute | solution.py:147
  56.5 20.8 %collective-permute-start.9 = (bf16[24,19456]{1,0:T(8,128)(2,1)S(1)}, bf16[24,19456]{1,0:T(8,128)(2,1)S(1)}, u32[]{:S(2)}, u32[]{:S(2)}) collective-permute-start(bf16[24,19456]{1,0:T(8,128)(2,1)S(1)} %collective-permute-done.5.refs_4_.refs_6_), channel_id=1, source_target_pairs={{4,0},{8,4},{12,8},{14,12},{10,14},{6,10},{2,6},{0,2},{5,1},{9,5},... | collective-permute-start | bytes 2801672 | tf_op jit(solution)/shard_map/ppermute | solution.py:150
  57.1 28.7 %collective-permute-start.13 = (bf16[128,5120]{1,0:T(8,128)(2,1)}, bf16[128,5120]{1,0:T(8,128)(2,1)}, u32[]{:S(2)}, u32[]{:S(2)}) collective-permute-start(bf16[128,5120]{1,0:T(8,128)(2,1)} %get-tuple-element.31), channel_id=1, source_target_pairs={{0,16},{16,0},{1,17},{17,1},{2,18},{18,2},{3,19},{19,3},{4,20},{20... | collective-permute-start | bytes 3932168 | tf_op jit(solution)/shard_map/ppermute | solution.py:144
  75.9 11.2 %copy-start.3 = (bf16[24,19456]{1,0:T(8,128)(2,1)}, bf16[24,19456]{1,0:T(8,128)(2,1)S(1)}, u32[]{:S(2)}) copy-start(bf16[24,19456]{1,0:T(8,128)(2,1)S(1)} %collective-permute-done.8.refs_5_.refs_7_) | copy-start | bytes 2801668
  75.9 10.1 %collective-permute-start.10 = (bf16[24,9728]{1,0:T(8,128)(2,1)S(1)}, bf16[24,9728]{1,0:T(8,128)(2,1)S(1)}, u32[]{:S(2)}, u32[]{:S(2)}) collective-permute-start(bf16[24,9728]{1,0:T(8,128)(2,1)S(1)} %slice.12), channel_id=1, source_target_pairs={{0,4},{4,8},{8,12},{12,14},{14,10},{10,6},{6,2},{2,0},{1,5},{5,9},... | collective-permute-start | bytes 1400840 | tf_op jit(solution)/shard_map/ppermute | solution.py:147
  77.3 9.7 %copy-start.4 = (bf16[24,19456]{1,0:T(8,128)(2,1)}, bf16[24,19456]{1,0:T(8,128)(2,1)S(1)}, u32[]{:S(2)}) copy-start(bf16[24,19456]{1,0:T(8,128)(2,1)S(1)} %collective-permute-done.9.refs_6_.refs_8_) | copy-start | bytes 2801668
  77.4 9.7 %collective-permute-start.14 = (bf16[24,9728]{1,0:T(8,128)(2,1)S(1)}, bf16[24,9728]{1,0:T(8,128)(2,1)S(1)}, u32[]{:S(2)}, u32[]{:S(2)}) collective-permute-start(bf16[24,9728]{1,0:T(8,128)(2,1)S(1)} %slice.13), channel_id=1, source_target_pairs={{4,0},{8,4},{12,8},{14,12},{10,14},{6,10},{2,6},{0,2},{5,1},{9,5},... | collective-permute-start | bytes 1400840 | tf_op jit(solution)/shard_map/ppermute | solution.py:150
  87.1 8.2 %collective-permute-start.15 = (bf16[128,5120]{1,0:T(8,128)(2,1)}, bf16[128,5120]{1,0:T(8,128)(2,1)}, u32[]{:S(2)}, u32[]{:S(2)}) collective-permute-start(bf16[128,5120]{1,0:T(8,128)(2,1)} %collective-permute-done.13.refs_16_), channel_id=1, source_target_pairs={{0,1},{1,0},{2,3},{3,2},{4,5},{5,4},{6,7},{7,6},{8,9},{9,8},{10,11... | collective-permute-start | bytes 3932168 | tf_op jit(solution)/shard_map/ppermute | solution.py:141
  87.1 8.1 %collective-permute-start.11 = (bf16[128,4096]{1,0:T(8,128)(2,1)}, bf16[128,4096]{1,0:T(8,128)(2,1)}, u32[]{:S(2)}, u32[]{:S(2)}) collective-permute-start(bf16[128,4096]{1,0:T(8,128)(2,1)} %collective-permute-done.2.refs_10_), channel_id=1, source_target_pairs={{0,1},{1,0},{2,3},{3,2},{4,5},{5,4},{6,7},{7,6},{8,9},{9,8},{10,11... | collective-permute-start | bytes 3145736 | tf_op jit(solution)/shard_map/ppermute | solution.py:141
  87.6 7.6 %collective-permute-start.12 = (bf16[128,4096]{1,0:T(8,128)(2,1)}, bf16[128,4096]{1,0:T(8,128)(2,1)}, u32[]{:S(2)}, u32[]{:S(2)}) collective-permute-start(bf16[128,4096]{1,0:T(8,128)(2,1)} %collective-permute-done.6.refs_12_), channel_id=1, source_target_pairs={{0,1},{1,0},{2,3},{3,2},{4,5},{5,4},{6,7},{7,6},{8,9},{9,8},{10,11... | collective-permute-start | bytes 3145736 | tf_op jit(solution)/shard_map/ppermute | solution.py:141
  92.8 0.7 copy-start.1
  93.5 11.8 %collective-permute-start.16 = (f32[256,256]{1,0:T(8,128)}, f32[256,256]{1,0:T(8,128)}, u32[]{:S(2)}, u32[]{:S(2)}) collective-permute-start(f32[256,256]{1,0:T(8,128)} %get-tuple-element.36), channel_id=1, source_target_pairs={{0,16},{16,0},{1,17},{17,1},{2,18},{18,2},{3,19},{19,3},{4,20},{20... | collective-permute-start | bytes 786440 | tf_op jit(solution)/shard_map/ppermute | solution.py:144
  95.2 10.1 %copy-start.2 = (f32[256,256]{1,0:T(8,128)S(1)}, f32[256,256]{1,0:T(8,128)}, u32[]{:S(2)}) copy-start(f32[256,256]{1,0:T(8,128)} %copy-done.1) | copy-start | bytes 786436
  106.8 3.5 %collective-permute-start.17 = (f32[1,128]{1,0:T(1,128)S(1)}, f32[1,128]{1,0:T(1,128)S(1)}, u32[]{:S(2)}, u32[]{:S(2)}) collective-permute-start(f32[1,128]{1,0:T(1,128)S(1)} %get-tuple-element.38), channel_id=1, source_target_pairs={{0,16},{16,0},{1,17},{17,1},{2,18},{18,2},{3,19},{19,3},{4,20},{20... | collective-permute-start | bytes 1544 | tf_op jit(solution)/shard_map/ppermute | solution.py:144
  110.4 1.1 collective-permute-start.18
  111.6 3.6 %collective-permute-start.19 = (f32[2,1,128]{2,1,0:T(1,128)S(1)}, f32[2,1,128]{2,1,0:T(1,128)S(1)}, u32[]{:S(2)}, u32[]{:S(2)}) collective-permute-start(f32[2,1,128]{2,1,0:T(1,128)S(1)} %fusion.1), channel_id=1, source_target_pairs={{0,2},{1,3},{2,0},{3,1},{4,6},{5,7},{6,4},{7,5},{8,10},{9,11},{10,... | collective-permute-start | bytes 3080 | tf_op jit(solution)/shard_map/ppermute | solution.py:356
  115.2 3.6 %collective-permute-start.20 = (f32[2,1,128]{2,1,0:T(1,128)S(1)}, f32[2,1,128]{2,1,0:T(1,128)S(1)}, u32[]{:S(2)}, u32[]{:S(2)}) collective-permute-start(f32[2,1,128]{2,1,0:T(1,128)S(1)} %fusion.2), channel_id=1, source_target_pairs={{0,4},{1,5},{2,6},{3,7},{4,0},{5,1},{6,2},{7,3},{8,12},{9,13},{10,... | collective-permute-start | bytes 3080 | tf_op jit(solution)/shard_map/ppermute | solution.py:356
  118.8 4.5 %collective-permute-start.21 = (f32[2,1,128]{2,1,0:T(1,128)S(1)}, f32[2,1,128]{2,1,0:T(1,128)S(1)}, u32[]{:S(2)}, u32[]{:S(2)}) collective-permute-start(f32[2,1,128]{2,1,0:T(1,128)S(1)} %add.16), channel_id=1, source_target_pairs={{0,8},{1,9},{2,10},{3,11},{4,12},{5,13},{6,14},{7,15},{8,0},{9,1},... | collective-permute-start | bytes 3080 | tf_op jit(solution)/shard_map/ppermute | solution.py:356

commit v4 on v3

--- a/solution.py
+++ b/solution.py
@@ -172,7 +172,7 @@
                 ranges.append((in_source, layer, max(start - width, 0), stop - width))
             return ranges
 
-        edges = [0, width // 2, width, packed]
+        edges = [0, width * 3 // 8, width * 7 // 8, packed]
 
         def away_part(k):
             return packing(1, 0, "other", edges[k], edges[k + 1])
@@ -193,18 +193,14 @@
         ahead = back = piece
         away, away_sib = [], []
         for step in range(full):
-            given = [ahead, back]
+            ahead, back = ahead_of(ahead), back_of(back)
             if step < 3:
-                given.append(chunks[step])
-            if step == 1:
-                given = after(given, away[0], *chunks[1:], backs_sib)
-            if step == 2:
-                given = after(given, away[1], acts_sib)
-                away_sib = [swap_core(x) for x in away]
-            ahead, back = ahead_of(given[0]), back_of(given[1])
-            if step < 3:
-                away.append(swap_grp(given[2]))
+                chunk = chunks[step]
+                if step:
+                    chunk = after((chunk,), away[-1])[0]
+                away.append(swap_grp(chunk))
             got += [ahead, back]
+        away_sib = [swap_core(x) for x in away[:2]]
         total = packed + 2 * beyond
         middle = total // 2
         chip_tokens = 2 * tokens_here

time: 124 us -> 119 us (0.960)
  waiting for transfers between devices: 77.7 us -> 70.2 us
  local copies, waits for them, and re-layouts: 0.8 us -> 2.8 us
  starting transfers between devices: 21.9 us -> 23.4 us
  Pallas kernels: 21.9 us -> 20.6 us
    ppermute x4, waiting for transfers between devices: 54.6 us -> 1.87 us  [ahead_of(): return lax.ppermute(x, 'blk', forward)]
    ppermute x4, waiting for transfers between devices: 4 us -> 27.4 us  [back_of(): return lax.ppermute(x, 'blk', backward)]
    ppermute x5, waiting for transfers between devices: 11 us -> 33.9 us  [swap_grp(): return lax.ppermute(x, 'grp', [(0, 1), (1, 0)])]
    ppermute x4, starting transfers between devices: 2.15 us -> 6.02 us  [back_of(): return lax.ppermute(x, 'blk', backward)]
    ppermute x4, starting transfers between devices: 6.06 us -> 2.78 us  [ahead_of(): return lax.ppermute(x, 'blk', forward)]
    unnamed x14 -> x16, local copies, waits for them, and re-layouts: 0.74 us -> 2.74 us
  transfers between devices with their start and end apart: 22 -> 22, of which waited for: 14 -> 12; matrix products, arithmetic and copies ran while one was open for 0% -> 0% of each run, Pallas kernels for 17% -> 15%
where the time goes in v4:
time: 119 us
  waiting for transfers between devices  70.2 us (59%)
  starting transfers between devices  23.4 us (20%)
  Pallas kernels  20.6 us (17%)
  local copies, waits for them, and re-layouts  2.8 us (2%)
    ppermute x5, waiting for transfers between devices, swap_grp(): return lax.ppermute(x, 'grp', [(0, 1), (1, 0)])  33.9 us
    ppermute x4, waiting for transfers between devices, back_of(): return lax.ppermute(x, 'blk', backward)  27.4 us
    pallas_call x1, Pallas kernels, shards(): pl.pallas_call(main_kernel, out_shape=[proj] * 2, in_specs=[ANYWHERE] * c...  9.73 us
    ppermute x5, starting transfers between devices, swap_grp(): return lax.ppermute(x, 'grp', [(0, 1), (1, 0)])  8.29 us
    ppermute x4, waiting for transfers between devices, shards(): lax.ppermute(value, 'blk', [(i, i ^ bit) for i in range(blk)])  7.07 us
    ppermute x4, starting transfers between devices, back_of(): return lax.ppermute(x, 'blk', backward)  6.02 us
    pallas_call x2, Pallas kernels, move(): pl.pallas_call(kernel, out_shape=shapes, in_specs=[ANYWHERE] * (count + l...  5.93 us
    ppermute x4, starting transfers between devices, shards(): lax.ppermute(value, 'blk', [(i, i ^ bit) for i in range(blk)])  5.68 us
  transfers between devices with their start and end apart: 22, of which 12 were waited for; matrix products, arithmetic and copies ran while one was open for 0% of the time, Pallas kernels for 15%

profile of v4, /device:TPU:0, one launch (start us, length us, event | category | flops | bytes accessed | tf_op | source)
XLA Modules:
  0.0 118.5 jit_solution(11939234068256721496)
XLA Ops:
  0.0 2.7 %shard_map.55 = (bf16[24,19456]{1,0:T(8,128)(2,1)}, bf16[128,3072]{1,0:T(8,128)(2,1)}) custom-call(bf16[2,128,8192]{2,1,0:T(8,128)(2,1)} %refs_0_.5, bf16[2,128,8192]{2,1,0:T(8,128)(2,1)} %refs_8_.1, bf16[2,24,8192]{2,1,0:T(8,128)(2,1)} %refs_2_.1, bf16[2,24,8192]{2,1,0:T(8,128)(2,1)} %refs_3_.1), custom_call_target="tpu_custom_call" | custom-call | bytes 6881280 | tf_op jit(solution)/shard_map/pallas_call | solution.py:61
  2.7 3.0 %collective-permute-start.8 = (bf16[128,3072]{1,0:T(8,128)(2,1)}, bf16[128,3072]{1,0:T(8,128)(2,1)}, u32[]{:S(2)}, u32[]{:S(2)}) collective-permute-start(bf16[128,3072]{1,0:T(8,128)(2,1)} %get-tuple-element.19), channel_id=1, source_target_pairs={{0,16},{16,0},{1,17},{17,1},{2,18},{18,2},{3,19},{19,3},{4,20},{20... | collective-permute-start | bytes 2359304 | tf_op jit(solution)/shard_map/ppermute | solution.py:144
  5.8 0.0 copy-start
  5.8 1.5 %collective-permute-start.1 = (bf16[24,19456]{1,0:T(8,128)(2,1)}, bf16[24,19456]{1,0:T(8,128)(2,1)S(1)}, u32[]{:S(2)}, u32[]{:S(2)}) collective-permute-start(bf16[24,19456]{1,0:T(8,128)(2,1)} %get-tuple-element.18.refs_2_.refs_0_), channel_id=1, source_target_pairs={{4,0},{8,4},{12,8},{14,12},{10,14},{6,10},{2,6},{0,2},{5,1},{9,5},... | collective-permute-start | bytes 2801672 | tf_op jit(solution)/shard_map/ppermute | solution.py:150
  7.3 0.5 collective-permute-start
  7.8 0.0 collective-permute-start.15
  7.8 3.2 %shard_map.56 = (bf16[128,4096]{1,0:T(8,128)(2,1)}, bf16[128,6144]{1,0:T(8,128)(2,1)}) custom-call(bf16[2,128,8192]{2,1,0:T(8,128)(2,1)} %refs_0_.5, bf16[2,128,8192]{2,1,0:T(8,128)(2,1)} %refs_8_.1, bf16[24,19456]{1,0:T(8,128)(2,1)} %get-tuple-element.18.refs_2_.refs_0_), custom_call_target="tpu_custom_call" | custom-call | bytes 10485760 | tf_op jit(solution)/shard_map/pallas_call | solution.py:61
  11.0 12.6 %collective-permute-done.8.refs_10_ = bf16[128,3072]{1,0:T(8,128)(2,1)} collective-permute-done((bf16[128,3072]{1,0:T(8,128)(2,1)}, bf16[128,3072]{1,0:T(8,128)(2,1)}, u32[]{:S(2)}, u32[]{:S(2)}) %collective-permute-start.8) | collective-permute-done | bytes 786464 | tf_op jit(solution)/shard_map/ppermute | solution.py:144
  23.6 1.7 %collective-permute-start.10 = (bf16[128,4096]{1,0:T(8,128)(2,1)}, bf16[128,4096]{1,0:T(8,128)(2,1)}, u32[]{:S(2)}, u32[]{:S(2)}) collective-permute-start(bf16[128,4096]{1,0:T(8,128)(2,1)} %get-tuple-element.21), channel_id=1, source_target_pairs={{0,16},{16,0},{1,17},{17,1},{2,18},{18,2},{3,19},{19,3},{4,20},{20... | collective-permute-start | bytes 3145736 | tf_op jit(solution)/shard_map/ppermute | solution.py:144
  25.4 0.0 collective-permute-start.7
  25.4 2.8 %collective-permute-done.1.refs_2_.refs_4_ = bf16[24,19456]{1,0:T(8,128)(2,1)S(1)} collective-permute-done((bf16[24,19456]{1,0:T(8,128)(2,1)}, bf16[24,19456]{1,0:T(8,128)(2,1)S(1)}, u32[]{:S(2)}, u32[]{:S(2)}) %collective-permute-start.1) | collective-permute-done | bytes 933920 | tf_op jit(solution)/shard_map/ppermute | solution.py:150
  28.1 1.5 %collective-permute-start.3 = (bf16[24,19456]{1,0:T(8,128)(2,1)S(1)}, bf16[24,19456]{1,0:T(8,128)(2,1)S(1)}, u32[]{:S(2)}, u32[]{:S(2)}) collective-permute-start(bf16[24,19456]{1,0:T(8,128)(2,1)S(1)} %collective-permute-done.1.refs_2_.refs_4_), channel_id=1, source_target_pairs={{4,0},{8,4},{12,8},{14,12},{10,14},{6,10},{2,6},{0,2},{5,1},{9,5},... | collective-permute-start | bytes 2801672 | tf_op jit(solution)/shard_map/ppermute | solution.py:150
  29.6 0.0 collective-permute-done.refs_1_.refs_3_
  29.6 0.5 collective-permute-start.2
  30.2 18.1 %collective-permute-done.10.refs_12_ = bf16[128,4096]{1,0:T(8,128)(2,1)} collective-permute-done((bf16[128,4096]{1,0:T(8,128)(2,1)}, bf16[128,4096]{1,0:T(8,128)(2,1)}, u32[]{:S(2)}, u32[]{:S(2)}) %collective-permute-start.10) | collective-permute-done | bytes 1048608 | tf_op jit(solution)/shard_map/ppermute | solution.py:144
  48.3 1.4 %collective-permute-start.12 = (bf16[128,6144]{1,0:T(8,128)(2,1)}, bf16[128,6144]{1,0:T(8,128)(2,1)}, u32[]{:S(2)}, u32[]{:S(2)}) collective-permute-start(bf16[128,6144]{1,0:T(8,128)(2,1)} %get-tuple-element.23), channel_id=1, source_target_pairs={{0,16},{16,0},{1,17},{17,1},{2,18},{18,2},{3,19},{19,3},{4,20},{20... | collective-permute-start | bytes 4718600 | tf_op jit(solution)/shard_map/ppermute | solution.py:144
  49.7 0.0 collective-permute-done.3.refs_4_.refs_6_
  49.7 1.5 %collective-permute-start.5 = (bf16[24,19456]{1,0:T(8,128)(2,1)S(1)}, bf16[24,19456]{1,0:T(8,128)(2,1)S(1)}, u32[]{:S(2)}, u32[]{:S(2)}) collective-permute-start(bf16[24,19456]{1,0:T(8,128)(2,1)S(1)} %collective-permute-done.3.refs_4_.refs_6_), channel_id=1, source_target_pairs={{4,0},{8,4},{12,8},{14,12},{10,14},{6,10},{2,6},{0,2},{5,1},{9,5},... | collective-permute-start | bytes 2801672 | tf_op jit(solution)/shard_map/ppermute | solution.py:150
  51.2 0.0 collective-permute-done.2.refs_3_.refs_5_
  51.2 0.0 copy-done.6
  51.2 1.0 collective-permute-start.4
  52.2 18.1 %collective-permute-done.5.refs_6_.refs_8_ = bf16[24,19456]{1,0:T(8,128)(2,1)S(1)} collective-permute-done((bf16[24,19456]{1,0:T(8,128)(2,1)S(1)}, bf16[24,19456]{1,0:T(8,128)(2,1)S(1)}, u32[]{:S(2)}, u32[]{:S(2)}) %collective-permute-start.5) | collective-permute-done | bytes 933920 | tf_op jit(solution)/shard_map/ppermute | solution.py:150
  70.4 0.0 copy-start.4
  70.4 1.5 %collective-permute-start.13 = (bf16[24,9728]{1,0:T(8,128)(2,1)S(1)}, bf16[24,9728]{1,0:T(8,128)(2,1)S(1)}, u32[]{:S(2)}, u32[]{:S(2)}) collective-permute-start(bf16[24,9728]{1,0:T(8,128)(2,1)S(1)} %slice.13), channel_id=1, source_target_pairs={{4,0},{8,4},{12,8},{14,12},{10,14},{6,10},{2,6},{0,2},{5,1},{9,5},... | collective-permute-start | bytes 1400840 | tf_op jit(solution)/shard_map/ppermute | solution.py:150
  72.0 0.0 collective-permute-done.4.refs_5_.refs_7_
  72.0 0.9 copy-done.5
  72.9 0.7 collective-permute-start.6
  73.6 6.5 %collective-permute-done.13.refs_18_.refs_9_ = bf16[24,9728]{1,0:T(8,128)(2,1)S(1)} collective-permute-done((bf16[24,9728]{1,0:T(8,128)(2,1)S(1)}, bf16[24,9728]{1,0:T(8,128)(2,1)S(1)}, u32[]{:S(2)}, u32[]{:S(2)}) %collective-permute-start.13) | collective-permute-done | bytes 466976 | tf_op jit(solution)/shard_map/ppermute | solution.py:150
  80.1 1.9 %collective-permute-done.6.refs_7_ = bf16[24,9728]{1,0:T(8,128)(2,1)S(1)} collective-permute-done((bf16[24,9728]{1,0:T(8,128)(2,1)S(1)}, bf16[24,9728]{1,0:T(8,128)(2,1)S(1)}, u32[]{:S(2)}, u32[]{:S(2)}) %collective-permute-start.6) | collective-permute-done | bytes 466976 | tf_op jit(solution)/shard_map/ppermute | solution.py:147
  82.0 0.8 copy-done.2
  82.7 0.5 collective-permute-done.12.refs_14_
  83.3 0.0 collective-permute-start.14
  83.3 0.0 copy-done.4
  83.3 0.5 collective-permute-start.11
  83.8 0.0 copy-done.7
  83.8 0.1 collective-permute-start.9
  84.5 0.0 collective-permute-done.15.refs_17_.refs_1_
  84.5 0.0 copy-done
  84.5 4.5 %shard_map.58 = (f32[256,256]{1,0:T(8,128)S(1)}, f32[256,256]{1,0:T(8,128)}) custom-call(bf16[2,128,8192]{2,1,0:T(8,128)(2,1)} %refs_0_.5, bf16[2,128,8192]{2,1,0:T(8,128)(2,1)} %collective-permute-done.15.refs_17_.refs_1_, bf16[24,19456]{1,0:T(8,128)(2,1)S(1)} %copy-done, bf16[24,19456]{1,0:T(8,128)(2,1)} %collective-permute-done.refs_1_.refs_3_, ...), custom_call_target="tpu_custom_call" | custom-call | flops 603979776 | bytes 9437184 | tf_op jit(solution)/shard_map/pallas_call | solution.py:257
  89.0 0.0 copy-done.1
  89.0 1.2 collective-permute-start.16
  90.2 0.0 collective-permute-done.9.refs_11_
  90.2 0.0 collective-permute-done.11.refs_13_
  90.2 0.0 collective-permute-done.7.refs_9_
  90.2 0.0 collective-permute-done.14.refs_15_
  90.2 0.0 copy-start.3
  90.2 1.0 copy-done.3
  91.2 9.7 %shard_map.57 = (f32[512,192]{1,0:T(8,128)S(1)}, f32[512,192]{1,0:T(8,128)S(1)}) custom-call(bf16[24,19456]{1,0:T(8,128)(2,1)} %get-tuple-element.18.refs_2_.refs_0_, bf16[24,19456]{1,0:T(8,128)(2,1)} %collective-permute-done.refs_1_.refs_3_, bf16[24,19456]{1,0:T(8,128)(2,1)} %copy-done.1, bf16[24,19456]{1,0:T(8,128)(2,1)} %copy-done.7, ...), custom_call_target="tpu_custom_call" | custom-call | flops 2617245696 | bytes 40894464 | tf_op jit(solution)/shard_map/pallas_call | solution.py:292
  101.0 0.0 collective-permute-done.16.refs_3_
  101.0 0.5 shard_map.59
  101.4 0.9 collective-permute-start.17
  102.4 2.6 %collective-permute-done.17 = f32[1,128]{1,0:T(1,128)S(1)} collective-permute-done((f32[1,128]{1,0:T(1,128)S(1)}, f32[1,128]{1,0:T(1,128)S(1)}, u32[]{:S(2)}, u32[]{:S(2)}) %collective-permute-start.17) | collective-permute-done | bytes 544 | tf_op jit(solution)/shard_map/ppermute | solution.py:144
  105.0 0.1 fusion
  105.1 0.0 collective-permute-start.18
  105.1 1.1 collective-permute-done.18
  106.2 0.1 fusion.1
  106.3 1.5 %collective-permute-start.19 = (f32[2,1,128]{2,1,0:T(1,128)S(1)}, f32[2,1,128]{2,1,0:T(1,128)S(1)}, u32[]{:S(2)}, u32[]{:S(2)}) collective-permute-start(f32[2,1,128]{2,1,0:T(1,128)S(1)} %fusion.1), channel_id=1, source_target_pairs={{0,2},{1,3},{2,0},{3,1},{4,6},{5,7},{6,4},{7,5},{8,10},{9,11},{10,... | collective-permute-start | bytes 3080 | tf_op jit(solution)/shard_map/ppermute | solution.py:352
  107.8 2.1 %collective-permute-done.19 = f32[2,1,128]{2,1,0:T(1,128)S(1)} collective-permute-done((f32[2,1,128]{2,1,0:T(1,128)S(1)}, f32[2,1,128]{2,1,0:T(1,128)S(1)}, u32[]{:S(2)}, u32[]{:S(2)}) %collective-permute-start.19) | collective-permute-done | bytes 1056 | tf_op jit(solution)/shard_map/ppermute | solution.py:352
  109.8 0.1 fusion.2
  109.9 1.6 %collective-permute-start.20 = (f32[2,1,128]{2,1,0:T(1,128)S(1)}, f32[2,1,128]{2,1,0:T(1,128)S(1)}, u32[]{:S(2)}, u32[]{:S(2)}) collective-permute-start(f32[2,1,128]{2,1,0:T(1,128)S(1)} %fusion.2), channel_id=1, source_target_pairs={{0,4},{1,5},{2,6},{3,7},{4,0},{5,1},{6,2},{7,3},{8,12},{9,13},{10,... | collective-permute-start | bytes 3080 | tf_op jit(solution)/shard_map/ppermute | solution.py:352
  111.5 2.0 %collective-permute-done.20 = f32[2,1,128]{2,1,0:T(1,128)S(1)} collective-permute-done((f32[2,1,128]{2,1,0:T(1,128)S(1)}, f32[2,1,128]{2,1,0:T(1,128)S(1)}, u32[]{:S(2)}, u32[]{:S(2)}) %collective-permute-start.20) | collective-permute-done | bytes 1056 | tf_op jit(solution)/shard_map/ppermute | solution.py:352
  113.5 2.6 %collective-permute-start.21 = (f32[2,1,128]{2,1,0:T(1,128)S(1)}, f32[2,1,128]{2,1,0:T(1,128)S(1)}, u32[]{:S(2)}, u32[]{:S(2)}) collective-permute-start(f32[2,1,128]{2,1,0:T(1,128)S(1)} %add.16), channel_id=1, source_target_pairs={{0,8},{1,9},{2,10},{3,11},{4,12},{5,13},{6,14},{7,15},{8,0},{9,1},... | collective-permute-start | bytes 3080 | tf_op jit(solution)/shard_map/ppermute | solution.py:352
  116.1 1.9 %collective-permute-done.21 = f32[2,1,128]{2,1,0:T(1,128)S(1)} collective-permute-done((f32[2,1,128]{2,1,0:T(1,128)S(1)}, f32[2,1,128]{2,1,0:T(1,128)S(1)}, u32[]{:S(2)}, u32[]{:S(2)}) %collective-permute-start.21) | collective-permute-done | bytes 1056 | tf_op jit(solution)/shard_map/ppermute | solution.py:352
  118.0 0.6 slice_add_fusion
  (9 shorter events, 0.1 us)
Async XLA Ops:
  2.7 20.9 %collective-permute-start.8 = (bf16[128,3072]{1,0:T(8,128)(2,1)}, bf16[128,3072]{1,0:T(8,128)(2,1)}, u32[]{:S(2)}, u32[]{:S(2)}) collective-permute-start(bf16[128,3072]{1,0:T(8,128)(2,1)} %get-tuple-element.19), channel_id=1, source_target_pairs={{0,16},{16,0},{1,17},{17,1},{2,18},{18,2},{3,19},{19,3},{4,20},{20... | collective-permute-start | bytes 2359304 | tf_op jit(solution)/shard_map/ppermute | solution.py:144
  5.8 78.7 %copy-start = (bf16[24,19456]{1,0:T(8,128)(2,1)S(1)}, bf16[24,19456]{1,0:T(8,128)(2,1)}, u32[]{:S(2)}) copy-start(bf16[24,19456]{1,0:T(8,128)(2,1)} %get-tuple-element.18.refs_2_.refs_0_) | copy-start | bytes 2801668
  5.8 22.4 %collective-permute-start.1 = (bf16[24,19456]{1,0:T(8,128)(2,1)}, bf16[24,19456]{1,0:T(8,128)(2,1)S(1)}, u32[]{:S(2)}, u32[]{:S(2)}) collective-permute-start(bf16[24,19456]{1,0:T(8,128)(2,1)} %get-tuple-element.18.refs_2_.refs_0_), channel_id=1, source_target_pairs={{4,0},{8,4},{12,8},{14,12},{10,14},{6,10},{2,6},{0,2},{5,1},{9,5},... | collective-permute-start | bytes 2801672 | tf_op jit(solution)/shard_map/ppermute | solution.py:150
  7.3 22.4 %collective-permute-start = (bf16[24,19456]{1,0:T(8,128)(2,1)}, bf16[24,19456]{1,0:T(8,128)(2,1)}, u32[]{:S(2)}, u32[]{:S(2)}) collective-permute-start(bf16[24,19456]{1,0:T(8,128)(2,1)} %get-tuple-element.18.refs_2_.refs_0_), channel_id=1, source_target_pairs={{0,4},{4,8},{8,12},{12,14},{14,10},{10,6},{6,2},{2,0},{1,5},{5,9},... | collective-permute-start | bytes 2801672 | tf_op jit(solution)/shard_map/ppermute | solution.py:147
  7.8 76.7 %collective-permute-start.15 = (bf16[2,128,8192]{2,1,0:T(8,128)(2,1)}, bf16[2,128,8192]{2,1,0:T(8,128)(2,1)}, u32[]{:S(2)}, u32[]{:S(2)}) collective-permute-start(bf16[2,128,8192]{2,1,0:T(8,128)(2,1)} %refs_0_.5), channel_id=1, source_target_pairs={{0,1},{1,0},{2,3},{3,2},{4,5},{5,4},{6,7},{7,6},{8,9},{9,8},{10,11... | collective-permute-start | bytes 12582920 | tf_op jit(solution)/shard_map/ppermute | solution.py:141
  23.6 24.7 %collective-permute-start.10 = (bf16[128,4096]{1,0:T(8,128)(2,1)}, bf16[128,4096]{1,0:T(8,128)(2,1)}, u32[]{:S(2)}, u32[]{:S(2)}) collective-permute-start(bf16[128,4096]{1,0:T(8,128)(2,1)} %get-tuple-element.21), channel_id=1, source_target_pairs={{0,16},{16,0},{1,17},{17,1},{2,18},{18,2},{3,19},{19,3},{4,20},{20... | collective-permute-start | bytes 3145736 | tf_op jit(solution)/shard_map/ppermute | solution.py:144
  25.4 64.8 %collective-permute-start.7 = (bf16[2,128,8192]{2,1,0:T(8,128)(2,1)}, bf16[2,128,8192]{2,1,0:T(8,128)(2,1)}, u32[]{:S(2)}, u32[]{:S(2)}) collective-permute-start(bf16[2,128,8192]{2,1,0:T(8,128)(2,1)} %refs_8_.1), channel_id=1, source_target_pairs={{0,1},{1,0},{2,3},{3,2},{4,5},{5,4},{6,7},{7,6},{8,9},{9,8},{10,11... | collective-permute-start | bytes 12582920 | tf_op jit(solution)/shard_map/ppermute | solution.py:141
  28.1 60.8 %copy-start.1 = (bf16[24,19456]{1,0:T(8,128)(2,1)}, bf16[24,19456]{1,0:T(8,128)(2,1)S(1)}, u32[]{:S(2)}) copy-start(bf16[24,19456]{1,0:T(8,128)(2,1)S(1)} %collective-permute-done.1.refs_2_.refs_4_) | copy-start | bytes 2801668
  28.1 21.6 %collective-permute-start.3 = (bf16[24,19456]{1,0:T(8,128)(2,1)S(1)}, bf16[24,19456]{1,0:T(8,128)(2,1)S(1)}, u32[]{:S(2)}, u32[]{:S(2)}) collective-permute-start(bf16[24,19456]{1,0:T(8,128)(2,1)S(1)} %collective-permute-done.1.refs_2_.refs_4_), channel_id=1, source_target_pairs={{4,0},{8,4},{12,8},{14,12},{10,14},{6,10},{2,6},{0,2},{5,1},{9,5},... | collective-permute-start | bytes 2801672 | tf_op jit(solution)/shard_map/ppermute | solution.py:150
  29.6 21.6 %collective-permute-start.2 = (bf16[24,19456]{1,0:T(8,128)(2,1)}, bf16[24,19456]{1,0:T(8,128)(2,1)S(1)}, u32[]{:S(2)}, u32[]{:S(2)}) collective-permute-start(bf16[24,19456]{1,0:T(8,128)(2,1)} %collective-permute-done.refs_1_.refs_3_), channel_id=1, source_target_pairs={{0,4},{4,8},{8,12},{12,14},{14,10},{10,6},{6,2},{2,0},{1,5},{5,9},... | collective-permute-start | bytes 2801672 | tf_op jit(solution)/shard_map/ppermute | solution.py:147
  48.3 35.0 %collective-permute-start.12 = (bf16[128,6144]{1,0:T(8,128)(2,1)}, bf16[128,6144]{1,0:T(8,128)(2,1)}, u32[]{:S(2)}, u32[]{:S(2)}) collective-permute-start(bf16[128,6144]{1,0:T(8,128)(2,1)} %get-tuple-element.23), channel_id=1, source_target_pairs={{0,16},{16,0},{1,17},{17,1},{2,18},{18,2},{3,19},{19,3},{4,20},{20... | collective-permute-start | bytes 4718600 | tf_op jit(solution)/shard_map/ppermute | solution.py:144
  49.7 1.5 %copy-start.6 = (bf16[24,19456]{1,0:T(8,128)(2,1)}, bf16[24,19456]{1,0:T(8,128)(2,1)S(1)}, u32[]{:S(2)}) copy-start(bf16[24,19456]{1,0:T(8,128)(2,1)S(1)} %collective-permute-done.3.refs_4_.refs_6_) | copy-start | bytes 2801668
  49.7 20.7 %collective-permute-start.5 = (bf16[24,19456]{1,0:T(8,128)(2,1)S(1)}, bf16[24,19456]{1,0:T(8,128)(2,1)S(1)}, u32[]{:S(2)}, u32[]{:S(2)}) collective-permute-start(bf16[24,19456]{1,0:T(8,128)(2,1)S(1)} %collective-permute-done.3.refs_4_.refs_6_), channel_id=1, source_target_pairs={{4,0},{8,4},{12,8},{14,12},{10,14},{6,10},{2,6},{0,2},{5,1},{9,5},... | collective-permute-start | bytes 2801672 | tf_op jit(solution)/shard_map/ppermute | solution.py:150
  51.2 32.6 %copy-start.7 = (bf16[24,19456]{1,0:T(8,128)(2,1)}, bf16[24,19456]{1,0:T(8,128)(2,1)S(1)}, u32[]{:S(2)}) copy-start(bf16[24,19456]{1,0:T(8,128)(2,1)S(1)} %collective-permute-done.2.refs_3_.refs_5_) | copy-start | bytes 2801668
  51.2 20.8 %collective-permute-start.4 = (bf16[24,19456]{1,0:T(8,128)(2,1)S(1)}, bf16[24,19456]{1,0:T(8,128)(2,1)S(1)}, u32[]{:S(2)}, u32[]{:S(2)}) collective-permute-start(bf16[24,19456]{1,0:T(8,128)(2,1)S(1)} %collective-permute-done.2.refs_3_.refs_5_), channel_id=1, source_target_pairs={{0,4},{4,8},{8,12},{12,14},{14,10},{10,6},{6,2},{2,0},{1,5},{5,9},... | collective-permute-start | bytes 2801672 | tf_op jit(solution)/shard_map/ppermute | solution.py:147
  70.4 12.9 %copy-start.4 = (bf16[24,19456]{1,0:T(8,128)(2,1)}, bf16[24,19456]{1,0:T(8,128)(2,1)S(1)}, u32[]{:S(2)}) copy-start(bf16[24,19456]{1,0:T(8,128)(2,1)S(1)} %collective-permute-done.5.refs_6_.refs_8_) | copy-start | bytes 2801668
  70.4 9.7 %collective-permute-start.13 = (bf16[24,9728]{1,0:T(8,128)(2,1)S(1)}, bf16[24,9728]{1,0:T(8,128)(2,1)S(1)}, u32[]{:S(2)}, u32[]{:S(2)}) collective-permute-start(bf16[24,9728]{1,0:T(8,128)(2,1)S(1)} %slice.13), channel_id=1, source_target_pairs={{4,0},{8,4},{12,8},{14,12},{10,14},{6,10},{2,6},{0,2},{5,1},{9,5},... | collective-permute-start | bytes 1400840 | tf_op jit(solution)/shard_map/ppermute | solution.py:150
  72.0 0.9 copy-start.5
  72.9 9.0 %collective-permute-start.6 = (bf16[24,9728]{1,0:T(8,128)(2,1)S(1)}, bf16[24,9728]{1,0:T(8,128)(2,1)S(1)}, u32[]{:S(2)}, u32[]{:S(2)}) collective-permute-start(bf16[24,9728]{1,0:T(8,128)(2,1)S(1)} %slice.12), channel_id=1, source_target_pairs={{0,4},{4,8},{8,12},{12,14},{14,10},{10,6},{6,2},{2,0},{1,5},{5,9},... | collective-permute-start | bytes 1400840 | tf_op jit(solution)/shard_map/ppermute | solution.py:147
  82.0 0.8 copy-start.2
  83.3 6.9 %collective-permute-start.14 = (bf16[128,6144]{1,0:T(8,128)(2,1)}, bf16[128,6144]{1,0:T(8,128)(2,1)}, u32[]{:S(2)}, u32[]{:S(2)}) collective-permute-start(bf16[128,6144]{1,0:T(8,128)(2,1)} %collective-permute-done.12.refs_14_), channel_id=1, source_target_pairs={{0,1},{1,0},{2,3},{3,2},{4,5},{5,4},{6,7},{7,6},{8,9},{9,8},{10,11... | collective-permute-start | bytes 4718600 | tf_op jit(solution)/shard_map/ppermute | solution.py:141
  83.3 6.9 %collective-permute-start.11 = (bf16[128,4096]{1,0:T(8,128)(2,1)}, bf16[128,4096]{1,0:T(8,128)(2,1)}, u32[]{:S(2)}, u32[]{:S(2)}) collective-permute-start(bf16[128,4096]{1,0:T(8,128)(2,1)} %collective-permute-done.10.refs_12_), channel_id=1, source_target_pairs={{0,1},{1,0},{2,3},{3,2},{4,5},{5,4},{6,7},{7,6},{8,9},{9,8},{10,11... | collective-permute-start | bytes 3145736 | tf_op jit(solution)/shard_map/ppermute | solution.py:141
  83.8 6.4 %collective-permute-start.9 = (bf16[128,3072]{1,0:T(8,128)(2,1)}, bf16[128,3072]{1,0:T(8,128)(2,1)S(1)}, u32[]{:S(2)}, u32[]{:S(2)}) collective-permute-start(bf16[128,3072]{1,0:T(8,128)(2,1)} %collective-permute-done.8.refs_10_), channel_id=1, source_target_pairs={{0,1},{1,0},{2,3},{3,2},{4,5},{5,4},{6,7},{7,6},{8,9},{9,8},{10,11... | collective-permute-start | bytes 2359304 | tf_op jit(solution)/shard_map/ppermute | solution.py:141
  89.0 12.0 %collective-permute-start.16 = (f32[256,256]{1,0:T(8,128)}, f32[256,256]{1,0:T(8,128)S(1)}, u32[]{:S(2)}, u32[]{:S(2)}) collective-permute-start(f32[256,256]{1,0:T(8,128)} %get-tuple-element.28), channel_id=1, source_target_pairs={{0,16},{16,0},{1,17},{17,1},{2,18},{18,2},{3,19},{19,3},{4,20},{20... | collective-permute-start | bytes 786440 | tf_op jit(solution)/shard_map/ppermute | solution.py:144
  90.2 1.0 copy-start.3
  101.4 3.5 %collective-permute-start.17 = (f32[1,128]{1,0:T(1,128)S(1)}, f32[1,128]{1,0:T(1,128)S(1)}, u32[]{:S(2)}, u32[]{:S(2)}) collective-permute-start(f32[1,128]{1,0:T(1,128)S(1)} %get-tuple-element.30), channel_id=1, source_target_pairs={{0,16},{16,0},{1,17},{17,1},{2,18},{18,2},{3,19},{19,3},{4,20},{20... | collective-permute-start | bytes 1544 | tf_op jit(solution)/shard_map/ppermute | solution.py:144
  105.1 1.1 collective-permute-start.18
  106.3 3.6 %collective-permute-start.19 = (f32[2,1,128]{2,1,0:T(1,128)S(1)}, f32[2,1,128]{2,1,0:T(1,128)S(1)}, u32[]{:S(2)}, u32[]{:S(2)}) collective-permute-start(f32[2,1,128]{2,1,0:T(1,128)S(1)} %fusion.1), channel_id=1, source_target_pairs={{0,2},{1,3},{2,0},{3,1},{4,6},{5,7},{6,4},{7,5},{8,10},{9,11},{10,... | collective-permute-start | bytes 3080 | tf_op jit(solution)/shard_map/ppermute | solution.py:352
  109.9 3.6 %collective-permute-start.20 = (f32[2,1,128]{2,1,0:T(1,128)S(1)}, f32[2,1,128]{2,1,0:T(1,128)S(1)}, u32[]{:S(2)}, u32[]{:S(2)}) collective-permute-start(f32[2,1,128]{2,1,0:T(1,128)S(1)} %fusion.2), channel_id=1, source_target_pairs={{0,4},{1,5},{2,6},{3,7},{4,0},{5,1},{6,2},{7,3},{8,12},{9,13},{10,... | collective-permute-start | bytes 3080 | tf_op jit(solution)/shard_map/ppermute | solution.py:352
  113.5 4.5 %collective-permute-start.21 = (f32[2,1,128]{2,1,0:T(1,128)S(1)}, f32[2,1,128]{2,1,0:T(1,128)S(1)}, u32[]{:S(2)}, u32[]{:S(2)}) collective-permute-start(f32[2,1,128]{2,1,0:T(1,128)S(1)} %add.16), channel_id=1, source_target_pairs={{0,8},{1,9},{2,10},{3,11},{4,12},{5,13},{6,14},{7,15},{8,0},{9,1},... | collective-permute-start | bytes 3080 | tf_op jit(solution)/shard_map/ppermute | solution.py:352

commit v5 on v4

--- a/solution.py
+++ b/solution.py
@@ -13,6 +13,8 @@
 SPAN = 512
 RESERVE = 8
 OUTER = 50
+HOME = 60
+LOAD = 4096
 ANYWHERE = pl.BlockSpec(memory_space=pl.ANY)
 CHIP = pl.BlockSpec(memory_space=pltpu.VMEM)
 
@@ -64,7 +66,7 @@
         in_specs=[ANYWHERE] * (count + len(after)),
         out_specs=[CHIP] * len(shapes),
         scratch_shapes=[pltpu.SemaphoreType.DMA((len(moves),))],
-        compiler_params=pltpu.CompilerParams(vmem_limit_bytes=62 * MIB),
+        compiler_params=pltpu.CompilerParams(vmem_limit_bytes=60 * MIB),
         cost_estimate=pl.CostEstimate(
             flops=0,
             transcendentals=0,
@@ -99,14 +101,17 @@
         ]
         return [*buffers, pltpu.SemaphoreType.DMA((len(self.keys),))]
 
-    def start(self, ins, buffers):
+    def bind(self, ins, buffers):
         self.copies, self.refs = [], buffers[:-1]
         for i, (k, lead, first, width) in enumerate(self.keys):
             columns = pl.ds(first, width)
             row = lax.axis_index("grp") if lead == "mine" else lead
             source = ins[k].at[:, columns] if lead is None else ins[k].at[row, :, columns]
             self.copies.append(pltpu.make_async_copy(source, buffers[i], buffers[-1].at[i]))
-            self.copies[-1].start()
+
+    def start(self, wanted):
+        for i in wanted:
+            self.copies[i].start()
 
     def wait(self, wanted):
         for i in sorted(set(wanted)):
@@ -115,14 +120,16 @@
                 self.copies[i] = None
 
 
-def products(total, tokens, factors, width):
+def add_products(target, fresh, tokens, factors, width):
     for a in range(0, width, SPAN):
         span = min(SPAN, width - a)
         left = rows_of([ref[:, first + a : first + a + span] for ref, first in tokens])
         right = rows_of([ref[:, first + a : first + a + span] for ref, first in factors])
         product = contract(left, right)
-        total = product if total is None else total + product
-    return total
+        if fresh and a == 0:
+            target[...] = product
+        else:
+            target[...] += product
 
 
 def solution(mesh):
@@ -156,7 +163,7 @@
         tokens_here = activations.shape[1]
         width = backprops.shape[2]
         depth = activations.shape[2]
-        cut = depth * 5 // 8
+        cut = depth * 19 // 32
         packed = width + cut
         beyond = depth - cut
         columns = out_factors.shape[1]
@@ -172,7 +179,7 @@
                 ranges.append((in_source, layer, max(start - width, 0), stop - width))
             return ranges
 
-        edges = [0, width * 3 // 8, width * 7 // 8, packed]
+        edges = [0, width * 6 // 16, width * 13 // 16, packed]
 
         def away_part(k):
             return packing(1, 0, "other", edges[k], edges[k + 1])
@@ -232,8 +239,9 @@
         count_home = len(home_loads.arrays)
 
         def home_kernel(*refs):
-            lengths_ref, mine_ref, other_ref, *scratch = refs[count_home:]
-            home_loads.start(refs[:count_home], scratch)
+            lengths_ref, mine_ref, other_ref, total, *scratch = refs[count_home:]
+            home_loads.bind(refs[:count_home], scratch)
+            home_loads.start(range(len(home_loads.keys)))
             me = lax.axis_index("grp")
             first = lax.axis_index("blk") // 2 * chip_tokens
             limit = lengths_ref[first // LEN].astype(jnp.float32)
@@ -243,15 +251,15 @@
                 for side in sides:
                     home_loads.wait(side)
                 tokens, factors = ([(home_loads.refs[i], 0) for i in side] for side in sides)
-                value = products(None, tokens, factors, beyond)
+                add_products(total, True, tokens, factors, beyond)
 
                 @pl.when(me == k)
                 def _():
-                    mine_ref[:, :shard_rows] = value
+                    mine_ref[:, :shard_rows] = total[...]
 
                 @pl.when(me != k)
                 def _():
-                    other_ref[:, :shard_rows] = value
+                    other_ref[:, :shard_rows] = total[...]
 
         extra = jax.ShapeDtypeStruct((chip_tokens, lanes), jnp.float32)
         home_mine, home_away = pl.pallas_call(
@@ -259,15 +267,18 @@
             out_shape=[extra] * 2,
             in_specs=[ANYWHERE] * count_home + [pl.BlockSpec(memory_space=pltpu.SMEM)],
             out_specs=[CHIP] * 2,
-            scratch_shapes=home_loads.scratch(),
-            compiler_params=pltpu.CompilerParams(vmem_limit_bytes=OUTER * MIB),
+            scratch_shapes=[
+                pltpu.VMEM((chip_tokens, shard_rows), jnp.float32),
+                *home_loads.scratch(),
+            ],
+            compiler_params=pltpu.CompilerParams(vmem_limit_bytes=HOME * MIB),
             cost_estimate=cost(2 * shard_rows * chip_tokens * 2 * beyond),
         )(*home_loads.arrays, lengths)
         home_away = swap_grp(home_away)
 
         main_loads = Loads()
         main_plan = []
-        points = sorted({0, width // 2, width, middle, packed, *edges[1:]})
+        points = sorted({*range(0, packed, LOAD), width, middle, packed, *edges[1:]})
         for a, b in zip(points[:-1], points[1:]):
             k = max(i for i in range(3) if edges[i] <= a)
             side = int(a >= width)
@@ -279,14 +290,14 @@
 
         def main_kernel(*refs):
             out_refs, scratch = refs[count_main : count_main + 2], refs[count_main + 2 :]
-            main_loads.start(refs[:count_main], scratch)
-            totals = [None, None]
-            for side, tokens, factors, span in main_plan:
-                main_loads.wait([*tokens, *factors])
+            main_loads.bind(refs[:count_main], scratch)
+            wanted = [[*tokens, *factors] for _, tokens, factors, _ in main_plan]
+            for some in wanted:
+                main_loads.start(some)
+            for i, (side, tokens, factors, span) in enumerate(main_plan):
+                main_loads.wait(wanted[i])
                 pieces = ([(main_loads.refs[i], 0) for i in x] for x in (tokens, factors))
-                totals[side] = products(totals[side], *pieces, span)
-            for ref, total in zip(out_refs, totals):
-                ref[...] = total
+                add_products(out_refs[side], main_plan[i - 1][0] != side or not i, *pieces, span)
 
         proj = jax.ShapeDtypeStruct((2 * chip_tokens, shard_rows), jnp.float32)
         proj_out, proj_in = pl.pallas_call(

time: 119 us -> 116 us (0.975)
  local copies, waits for them, and re-layouts: 2.8 us -> 1.11 us
  Pallas kernels: 20.6 us -> 19.3 us
    ppermute x4, waiting for transfers between devices: 27.4 us -> 31.9 us  [back_of(): return lax.ppermute(x, 'blk', backward)]
    ppermute x5, waiting for transfers between devices: 33.9 us -> 29.9 us  [swap_grp(): return lax.ppermute(x, 'grp', [(0, 1), (1, 0)])]
    unnamed x16 -> x18, local copies, waits for them, and re-layouts: 2.74 us -> 1.05 us
    pallas_call x1, Pallas kernels: 9.73 us -> 8.52 us  [shards(): pl.pallas_call(main_kernel, out_shape=[proj] * 2, in_specs=[ANYWHERE] * c...]
  transfers between devices with their start and end apart: 22 -> 22, of which waited for: 12 -> 12; matrix products, arithmetic and copies ran while one was open for 0% -> 0% of each run, Pallas kernels for 15% -> 14%
where the time goes in v5:
time: 116 us
  waiting for transfers between devices  70.1 us (60%)
  starting transfers between devices  23.7 us (20%)
  Pallas kernels  19.3 us (17%)
    ppermute x4, waiting for transfers between devices, back_of(): return lax.ppermute(x, 'blk', backward)  31.9 us
    ppermute x5, waiting for transfers between devices, swap_grp(): return lax.ppermute(x, 'grp', [(0, 1), (1, 0)])  29.9 us
    pallas_call x1, Pallas kernels, shards(): pl.pallas_call(main_kernel, out_shape=[proj] * 2, in_specs=[ANYWHERE] * c...  8.52 us
    ppermute x5, starting transfers between devices, swap_grp(): return lax.ppermute(x, 'grp', [(0, 1), (1, 0)])  8.29 us
    ppermute x4, waiting for transfers between devices, shards(): lax.ppermute(value, 'blk', [(i, i ^ bit) for i in range(blk)])  7.05 us
    ppermute x4, starting transfers between devices, back_of(): return lax.ppermute(x, 'blk', backward)  6.02 us
    pallas_call x2, Pallas kernels, move(): pl.pallas_call(kernel, out_shape=shapes, in_specs=[ANYWHERE] * (count + l...  5.93 us
    ppermute x4, starting transfers between devices, shards(): lax.ppermute(value, 'blk', [(i, i ^ bit) for i in range(blk)])  5.69 us
  transfers between devices with their start and end apart: 22, of which 12 were waited for; matrix products, arithmetic and copies ran while one was open for 0% of the time, Pallas kernels for 14%

profile of v5, /device:TPU:0, one launch (start us, length us, event | category | flops | bytes accessed | tf_op | source)
XLA Modules:
  0.0 115.7 jit_solution(1019567238217735017)
XLA Ops:
  0.0 2.7 %shard_map.55 = (bf16[24,19712]{1,0:T(8,128)(2,1)}, bf16[128,3072]{1,0:T(8,128)(2,1)}) custom-call(bf16[2,128,8192]{2,1,0:T(8,128)(2,1)} %refs_0_.5, bf16[2,128,8192]{2,1,0:T(8,128)(2,1)} %refs_8_.1, bf16[2,24,8192]{2,1,0:T(8,128)(2,1)} %refs_2_.1, bf16[2,24,8192]{2,1,0:T(8,128)(2,1)} %refs_3_.1), custom_call_target="tpu_custom_call" | custom-call | bytes 6930432 | tf_op jit(solution)/shard_map/pallas_call | solution.py:63
  2.7 3.0 %collective-permute-start.8 = (bf16[128,3072]{1,0:T(8,128)(2,1)}, bf16[128,3072]{1,0:T(8,128)(2,1)S(1)}, u32[]{:S(2)}, u32[]{:S(2)}) collective-permute-start(bf16[128,3072]{1,0:T(8,128)(2,1)} %get-tuple-element.19), channel_id=1, source_target_pairs={{0,16},{16,0},{1,17},{17,1},{2,18},{18,2},{3,19},{19,3},{4,20},{20... | collective-permute-start | bytes 2359304 | tf_op jit(solution)/shard_map/ppermute | solution.py:151
  5.8 1.5 %collective-permute-start.1 = (bf16[24,19712]{1,0:T(8,128)(2,1)}, bf16[24,19712]{1,0:T(8,128)(2,1)S(1)}, u32[]{:S(2)}, u32[]{:S(2)}) collective-permute-start(bf16[24,19712]{1,0:T(8,128)(2,1)} %get-tuple-element.18.refs_2_.refs_0_), channel_id=1, source_target_pairs={{4,0},{8,4},{12,8},{14,12},{10,14},{6,10},{2,6},{0,2},{5,1},{9,5},... | collective-permute-start | bytes 2838536 | tf_op jit(solution)/shard_map/ppermute | solution.py:157
  7.3 0.5 collective-permute-start
  7.8 0.0 collective-permute-start.15
  7.8 3.2 %shard_map.56 = (bf16[128,3584]{1,0:T(8,128)(2,1)}, bf16[128,6400]{1,0:T(8,128)(2,1)}) custom-call(bf16[2,128,8192]{2,1,0:T(8,128)(2,1)} %refs_0_.5, bf16[2,128,8192]{2,1,0:T(8,128)(2,1)} %refs_8_.1, bf16[24,19712]{1,0:T(8,128)(2,1)} %get-tuple-element.18.refs_2_.refs_0_), custom_call_target="tpu_custom_call" | custom-call | bytes 10223616 | tf_op jit(solution)/shard_map/pallas_call | solution.py:63
  11.0 12.5 %collective-permute-done.8.refs_10_ = bf16[128,3072]{1,0:T(8,128)(2,1)S(1)} collective-permute-done((bf16[128,3072]{1,0:T(8,128)(2,1)}, bf16[128,3072]{1,0:T(8,128)(2,1)S(1)}, u32[]{:S(2)}, u32[]{:S(2)}) %collective-permute-start.8) | collective-permute-done | bytes 786464 | tf_op jit(solution)/shard_map/ppermute | solution.py:151
  23.5 1.7 %collective-permute-start.10 = (bf16[128,3584]{1,0:T(8,128)(2,1)}, bf16[128,3584]{1,0:T(8,128)(2,1)}, u32[]{:S(2)}, u32[]{:S(2)}) collective-permute-start(bf16[128,3584]{1,0:T(8,128)(2,1)} %get-tuple-element.21), channel_id=1, source_target_pairs={{0,16},{16,0},{1,17},{17,1},{2,18},{18,2},{3,19},{19,3},{4,20},{20... | collective-permute-start | bytes 2752520 | tf_op jit(solution)/shard_map/ppermute | solution.py:151
  25.3 0.0 collective-permute-start.7
  25.3 3.1 %collective-permute-done.1.refs_2_.refs_4_ = bf16[24,19712]{1,0:T(8,128)(2,1)S(1)} collective-permute-done((bf16[24,19712]{1,0:T(8,128)(2,1)}, bf16[24,19712]{1,0:T(8,128)(2,1)S(1)}, u32[]{:S(2)}, u32[]{:S(2)}) %collective-permute-start.1) | collective-permute-done | bytes 946208 | tf_op jit(solution)/shard_map/ppermute | solution.py:157
  28.4 0.0 copy-start.5
  28.4 1.5 %collective-permute-start.3 = (bf16[24,19712]{1,0:T(8,128)(2,1)S(1)}, bf16[24,19712]{1,0:T(8,128)(2,1)S(1)}, u32[]{:S(2)}, u32[]{:S(2)}) collective-permute-start(bf16[24,19712]{1,0:T(8,128)(2,1)S(1)} %collective-permute-done.1.refs_2_.refs_4_), channel_id=1, source_target_pairs={{4,0},{8,4},{12,8},{14,12},{10,14},{6,10},{2,6},{0,2},{5,1},{9,5},... | collective-permute-start | bytes 2838536 | tf_op jit(solution)/shard_map/ppermute | solution.py:157
  29.9 0.0 collective-permute-done.refs_1_.refs_3_
  29.9 0.5 collective-permute-start.2
  30.4 14.9 %collective-permute-done.10.refs_12_ = bf16[128,3584]{1,0:T(8,128)(2,1)} collective-permute-done((bf16[128,3584]{1,0:T(8,128)(2,1)}, bf16[128,3584]{1,0:T(8,128)(2,1)}, u32[]{:S(2)}, u32[]{:S(2)}) %collective-permute-start.10) | collective-permute-done | bytes 917536 | tf_op jit(solution)/shard_map/ppermute | solution.py:151
  45.4 1.4 %collective-permute-start.12 = (bf16[128,6400]{1,0:T(8,128)(2,1)}, bf16[128,6400]{1,0:T(8,128)(2,1)}, u32[]{:S(2)}, u32[]{:S(2)}) collective-permute-start(bf16[128,6400]{1,0:T(8,128)(2,1)} %get-tuple-element.23), channel_id=1, source_target_pairs={{0,16},{16,0},{1,17},{17,1},{2,18},{18,2},{3,19},{19,3},{4,20},{20... | collective-permute-start | bytes 4915208 | tf_op jit(solution)/shard_map/ppermute | solution.py:151
  46.8 3.1 %collective-permute-done.3.refs_4_.refs_6_ = bf16[24,19712]{1,0:T(8,128)(2,1)S(1)} collective-permute-done((bf16[24,19712]{1,0:T(8,128)(2,1)S(1)}, bf16[24,19712]{1,0:T(8,128)(2,1)S(1)}, u32[]{:S(2)}, u32[]{:S(2)}) %collective-permute-start.3) | collective-permute-done | bytes 946208 | tf_op jit(solution)/shard_map/ppermute | solution.py:157
  49.9 1.5 %collective-permute-start.5 = (bf16[24,19712]{1,0:T(8,128)(2,1)S(1)}, bf16[24,19712]{1,0:T(8,128)(2,1)S(1)}, u32[]{:S(2)}, u32[]{:S(2)}) collective-permute-start(bf16[24,19712]{1,0:T(8,128)(2,1)S(1)} %collective-permute-done.3.refs_4_.refs_6_), channel_id=1, source_target_pairs={{4,0},{8,4},{12,8},{14,12},{10,14},{6,10},{2,6},{0,2},{5,1},{9,5},... | collective-permute-start | bytes 2838536 | tf_op jit(solution)/shard_map/ppermute | solution.py:157
  51.4 0.0 collective-permute-done.2.refs_3_.refs_5_
  51.4 0.0 copy-done.7
  51.4 1.0 collective-permute-start.4
  52.5 18.4 %collective-permute-done.5.refs_6_.refs_8_ = bf16[24,19712]{1,0:T(8,128)(2,1)S(1)} collective-permute-done((bf16[24,19712]{1,0:T(8,128)(2,1)S(1)}, bf16[24,19712]{1,0:T(8,128)(2,1)S(1)}, u32[]{:S(2)}, u32[]{:S(2)}) %collective-permute-start.5) | collective-permute-done | bytes 946208 | tf_op jit(solution)/shard_map/ppermute | solution.py:157
  70.9 0.0 copy-done.6
  70.9 1.5 %collective-permute-start.13 = (bf16[24,9856]{1,0:T(8,128)(2,1)S(1)}, bf16[24,9856]{1,0:T(8,128)(2,1)S(1)}, u32[]{:S(2)}, u32[]{:S(2)}) collective-permute-start(bf16[24,9856]{1,0:T(8,128)(2,1)S(1)} %slice.13), channel_id=1, source_target_pairs={{4,0},{8,4},{12,8},{14,12},{10,14},{6,10},{2,6},{0,2},{5,1},{9,5},... | collective-permute-start | bytes 1419272 | tf_op jit(solution)/shard_map/ppermute | solution.py:157
  72.4 0.0 collective-permute-done.4.refs_5_.refs_7_
  72.4 0.0 copy-done.5
  72.5 1.0 collective-permute-start.6
  73.5 7.2 %collective-permute-done.13.refs_18_.refs_9_ = bf16[24,9856]{1,0:T(8,128)(2,1)S(1)} collective-permute-done((bf16[24,9856]{1,0:T(8,128)(2,1)S(1)}, bf16[24,9856]{1,0:T(8,128)(2,1)S(1)}, u32[]{:S(2)}, u32[]{:S(2)}) %collective-permute-start.13) | collective-permute-done | bytes 473120 | tf_op jit(solution)/shard_map/ppermute | solution.py:157
  80.7 1.3 %collective-permute-done.6.refs_7_ = bf16[24,9856]{1,0:T(8,128)(2,1)S(1)} collective-permute-done((bf16[24,9856]{1,0:T(8,128)(2,1)S(1)}, bf16[24,9856]{1,0:T(8,128)(2,1)S(1)}, u32[]{:S(2)}, u32[]{:S(2)}) %collective-permute-start.6) | collective-permute-done | bytes 473120 | tf_op jit(solution)/shard_map/ppermute | solution.py:154
  81.9 0.0 collective-permute-done.12.refs_14_
  81.9 0.0 collective-permute-start.14
  81.9 0.0 copy-done.4
  81.9 0.5 collective-permute-start.11
  82.4 0.0 copy-done.8
  82.4 0.1 collective-permute-start.9
  83.2 0.0 collective-permute-done.15.refs_17_.refs_1_
  83.2 0.0 copy-done.3
  83.2 0.0 copy-done
  83.2 4.4 %shard_map.58 = (f32[256,256]{1,0:T(8,128)}, f32[256,256]{1,0:T(8,128)}) custom-call(bf16[2,128,8192]{2,1,0:T(8,128)(2,1)} %refs_0_.5, bf16[2,128,8192]{2,1,0:T(8,128)(2,1)} %collective-permute-done.15.refs_17_.refs_1_, bf16[24,19712]{1,0:T(8,128)(2,1)} %get-tuple-element.18.refs_2_.refs_0_, bf16[24,19712]{1,0:T(8,128)(2,1)} %copy-done.6, ...), custom_call_target="tpu_custom_call" | custom-call | flops 654311424 | bytes 10223616 | tf_op jit(solution)/shard_map/pallas_call | solution.py:265
  87.6 1.0 collective-permute-start.16
  88.6 0.0 collective-permute-done.9.refs_11_
  88.6 0.0 collective-permute-done.11.refs_13_
  88.6 0.0 collective-permute-done.7.refs_9_
  88.6 0.0 collective-permute-done.14.refs_15_
  88.6 0.0 copy-start.1
  88.6 1.0 copy-done.1
  89.6 8.5 %shard_map.57 = (f32[512,192]{1,0:T(8,128)S(1)}, f32[512,192]{1,0:T(8,128)S(1)}) custom-call(bf16[24,19712]{1,0:T(8,128)(2,1)} %get-tuple-element.18.refs_2_.refs_0_, bf16[24,19712]{1,0:T(8,128)(2,1)} %copy-done.6, bf16[24,19712]{1,0:T(8,128)(2,1)} %copy-done.5, bf16[24,19712]{1,0:T(8,128)(2,1)} %copy-done.8, bf16[24,19712]{1,0:T(8,128)(2,1)} %copy-done.7, ...), custom_call_target="tpu_custom_call" | custom-call | flops 2566914048 | bytes 40108032 | tf_op jit(solution)/shard_map/pallas_call | solution.py:303
  98.2 0.0 collective-permute-done.16.refs_3_
  98.2 0.0 copy-done.2
  98.2 0.4 shard_map.59
  98.6 1.1 collective-permute-start.17
  99.8 2.4 %collective-permute-done.17 = f32[1,128]{1,0:T(1,128)S(1)} collective-permute-done((f32[1,128]{1,0:T(1,128)S(1)}, f32[1,128]{1,0:T(1,128)S(1)}, u32[]{:S(2)}, u32[]{:S(2)}) %collective-permute-start.17) | collective-permute-done | bytes 544 | tf_op jit(solution)/shard_map/ppermute | solution.py:151
  102.2 0.1 fusion
  102.3 0.0 collective-permute-start.18
  102.3 1.1 collective-permute-done.18
  103.4 0.1 fusion.1
  103.5 1.5 %collective-permute-start.19 = (f32[2,1,128]{2,1,0:T(1,128)S(1)}, f32[2,1,128]{2,1,0:T(1,128)S(1)}, u32[]{:S(2)}, u32[]{:S(2)}) collective-permute-start(f32[2,1,128]{2,1,0:T(1,128)S(1)} %fusion.1), channel_id=1, source_target_pairs={{0,2},{1,3},{2,0},{3,1},{4,6},{5,7},{6,4},{7,5},{8,10},{9,11},{10,... | collective-permute-start | bytes 3080 | tf_op jit(solution)/shard_map/ppermute | solution.py:363
  105.0 2.1 %collective-permute-done.19 = f32[2,1,128]{2,1,0:T(1,128)S(1)} collective-permute-done((f32[2,1,128]{2,1,0:T(1,128)S(1)}, f32[2,1,128]{2,1,0:T(1,128)S(1)}, u32[]{:S(2)}, u32[]{:S(2)}) %collective-permute-start.19) | collective-permute-done | bytes 1056 | tf_op jit(solution)/shard_map/ppermute | solution.py:363
  107.0 0.1 fusion.2
  107.1 1.6 %collective-permute-start.20 = (f32[2,1,128]{2,1,0:T(1,128)S(1)}, f32[2,1,128]{2,1,0:T(1,128)S(1)}, u32[]{:S(2)}, u32[]{:S(2)}) collective-permute-start(f32[2,1,128]{2,1,0:T(1,128)S(1)} %fusion.2), channel_id=1, source_target_pairs={{0,4},{1,5},{2,6},{3,7},{4,0},{5,1},{6,2},{7,3},{8,12},{9,13},{10,... | collective-permute-start | bytes 3080 | tf_op jit(solution)/shard_map/ppermute | solution.py:363
  108.7 2.0 %collective-permute-done.20 = f32[2,1,128]{2,1,0:T(1,128)S(1)} collective-permute-done((f32[2,1,128]{2,1,0:T(1,128)S(1)}, f32[2,1,128]{2,1,0:T(1,128)S(1)}, u32[]{:S(2)}, u32[]{:S(2)}) %collective-permute-start.20) | collective-permute-done | bytes 1056 | tf_op jit(solution)/shard_map/ppermute | solution.py:363
  110.7 2.6 %collective-permute-start.21 = (f32[2,1,128]{2,1,0:T(1,128)S(1)}, f32[2,1,128]{2,1,0:T(1,128)S(1)}, u32[]{:S(2)}, u32[]{:S(2)}) collective-permute-start(f32[2,1,128]{2,1,0:T(1,128)S(1)} %add.16), channel_id=1, source_target_pairs={{0,8},{1,9},{2,10},{3,11},{4,12},{5,13},{6,14},{7,15},{8,0},{9,1},... | collective-permute-start | bytes 3080 | tf_op jit(solution)/shard_map/ppermute | solution.py:363
  113.3 1.9 %collective-permute-done.21 = f32[2,1,128]{2,1,0:T(1,128)S(1)} collective-permute-done((f32[2,1,128]{2,1,0:T(1,128)S(1)}, f32[2,1,128]{2,1,0:T(1,128)S(1)}, u32[]{:S(2)}, u32[]{:S(2)}) %collective-permute-start.21) | collective-permute-done | bytes 1056 | tf_op jit(solution)/shard_map/ppermute | solution.py:363
  115.2 0.6 slice_add_fusion
  (11 shorter events, 0.1 us)
Async XLA Ops:
  2.7 20.8 %collective-permute-start.8 = (bf16[128,3072]{1,0:T(8,128)(2,1)}, bf16[128,3072]{1,0:T(8,128)(2,1)S(1)}, u32[]{:S(2)}, u32[]{:S(2)}) collective-permute-start(bf16[128,3072]{1,0:T(8,128)(2,1)} %get-tuple-element.19), channel_id=1, source_target_pairs={{0,16},{16,0},{1,17},{17,1},{2,18},{18,2},{3,19},{19,3},{4,20},{20... | collective-permute-start | bytes 2359304 | tf_op jit(solution)/shard_map/ppermute | solution.py:151
  5.8 22.6 %collective-permute-start.1 = (bf16[24,19712]{1,0:T(8,128)(2,1)}, bf16[24,19712]{1,0:T(8,128)(2,1)S(1)}, u32[]{:S(2)}, u32[]{:S(2)}) collective-permute-start(bf16[24,19712]{1,0:T(8,128)(2,1)} %get-tuple-element.18.refs_2_.refs_0_), channel_id=1, source_target_pairs={{4,0},{8,4},{12,8},{14,12},{10,14},{6,10},{2,6},{0,2},{5,1},{9,5},... | collective-permute-start | bytes 2838536 | tf_op jit(solution)/shard_map/ppermute | solution.py:157
  7.3 22.6 %collective-permute-start = (bf16[24,19712]{1,0:T(8,128)(2,1)}, bf16[24,19712]{1,0:T(8,128)(2,1)S(1)}, u32[]{:S(2)}, u32[]{:S(2)}) collective-permute-start(bf16[24,19712]{1,0:T(8,128)(2,1)} %get-tuple-element.18.refs_2_.refs_0_), channel_id=1, source_target_pairs={{0,4},{4,8},{8,12},{12,14},{14,10},{10,6},{6,2},{2,0},{1,5},{5,9},... | collective-permute-start | bytes 2838536 | tf_op jit(solution)/shard_map/ppermute | solution.py:154
  7.8 75.4 %collective-permute-start.15 = (bf16[2,128,8192]{2,1,0:T(8,128)(2,1)}, bf16[2,128,8192]{2,1,0:T(8,128)(2,1)}, u32[]{:S(2)}, u32[]{:S(2)}) collective-permute-start(bf16[2,128,8192]{2,1,0:T(8,128)(2,1)} %refs_0_.5), channel_id=1, source_target_pairs={{0,1},{1,0},{2,3},{3,2},{4,5},{5,4},{6,7},{7,6},{8,9},{9,8},{10,11... | collective-permute-start | bytes 12582920 | tf_op jit(solution)/shard_map/ppermute | solution.py:148
  23.5 21.9 %collective-permute-start.10 = (bf16[128,3584]{1,0:T(8,128)(2,1)}, bf16[128,3584]{1,0:T(8,128)(2,1)}, u32[]{:S(2)}, u32[]{:S(2)}) collective-permute-start(bf16[128,3584]{1,0:T(8,128)(2,1)} %get-tuple-element.21), channel_id=1, source_target_pairs={{0,16},{16,0},{1,17},{17,1},{2,18},{18,2},{3,19},{19,3},{4,20},{20... | collective-permute-start | bytes 2752520 | tf_op jit(solution)/shard_map/ppermute | solution.py:151
  25.3 63.3 %collective-permute-start.7 = (bf16[2,128,8192]{2,1,0:T(8,128)(2,1)}, bf16[2,128,8192]{2,1,0:T(8,128)(2,1)}, u32[]{:S(2)}, u32[]{:S(2)}) collective-permute-start(bf16[2,128,8192]{2,1,0:T(8,128)(2,1)} %refs_8_.1), channel_id=1, source_target_pairs={{0,1},{1,0},{2,3},{3,2},{4,5},{5,4},{6,7},{7,6},{8,9},{9,8},{10,11... | collective-permute-start | bytes 12582920 | tf_op jit(solution)/shard_map/ppermute | solution.py:148
  28.4 44.0 %copy-start.5 = (bf16[24,19712]{1,0:T(8,128)(2,1)}, bf16[24,19712]{1,0:T(8,128)(2,1)S(1)}, u32[]{:S(2)}) copy-start(bf16[24,19712]{1,0:T(8,128)(2,1)S(1)} %collective-permute-done.1.refs_2_.refs_4_) | copy-start | bytes 2838532
  28.4 21.5 %collective-permute-start.3 = (bf16[24,19712]{1,0:T(8,128)(2,1)S(1)}, bf16[24,19712]{1,0:T(8,128)(2,1)S(1)}, u32[]{:S(2)}, u32[]{:S(2)}) collective-permute-start(bf16[24,19712]{1,0:T(8,128)(2,1)S(1)} %collective-permute-done.1.refs_2_.refs_4_), channel_id=1, source_target_pairs={{4,0},{8,4},{12,8},{14,12},{10,14},{6,10},{2,6},{0,2},{5,1},{9,5},... | collective-permute-start | bytes 2838536 | tf_op jit(solution)/shard_map/ppermute | solution.py:157
  29.9 41.0 %copy-start.6 = (bf16[24,19712]{1,0:T(8,128)(2,1)}, bf16[24,19712]{1,0:T(8,128)(2,1)S(1)}, u32[]{:S(2)}) copy-start(bf16[24,19712]{1,0:T(8,128)(2,1)S(1)} %collective-permute-done.refs_1_.refs_3_) | copy-start | bytes 2838532
  29.9 21.5 %collective-permute-start.2 = (bf16[24,19712]{1,0:T(8,128)(2,1)S(1)}, bf16[24,19712]{1,0:T(8,128)(2,1)S(1)}, u32[]{:S(2)}, u32[]{:S(2)}) collective-permute-start(bf16[24,19712]{1,0:T(8,128)(2,1)S(1)} %collective-permute-done.refs_1_.refs_3_), channel_id=1, source_target_pairs={{0,4},{4,8},{8,12},{12,14},{14,10},{10,6},{6,2},{2,0},{1,5},{5,9},... | collective-permute-start | bytes 2838536 | tf_op jit(solution)/shard_map/ppermute | solution.py:154
  45.4 36.6 %collective-permute-start.12 = (bf16[128,6400]{1,0:T(8,128)(2,1)}, bf16[128,6400]{1,0:T(8,128)(2,1)}, u32[]{:S(2)}, u32[]{:S(2)}) collective-permute-start(bf16[128,6400]{1,0:T(8,128)(2,1)} %get-tuple-element.23), channel_id=1, source_target_pairs={{0,16},{16,0},{1,17},{17,1},{2,18},{18,2},{3,19},{19,3},{4,20},{20... | collective-permute-start | bytes 4915208 | tf_op jit(solution)/shard_map/ppermute | solution.py:151
  49.9 1.5 %copy-start.7 = (bf16[24,19712]{1,0:T(8,128)(2,1)}, bf16[24,19712]{1,0:T(8,128)(2,1)S(1)}, u32[]{:S(2)}) copy-start(bf16[24,19712]{1,0:T(8,128)(2,1)S(1)} %collective-permute-done.3.refs_4_.refs_6_) | copy-start | bytes 2838532
  49.9 20.9 %collective-permute-start.5 = (bf16[24,19712]{1,0:T(8,128)(2,1)S(1)}, bf16[24,19712]{1,0:T(8,128)(2,1)S(1)}, u32[]{:S(2)}, u32[]{:S(2)}) collective-permute-start(bf16[24,19712]{1,0:T(8,128)(2,1)S(1)} %collective-permute-done.3.refs_4_.refs_6_), channel_id=1, source_target_pairs={{4,0},{8,4},{12,8},{14,12},{10,14},{6,10},{2,6},{0,2},{5,1},{9,5},... | collective-permute-start | bytes 2838536 | tf_op jit(solution)/shard_map/ppermute | solution.py:157
  51.4 31.0 %copy-start.8 = (bf16[24,19712]{1,0:T(8,128)(2,1)}, bf16[24,19712]{1,0:T(8,128)(2,1)S(1)}, u32[]{:S(2)}) copy-start(bf16[24,19712]{1,0:T(8,128)(2,1)S(1)} %collective-permute-done.2.refs_3_.refs_5_) | copy-start | bytes 2838532
  51.4 21.0 %collective-permute-start.4 = (bf16[24,19712]{1,0:T(8,128)(2,1)S(1)}, bf16[24,19712]{1,0:T(8,128)(2,1)S(1)}, u32[]{:S(2)}, u32[]{:S(2)}) collective-permute-start(bf16[24,19712]{1,0:T(8,128)(2,1)S(1)} %collective-permute-done.2.refs_3_.refs_5_), channel_id=1, source_target_pairs={{0,4},{4,8},{8,12},{12,14},{14,10},{10,6},{6,2},{2,0},{1,5},{5,9},... | collective-permute-start | bytes 2838536 | tf_op jit(solution)/shard_map/ppermute | solution.py:154
  70.9 12.3 %copy-start.3 = (bf16[24,19712]{1,0:T(8,128)(2,1)}, bf16[24,19712]{1,0:T(8,128)(2,1)S(1)}, u32[]{:S(2)}) copy-start(bf16[24,19712]{1,0:T(8,128)(2,1)S(1)} %collective-permute-done.5.refs_6_.refs_8_) | copy-start | bytes 2838532
  70.9 9.8 %collective-permute-start.13 = (bf16[24,9856]{1,0:T(8,128)(2,1)S(1)}, bf16[24,9856]{1,0:T(8,128)(2,1)S(1)}, u32[]{:S(2)}, u32[]{:S(2)}) collective-permute-start(bf16[24,9856]{1,0:T(8,128)(2,1)S(1)} %slice.13), channel_id=1, source_target_pairs={{4,0},{8,4},{12,8},{14,12},{10,14},{6,10},{2,6},{0,2},{5,1},{9,5},... | collective-permute-start | bytes 1419272 | tf_op jit(solution)/shard_map/ppermute | solution.py:157
  72.4 9.5 %copy-start.4 = (bf16[24,19712]{1,0:T(8,128)(2,1)}, bf16[24,19712]{1,0:T(8,128)(2,1)S(1)}, u32[]{:S(2)}) copy-start(bf16[24,19712]{1,0:T(8,128)(2,1)S(1)} %collective-permute-done.4.refs_5_.refs_7_) | copy-start | bytes 2838532
  72.5 9.4 %collective-permute-start.6 = (bf16[24,9856]{1,0:T(8,128)(2,1)S(1)}, bf16[24,9856]{1,0:T(8,128)(2,1)S(1)}, u32[]{:S(2)}, u32[]{:S(2)}) collective-permute-start(bf16[24,9856]{1,0:T(8,128)(2,1)S(1)} %slice.12), channel_id=1, source_target_pairs={{0,4},{4,8},{8,12},{12,14},{14,10},{10,6},{6,2},{2,0},{1,5},{5,9},... | collective-permute-start | bytes 1419272 | tf_op jit(solution)/shard_map/ppermute | solution.py:154
  80.7 2.5 %copy-start = (bf16[24,9856]{1,0:T(8,128)(2,1)}, bf16[24,9856]{1,0:T(8,128)(2,1)S(1)}, u32[]{:S(2)}) copy-start(bf16[24,9856]{1,0:T(8,128)(2,1)S(1)} %collective-permute-done.13.refs_18_.refs_9_) | copy-start | bytes 1419268
  81.9 6.7 %collective-permute-start.14 = (bf16[128,6400]{1,0:T(8,128)(2,1)}, bf16[128,6400]{1,0:T(8,128)(2,1)}, u32[]{:S(2)}, u32[]{:S(2)}) collective-permute-start(bf16[128,6400]{1,0:T(8,128)(2,1)} %collective-permute-done.12.refs_14_), channel_id=1, source_target_pairs={{0,1},{1,0},{2,3},{3,2},{4,5},{5,4},{6,7},{7,6},{8,9},{9,8},{10,11... | collective-permute-start | bytes 4915208 | tf_op jit(solution)/shard_map/ppermute | solution.py:148
  81.9 6.6 %collective-permute-start.11 = (bf16[128,3584]{1,0:T(8,128)(2,1)}, bf16[128,3584]{1,0:T(8,128)(2,1)}, u32[]{:S(2)}, u32[]{:S(2)}) collective-permute-start(bf16[128,3584]{1,0:T(8,128)(2,1)} %collective-permute-done.10.refs_12_), channel_id=1, source_target_pairs={{0,1},{1,0},{2,3},{3,2},{4,5},{5,4},{6,7},{7,6},{8,9},{9,8},{10,11... | collective-permute-start | bytes 2752520 | tf_op jit(solution)/shard_map/ppermute | solution.py:148
  82.4 6.1 %collective-permute-start.9 = (bf16[128,3072]{1,0:T(8,128)(2,1)S(1)}, bf16[128,3072]{1,0:T(8,128)(2,1)S(1)}, u32[]{:S(2)}, u32[]{:S(2)}) collective-permute-start(bf16[128,3072]{1,0:T(8,128)(2,1)S(1)} %collective-permute-done.8.refs_10_), channel_id=1, source_target_pairs={{0,1},{1,0},{2,3},{3,2},{4,5},{5,4},{6,7},{7,6},{8,9},{9,8},{10,11... | collective-permute-start | bytes 2359304 | tf_op jit(solution)/shard_map/ppermute | solution.py:148
  87.6 10.6 %collective-permute-start.16 = (f32[256,256]{1,0:T(8,128)}, f32[256,256]{1,0:T(8,128)S(1)}, u32[]{:S(2)}, u32[]{:S(2)}) collective-permute-start(f32[256,256]{1,0:T(8,128)} %get-tuple-element.28), channel_id=1, source_target_pairs={{0,16},{16,0},{1,17},{17,1},{2,18},{18,2},{3,19},{19,3},{4,20},{20... | collective-permute-start | bytes 786440 | tf_op jit(solution)/shard_map/ppermute | solution.py:151
  88.6 1.0 copy-start.1
  89.6 8.5 %copy-start.2 = (f32[256,256]{1,0:T(8,128)S(1)}, f32[256,256]{1,0:T(8,128)}, u32[]{:S(2)}) copy-start(f32[256,256]{1,0:T(8,128)} %get-tuple-element.27.refs_2_) | copy-start | bytes 786436
  98.6 3.5 %collective-permute-start.17 = (f32[1,128]{1,0:T(1,128)S(1)}, f32[1,128]{1,0:T(1,128)S(1)}, u32[]{:S(2)}, u32[]{:S(2)}) collective-permute-start(f32[1,128]{1,0:T(1,128)S(1)} %get-tuple-element.30), channel_id=1, source_target_pairs={{0,16},{16,0},{1,17},{17,1},{2,18},{18,2},{3,19},{19,3},{4,20},{20... | collective-permute-start | bytes 1544 | tf_op jit(solution)/shard_map/ppermute | solution.py:151
  102.3 1.1 collective-permute-start.18
  103.5 3.6 %collective-permute-start.19 = (f32[2,1,128]{2,1,0:T(1,128)S(1)}, f32[2,1,128]{2,1,0:T(1,128)S(1)}, u32[]{:S(2)}, u32[]{:S(2)}) collective-permute-start(f32[2,1,128]{2,1,0:T(1,128)S(1)} %fusion.1), channel_id=1, source_target_pairs={{0,2},{1,3},{2,0},{3,1},{4,6},{5,7},{6,4},{7,5},{8,10},{9,11},{10,... | collective-permute-start | bytes 3080 | tf_op jit(solution)/shard_map/ppermute | solution.py:363
  107.1 3.6 %collective-permute-start.20 = (f32[2,1,128]{2,1,0:T(1,128)S(1)}, f32[2,1,128]{2,1,0:T(1,128)S(1)}, u32[]{:S(2)}, u32[]{:S(2)}) collective-permute-start(f32[2,1,128]{2,1,0:T(1,128)S(1)} %fusion.2), channel_id=1, source_target_pairs={{0,4},{1,5},{2,6},{3,7},{4,0},{5,1},{6,2},{7,3},{8,12},{9,13},{10,... | collective-permute-start | bytes 3080 | tf_op jit(solution)/shard_map/ppermute | solution.py:363
  110.7 4.5 %collective-permute-start.21 = (f32[2,1,128]{2,1,0:T(1,128)S(1)}, f32[2,1,128]{2,1,0:T(1,128)S(1)}, u32[]{:S(2)}, u32[]{:S(2)}) collective-permute-start(f32[2,1,128]{2,1,0:T(1,128)S(1)} %add.16), channel_id=1, source_target_pairs={{0,8},{1,9},{2,10},{3,11},{4,12},{5,13},{6,14},{7,15},{8,0},{9,1},... | collective-permute-start | bytes 3080 | tf_op jit(solution)/shard_map/ppermute | solution.py:363

commit v6 on v5

--- a/solution.py
+++ b/solution.py
@@ -12,9 +12,9 @@
 MIB = 2**20
 SPAN = 512
 RESERVE = 8
-OUTER = 50
-HOME = 60
-LOAD = 4096
+OUTER = 52
+HOME = 52
+LOAD = 16384
 ANYWHERE = pl.BlockSpec(memory_space=pl.ANY)
 CHIP = pl.BlockSpec(memory_space=pltpu.VMEM)
 
@@ -239,9 +239,15 @@
         count_home = len(home_loads.arrays)
 
         def home_kernel(*refs):
-            lengths_ref, mine_ref, other_ref, total, *scratch = refs[count_home:]
+            back_ref, lengths_ref, mine_ref, other_ref, held_ref, total, held_sem, *scratch = refs[
+                count_home:
+            ]
+            held = pltpu.make_async_copy(
+                back_ref.at[:, pl.ds(0, packed - middle)], held_ref, held_sem
+            )
             home_loads.bind(refs[:count_home], scratch)
             home_loads.start(range(len(home_loads.keys)))
+            held.start()
             me = lax.axis_index("grp")
             first = lax.axis_index("blk") // 2 * chip_tokens
             limit = lengths_ref[first // LEN].astype(jnp.float32)
@@ -261,21 +267,29 @@
                 def _():
                     other_ref[:, :shard_rows] = total[...]
 
+            held.wait()
+
         extra = jax.ShapeDtypeStruct((chip_tokens, lanes), jnp.float32)
-        home_mine, home_away = pl.pallas_call(
+        home_mine, home_away, back_held = pl.pallas_call(
             home_kernel,
-            out_shape=[extra] * 2,
-            in_specs=[ANYWHERE] * count_home + [pl.BlockSpec(memory_space=pltpu.SMEM)],
-            out_specs=[CHIP] * 2,
+            out_shape=[
+                extra,
+                extra,
+                jax.ShapeDtypeStruct((columns, packed - middle), last[1].dtype),
+            ],
+            in_specs=[ANYWHERE] * (count_home + 1) + [pl.BlockSpec(memory_space=pltpu.SMEM)],
+            out_specs=[CHIP] * 3,
             scratch_shapes=[
                 pltpu.VMEM((chip_tokens, shard_rows), jnp.float32),
+                pltpu.SemaphoreType.DMA,
                 *home_loads.scratch(),
             ],
             compiler_params=pltpu.CompilerParams(vmem_limit_bytes=HOME * MIB),
             cost_estimate=cost(2 * shard_rows * chip_tokens * 2 * beyond),
-        )(*home_loads.arrays, lengths)
+        )(*home_loads.arrays, last[1], lengths)
         home_away = swap_grp(home_away)
 
+        last = (last[0], back_held)
         main_loads = Loads()
         main_plan = []
         points = sorted({*range(0, packed, LOAD), width, middle, packed, *edges[1:]})

time: 116 us -> 115 us (level)
  waiting for transfers between devices: 70.1 us -> 71.6 us
  transfers between devices with their start and end apart: 22 -> 22, of which waited for: 12 -> 13; matrix products, arithmetic and copies ran while one was open for 0% -> 0% of each run, Pallas kernels for 14% -> 13%
where the time goes in v6:
time: 115 us; the launch traced here: 114 us
  waiting for transfers between devices  71.6 us (62%)
  starting transfers between devices  22.7 us (20%)
  Pallas kernels  18.3 us (16%)
    ppermute x4, waiting for transfers between devices, back_of(): return lax.ppermute(x, 'blk', backward)  31.9 us
    ppermute x5, waiting for transfers between devices, swap_grp(): return lax.ppermute(x, 'grp', [(0, 1), (1, 0)])  30.2 us
    pallas_call x1, Pallas kernels, shards(): pl.pallas_call(main_kernel, out_shape=[proj] * 2, in_specs=[ANYWHERE] * c...  8.46 us
    ppermute x5, starting transfers between devices, swap_grp(): return lax.ppermute(x, 'grp', [(0, 1), (1, 0)])  7.92 us
    ppermute x4, waiting for transfers between devices, shards(): lax.ppermute(value, 'blk', [(i, i ^ bit) for i in range(blk)])  7.66 us
    ppermute x4, starting transfers between devices, back_of(): return lax.ppermute(x, 'blk', backward)  6.02 us
    pallas_call x2, Pallas kernels, move(): pl.pallas_call(kernel, out_shape=shapes, in_specs=[ANYWHERE] * (count + l...  5.91 us
    ppermute x4, starting transfers between devices, shards(): lax.ppermute(value, 'blk', [(i, i ^ bit) for i in range(blk)])  5.08 us
  transfers between devices with their start and end apart: 22, of which 13 were waited for; matrix products, arithmetic and copies ran while one was open for 0% of the time, Pallas kernels for 13%

profile of v6, /device:TPU:0, one launch (start us, length us, event | category | flops | bytes accessed | tf_op | source)
XLA Modules:
  0.0 114.3 jit_solution(4932084682800789735)
XLA Ops:
  0.0 2.7 %shard_map.55 = (bf16[24,19712]{1,0:T(8,128)(2,1)}, bf16[128,3072]{1,0:T(8,128)(2,1)}) custom-call(bf16[2,128,8192]{2,1,0:T(8,128)(2,1)} %refs_16_.1, bf16[2,128,8192]{2,1,0:T(8,128)(2,1)} %refs_8_.1, bf16[2,24,8192]{2,1,0:T(8,128)(2,1)} %refs_2_.1, bf16[2,24,8192]{2,1,0:T(8,128)(2,1)} %refs_3_.1), custom_call_target="tpu_custom_call" | custom-call | bytes 6930432 | tf_op jit(solution)/shard_map/pallas_call | solution.py:63
  2.8 3.0 %collective-permute-start.8 = (bf16[128,3072]{1,0:T(8,128)(2,1)}, bf16[128,3072]{1,0:T(8,128)(2,1)S(1)}, u32[]{:S(2)}, u32[]{:S(2)}) collective-permute-start(bf16[128,3072]{1,0:T(8,128)(2,1)} %get-tuple-element.20), channel_id=1, source_target_pairs={{0,16},{16,0},{1,17},{17,1},{2,18},{18,2},{3,19},{19,3},{4,20},{20... | collective-permute-start | bytes 2359304 | tf_op jit(solution)/shard_map/ppermute | solution.py:151
  5.8 1.5 %collective-permute-start.1 = (bf16[24,19712]{1,0:T(8,128)(2,1)}, bf16[24,19712]{1,0:T(8,128)(2,1)S(1)}, u32[]{:S(2)}, u32[]{:S(2)}) collective-permute-start(bf16[24,19712]{1,0:T(8,128)(2,1)} %get-tuple-element.19.refs_2_.refs_0_), channel_id=1, source_target_pairs={{4,0},{8,4},{12,8},{14,12},{10,14},{6,10},{2,6},{0,2},{5,1},{9,5},... | collective-permute-start | bytes 2838536 | tf_op jit(solution)/shard_map/ppermute | solution.py:157
  7.3 0.5 collective-permute-start
  7.8 0.0 collective-permute-start.15
  7.8 3.2 %shard_map.56 = (bf16[128,3584]{1,0:T(8,128)(2,1)}, bf16[128,6400]{1,0:T(8,128)(2,1)}) custom-call(bf16[2,128,8192]{2,1,0:T(8,128)(2,1)} %refs_16_.1, bf16[2,128,8192]{2,1,0:T(8,128)(2,1)} %refs_8_.1, bf16[24,19712]{1,0:T(8,128)(2,1)} %get-tuple-element.19.refs_2_.refs_0_), custom_call_target="tpu_custom_call" | custom-call | bytes 10223616 | tf_op jit(solution)/shard_map/pallas_call | solution.py:63
  11.0 12.5 %collective-permute-done.8.refs_10_ = bf16[128,3072]{1,0:T(8,128)(2,1)S(1)} collective-permute-done((bf16[128,3072]{1,0:T(8,128)(2,1)}, bf16[128,3072]{1,0:T(8,128)(2,1)S(1)}, u32[]{:S(2)}, u32[]{:S(2)}) %collective-permute-start.8) | collective-permute-done | bytes 786464 | tf_op jit(solution)/shard_map/ppermute | solution.py:151
  23.5 0.0 copy-start.6
  23.5 1.7 %collective-permute-start.10 = (bf16[128,3584]{1,0:T(8,128)(2,1)}, bf16[128,3584]{1,0:T(8,128)(2,1)}, u32[]{:S(2)}, u32[]{:S(2)}) collective-permute-start(bf16[128,3584]{1,0:T(8,128)(2,1)} %get-tuple-element.22), channel_id=1, source_target_pairs={{0,16},{16,0},{1,17},{17,1},{2,18},{18,2},{3,19},{19,3},{4,20},{20... | collective-permute-start | bytes 2752520 | tf_op jit(solution)/shard_map/ppermute | solution.py:151
  25.3 0.0 collective-permute-start.7
  25.3 3.1 %collective-permute-done.1.refs_4_.refs_2_ = bf16[24,19712]{1,0:T(8,128)(2,1)S(1)} collective-permute-done((bf16[24,19712]{1,0:T(8,128)(2,1)}, bf16[24,19712]{1,0:T(8,128)(2,1)S(1)}, u32[]{:S(2)}, u32[]{:S(2)}) %collective-permute-start.1) | collective-permute-done | bytes 946208 | tf_op jit(solution)/shard_map/ppermute | solution.py:157
  28.4 0.0 copy-start.2
  28.4 1.5 %collective-permute-start.3 = (bf16[24,19712]{1,0:T(8,128)(2,1)S(1)}, bf16[24,19712]{1,0:T(8,128)(2,1)S(1)}, u32[]{:S(2)}, u32[]{:S(2)}) collective-permute-start(bf16[24,19712]{1,0:T(8,128)(2,1)S(1)} %collective-permute-done.1.refs_4_.refs_2_), channel_id=1, source_target_pairs={{4,0},{8,4},{12,8},{14,12},{10,14},{6,10},{2,6},{0,2},{5,1},{9,5},... | collective-permute-start | bytes 2838536 | tf_op jit(solution)/shard_map/ppermute | solution.py:157
  29.9 0.0 collective-permute-done.refs_3_.refs_1_
  29.9 0.0 copy-start.3
  29.9 0.5 collective-permute-start.2
  30.5 14.9 %collective-permute-done.10.refs_12_ = bf16[128,3584]{1,0:T(8,128)(2,1)} collective-permute-done((bf16[128,3584]{1,0:T(8,128)(2,1)}, bf16[128,3584]{1,0:T(8,128)(2,1)}, u32[]{:S(2)}, u32[]{:S(2)}) %collective-permute-start.10) | collective-permute-done | bytes 917536 | tf_op jit(solution)/shard_map/ppermute | solution.py:151
  45.4 1.4 %collective-permute-start.12 = (bf16[128,6400]{1,0:T(8,128)(2,1)}, bf16[128,6400]{1,0:T(8,128)(2,1)}, u32[]{:S(2)}, u32[]{:S(2)}) collective-permute-start(bf16[128,6400]{1,0:T(8,128)(2,1)} %get-tuple-element.24), channel_id=1, source_target_pairs={{0,16},{16,0},{1,17},{17,1},{2,18},{18,2},{3,19},{19,3},{4,20},{20... | collective-permute-start | bytes 4915208 | tf_op jit(solution)/shard_map/ppermute | solution.py:151
  46.8 0.0 copy-done.6
  46.8 3.1 %collective-permute-done.3.refs_6_.refs_4_ = bf16[24,19712]{1,0:T(8,128)(2,1)S(1)} collective-permute-done((bf16[24,19712]{1,0:T(8,128)(2,1)S(1)}, bf16[24,19712]{1,0:T(8,128)(2,1)S(1)}, u32[]{:S(2)}, u32[]{:S(2)}) %collective-permute-start.3) | collective-permute-done | bytes 946208 | tf_op jit(solution)/shard_map/ppermute | solution.py:157
  49.9 1.5 %collective-permute-start.5 = (bf16[24,19712]{1,0:T(8,128)(2,1)S(1)}, bf16[24,19712]{1,0:T(8,128)(2,1)S(1)}, u32[]{:S(2)}, u32[]{:S(2)}) collective-permute-start(bf16[24,19712]{1,0:T(8,128)(2,1)S(1)} %collective-permute-done.3.refs_6_.refs_4_), channel_id=1, source_target_pairs={{4,0},{8,4},{12,8},{14,12},{10,14},{6,10},{2,6},{0,2},{5,1},{9,5},... | collective-permute-start | bytes 2838536 | tf_op jit(solution)/shard_map/ppermute | solution.py:157
  51.4 0.0 collective-permute-done.2.refs_5_.refs_3_
  51.4 0.0 copy-done.4
  51.4 1.0 collective-permute-start.4
  52.5 18.4 %collective-permute-done.5.refs_8_.refs_6_ = bf16[24,19712]{1,0:T(8,128)(2,1)S(1)} collective-permute-done((bf16[24,19712]{1,0:T(8,128)(2,1)S(1)}, bf16[24,19712]{1,0:T(8,128)(2,1)S(1)}, u32[]{:S(2)}, u32[]{:S(2)}) %collective-permute-start.5) | collective-permute-done | bytes 946208 | tf_op jit(solution)/shard_map/ppermute | solution.py:157
  70.9 1.5 %collective-permute-start.13 = (bf16[24,9856]{1,0:T(8,128)(2,1)S(1)}, bf16[24,9856]{1,0:T(8,128)(2,1)S(1)}, u32[]{:S(2)}, u32[]{:S(2)}) collective-permute-start(bf16[24,9856]{1,0:T(8,128)(2,1)S(1)} %slice.13), channel_id=1, source_target_pairs={{4,0},{8,4},{12,8},{14,12},{10,14},{6,10},{2,6},{0,2},{5,1},{9,5},... | collective-permute-start | bytes 1419272 | tf_op jit(solution)/shard_map/ppermute | solution.py:157
  72.5 0.0 collective-permute-done.4.refs_7_.refs_5_
  72.5 0.0 copy-done.2
  72.5 0.0 copy-done.3
  72.5 0.0 copy-start.1
  72.5 1.0 collective-permute-start.6
  73.5 7.2 %collective-permute-done.13.refs_9_.refs_10_ = bf16[24,9856]{1,0:T(8,128)(2,1)S(1)} collective-permute-done((bf16[24,9856]{1,0:T(8,128)(2,1)S(1)}, bf16[24,9856]{1,0:T(8,128)(2,1)S(1)}, u32[]{:S(2)}, u32[]{:S(2)}) %collective-permute-start.13) | collective-permute-done | bytes 473120 | tf_op jit(solution)/shard_map/ppermute | solution.py:157
  80.7 1.3 %collective-permute-done.6.refs_7_ = bf16[24,9856]{1,0:T(8,128)(2,1)S(1)} collective-permute-done((bf16[24,9856]{1,0:T(8,128)(2,1)S(1)}, bf16[24,9856]{1,0:T(8,128)(2,1)S(1)}, u32[]{:S(2)}, u32[]{:S(2)}) %collective-permute-start.6) | collective-permute-done | bytes 473120 | tf_op jit(solution)/shard_map/ppermute | solution.py:154
  81.9 0.0 copy-done.1
  81.9 0.0 collective-permute-done.12.refs_14_
  81.9 0.0 copy-done.5
  81.9 0.1 collective-permute-start.14
  82.0 0.5 collective-permute-start.11
  82.5 0.1 collective-permute-start.9
  83.3 0.0 collective-permute-done.15.refs_1_.refs_17_
  83.3 0.0 copy-done
  83.3 3.5 %shard_map.57 = (f32[256,256]{1,0:T(8,128)S(1)}, f32[256,256]{1,0:T(8,128)S(1)}, bf16[24,3200]{1,0:T(8,128)(2,1)S(1)}) custom-call(bf16[2,128,8192]{2,1,0:T(8,128)(2,1)} %refs_16_.1, bf16[2,128,8192]{2,1,0:T(8,128)(2,1)} %collective-permute-done.15.refs_1_.refs_17_, bf16[24,19712]{1,0:T(8,128)(2,1)} %get-tuple-element.19.refs_2_.refs_0_, ...), custom_call_target="tpu_custom_call" | custom-call | flops 654311424 | bytes 10223616 | tf_op jit(solution)/shard_map/pallas_call | solution.py:273
  86.8 0.9 collective-permute-start.16
  87.7 0.6 collective-permute-done.9.refs_11_
  88.3 0.0 collective-permute-done.11.refs_13_
  88.3 0.0 collective-permute-done.7.refs_9_
  88.3 0.0 collective-permute-done.14.refs_15_
  88.3 8.5 %shard_map.58 = (f32[512,192]{1,0:T(8,128)S(1)}, f32[512,192]{1,0:T(8,128)S(1)}) custom-call(bf16[24,19712]{1,0:T(8,128)(2,1)} %get-tuple-element.19.refs_2_.refs_0_, bf16[24,19712]{1,0:T(8,128)(2,1)} %copy-done.3, bf16[24,19712]{1,0:T(8,128)(2,1)} %copy-done.2, bf16[24,19712]{1,0:T(8,128)(2,1)} %copy-done.5, bf16[24,19712]{1,0:T(8,128)(2,1)} %copy-done.4, ...), custom_call_target="tpu_custom_call" | custom-call | flops 2566914048 | bytes 40108032 | tf_op jit(solution)/shard_map/pallas_call | solution.py:317
  96.8 0.0 collective-permute-done.16.refs_3_
  96.8 0.5 shard_map.59
  97.3 0.9 collective-permute-start.17
  98.1 2.7 %collective-permute-done.17 = f32[1,128]{1,0:T(1,128)S(1)} collective-permute-done((f32[1,128]{1,0:T(1,128)S(1)}, f32[1,128]{1,0:T(1,128)S(1)}, u32[]{:S(2)}, u32[]{:S(2)}) %collective-permute-start.17) | collective-permute-done | bytes 544 | tf_op jit(solution)/shard_map/ppermute | solution.py:151
  100.8 0.1 fusion
  100.9 0.0 collective-permute-start.18
  100.9 1.1 collective-permute-done.18
  102.0 0.1 fusion.1
  102.1 1.6 %collective-permute-start.19 = (f32[2,1,128]{2,1,0:T(1,128)S(1)}, f32[2,1,128]{2,1,0:T(1,128)S(1)}, u32[]{:S(2)}, u32[]{:S(2)}) collective-permute-start(f32[2,1,128]{2,1,0:T(1,128)S(1)} %fusion.1), channel_id=1, source_target_pairs={{0,2},{1,3},{2,0},{3,1},{4,6},{5,7},{6,4},{7,5},{8,10},{9,11},{10,... | collective-permute-start | bytes 3080 | tf_op jit(solution)/shard_map/ppermute | solution.py:377
  103.7 2.0 %collective-permute-done.19 = f32[2,1,128]{2,1,0:T(1,128)S(1)} collective-permute-done((f32[2,1,128]{2,1,0:T(1,128)S(1)}, f32[2,1,128]{2,1,0:T(1,128)S(1)}, u32[]{:S(2)}, u32[]{:S(2)}) %collective-permute-start.19) | collective-permute-done | bytes 1056 | tf_op jit(solution)/shard_map/ppermute | solution.py:377
  105.7 0.1 fusion.2
  105.7 1.2 %collective-permute-start.20 = (f32[2,1,128]{2,1,0:T(1,128)S(1)}, f32[2,1,128]{2,1,0:T(1,128)S(1)}, u32[]{:S(2)}, u32[]{:S(2)}) collective-permute-start(f32[2,1,128]{2,1,0:T(1,128)S(1)} %fusion.2), channel_id=1, source_target_pairs={{0,4},{1,5},{2,6},{3,7},{4,0},{5,1},{6,2},{7,3},{8,12},{9,13},{10,... | collective-permute-start | bytes 3080 | tf_op jit(solution)/shard_map/ppermute | solution.py:377
  107.0 2.3 %collective-permute-done.20 = f32[2,1,128]{2,1,0:T(1,128)S(1)} collective-permute-done((f32[2,1,128]{2,1,0:T(1,128)S(1)}, f32[2,1,128]{2,1,0:T(1,128)S(1)}, u32[]{:S(2)}, u32[]{:S(2)}) %collective-permute-start.20) | collective-permute-done | bytes 1056 | tf_op jit(solution)/shard_map/ppermute | solution.py:377
  109.3 2.3 %collective-permute-start.21 = (f32[2,1,128]{2,1,0:T(1,128)S(1)}, f32[2,1,128]{2,1,0:T(1,128)S(1)}, u32[]{:S(2)}, u32[]{:S(2)}) collective-permute-start(f32[2,1,128]{2,1,0:T(1,128)S(1)} %add.16), channel_id=1, source_target_pairs={{0,8},{1,9},{2,10},{3,11},{4,12},{5,13},{6,14},{7,15},{8,0},{9,1},... | collective-permute-start | bytes 3080 | tf_op jit(solution)/shard_map/ppermute | solution.py:377
  111.6 2.2 %collective-permute-done.21 = f32[2,1,128]{2,1,0:T(1,128)S(1)} collective-permute-done((f32[2,1,128]{2,1,0:T(1,128)S(1)}, f32[2,1,128]{2,1,0:T(1,128)S(1)}, u32[]{:S(2)}, u32[]{:S(2)}) %collective-permute-start.21) | collective-permute-done | bytes 1056 | tf_op jit(solution)/shard_map/ppermute | solution.py:377
  113.8 0.6 slice_add_fusion
  (7 shorter events, 0.1 us)
Async XLA Ops:
  2.8 20.8 %collective-permute-start.8 = (bf16[128,3072]{1,0:T(8,128)(2,1)}, bf16[128,3072]{1,0:T(8,128)(2,1)S(1)}, u32[]{:S(2)}, u32[]{:S(2)}) collective-permute-start(bf16[128,3072]{1,0:T(8,128)(2,1)} %get-tuple-element.20), channel_id=1, source_target_pairs={{0,16},{16,0},{1,17},{17,1},{2,18},{18,2},{3,19},{19,3},{4,20},{20... | collective-permute-start | bytes 2359304 | tf_op jit(solution)/shard_map/ppermute | solution.py:151
  5.8 22.6 %collective-permute-start.1 = (bf16[24,19712]{1,0:T(8,128)(2,1)}, bf16[24,19712]{1,0:T(8,128)(2,1)S(1)}, u32[]{:S(2)}, u32[]{:S(2)}) collective-permute-start(bf16[24,19712]{1,0:T(8,128)(2,1)} %get-tuple-element.19.refs_2_.refs_0_), channel_id=1, source_target_pairs={{4,0},{8,4},{12,8},{14,12},{10,14},{6,10},{2,6},{0,2},{5,1},{9,5},... | collective-permute-start | bytes 2838536 | tf_op jit(solution)/shard_map/ppermute | solution.py:157
  7.3 22.6 %collective-permute-start = (bf16[24,19712]{1,0:T(8,128)(2,1)}, bf16[24,19712]{1,0:T(8,128)(2,1)S(1)}, u32[]{:S(2)}, u32[]{:S(2)}) collective-permute-start(bf16[24,19712]{1,0:T(8,128)(2,1)} %get-tuple-element.19.refs_2_.refs_0_), channel_id=1, source_target_pairs={{0,4},{4,8},{8,12},{12,14},{14,10},{10,6},{6,2},{2,0},{1,5},{5,9},... | collective-permute-start | bytes 2838536 | tf_op jit(solution)/shard_map/ppermute | solution.py:154
  7.8 75.5 %collective-permute-start.15 = (bf16[2,128,8192]{2,1,0:T(8,128)(2,1)}, bf16[2,128,8192]{2,1,0:T(8,128)(2,1)}, u32[]{:S(2)}, u32[]{:S(2)}) collective-permute-start(bf16[2,128,8192]{2,1,0:T(8,128)(2,1)} %refs_16_.1), channel_id=1, source_target_pairs={{0,1},{1,0},{2,3},{3,2},{4,5},{5,4},{6,7},{7,6},{8,9},{9,8},{10,11... | collective-permute-start | bytes 12582920 | tf_op jit(solution)/shard_map/ppermute | solution.py:148
  23.5 23.3 %copy-start.6 = (bf16[128,3072]{1,0:T(8,128)(2,1)}, bf16[128,3072]{1,0:T(8,128)(2,1)S(1)}, u32[]{:S(2)}) copy-start(bf16[128,3072]{1,0:T(8,128)(2,1)S(1)} %collective-permute-done.8.refs_10_) | copy-start | bytes 2359300
  23.5 21.9 %collective-permute-start.10 = (bf16[128,3584]{1,0:T(8,128)(2,1)}, bf16[128,3584]{1,0:T(8,128)(2,1)}, u32[]{:S(2)}, u32[]{:S(2)}) collective-permute-start(bf16[128,3584]{1,0:T(8,128)(2,1)} %get-tuple-element.22), channel_id=1, source_target_pairs={{0,16},{16,0},{1,17},{17,1},{2,18},{18,2},{3,19},{19,3},{4,20},{20... | collective-permute-start | bytes 2752520 | tf_op jit(solution)/shard_map/ppermute | solution.py:151
  25.3 63.0 %collective-permute-start.7 = (bf16[2,128,8192]{2,1,0:T(8,128)(2,1)}, bf16[2,128,8192]{2,1,0:T(8,128)(2,1)}, u32[]{:S(2)}, u32[]{:S(2)}) collective-permute-start(bf16[2,128,8192]{2,1,0:T(8,128)(2,1)} %refs_8_.1), channel_id=1, source_target_pairs={{0,1},{1,0},{2,3},{3,2},{4,5},{5,4},{6,7},{7,6},{8,9},{9,8},{10,11... | collective-permute-start | bytes 12582920 | tf_op jit(solution)/shard_map/ppermute | solution.py:148
  28.4 44.0 %copy-start.2 = (bf16[24,19712]{1,0:T(8,128)(2,1)}, bf16[24,19712]{1,0:T(8,128)(2,1)S(1)}, u32[]{:S(2)}) copy-start(bf16[24,19712]{1,0:T(8,128)(2,1)S(1)} %collective-permute-done.1.refs_4_.refs_2_) | copy-start | bytes 2838532
  28.4 21.5 %collective-permute-start.3 = (bf16[24,19712]{1,0:T(8,128)(2,1)S(1)}, bf16[24,19712]{1,0:T(8,128)(2,1)S(1)}, u32[]{:S(2)}, u32[]{:S(2)}) collective-permute-start(bf16[24,19712]{1,0:T(8,128)(2,1)S(1)} %collective-permute-done.1.refs_4_.refs_2_), channel_id=1, source_target_pairs={{4,0},{8,4},{12,8},{14,12},{10,14},{6,10},{2,6},{0,2},{5,1},{9,5},... | collective-permute-start | bytes 2838536 | tf_op jit(solution)/shard_map/ppermute | solution.py:157
  29.9 42.5 %copy-start.3 = (bf16[24,19712]{1,0:T(8,128)(2,1)}, bf16[24,19712]{1,0:T(8,128)(2,1)S(1)}, u32[]{:S(2)}) copy-start(bf16[24,19712]{1,0:T(8,128)(2,1)S(1)} %collective-permute-done.refs_3_.refs_1_) | copy-start | bytes 2838532
  29.9 21.5 %collective-permute-start.2 = (bf16[24,19712]{1,0:T(8,128)(2,1)S(1)}, bf16[24,19712]{1,0:T(8,128)(2,1)S(1)}, u32[]{:S(2)}, u32[]{:S(2)}) collective-permute-start(bf16[24,19712]{1,0:T(8,128)(2,1)S(1)} %collective-permute-done.refs_3_.refs_1_), channel_id=1, source_target_pairs={{0,4},{4,8},{8,12},{12,14},{14,10},{10,6},{6,2},{2,0},{1,5},{5,9},... | collective-permute-start | bytes 2838536 | tf_op jit(solution)/shard_map/ppermute | solution.py:154
  45.4 36.6 %collective-permute-start.12 = (bf16[128,6400]{1,0:T(8,128)(2,1)}, bf16[128,6400]{1,0:T(8,128)(2,1)}, u32[]{:S(2)}, u32[]{:S(2)}) collective-permute-start(bf16[128,6400]{1,0:T(8,128)(2,1)} %get-tuple-element.24), channel_id=1, source_target_pairs={{0,16},{16,0},{1,17},{17,1},{2,18},{18,2},{3,19},{19,3},{4,20},{20... | collective-permute-start | bytes 4915208 | tf_op jit(solution)/shard_map/ppermute | solution.py:151
  49.9 1.5 %copy-start.4 = (bf16[24,19712]{1,0:T(8,128)(2,1)}, bf16[24,19712]{1,0:T(8,128)(2,1)S(1)}, u32[]{:S(2)}) copy-start(bf16[24,19712]{1,0:T(8,128)(2,1)S(1)} %collective-permute-done.3.refs_6_.refs_4_) | copy-start | bytes 2838532
  49.9 20.9 %collective-permute-start.5 = (bf16[24,19712]{1,0:T(8,128)(2,1)S(1)}, bf16[24,19712]{1,0:T(8,128)(2,1)S(1)}, u32[]{:S(2)}, u32[]{:S(2)}) collective-permute-start(bf16[24,19712]{1,0:T(8,128)(2,1)S(1)} %collective-permute-done.3.refs_6_.refs_4_), channel_id=1, source_target_pairs={{4,0},{8,4},{12,8},{14,12},{10,14},{6,10},{2,6},{0,2},{5,1},{9,5},... | collective-permute-start | bytes 2838536 | tf_op jit(solution)/shard_map/ppermute | solution.py:157
  51.4 30.5 %copy-start.5 = (bf16[24,19712]{1,0:T(8,128)(2,1)}, bf16[24,19712]{1,0:T(8,128)(2,1)S(1)}, u32[]{:S(2)}) copy-start(bf16[24,19712]{1,0:T(8,128)(2,1)S(1)} %collective-permute-done.2.refs_5_.refs_3_) | copy-start | bytes 2838532
  51.4 21.0 %collective-permute-start.4 = (bf16[24,19712]{1,0:T(8,128)(2,1)S(1)}, bf16[24,19712]{1,0:T(8,128)(2,1)S(1)}, u32[]{:S(2)}, u32[]{:S(2)}) collective-permute-start(bf16[24,19712]{1,0:T(8,128)(2,1)S(1)} %collective-permute-done.2.refs_5_.refs_3_), channel_id=1, source_target_pairs={{0,4},{4,8},{8,12},{12,14},{14,10},{10,6},{6,2},{2,0},{1,5},{5,9},... | collective-permute-start | bytes 2838536 | tf_op jit(solution)/shard_map/ppermute | solution.py:154
  70.9 12.4 %copy-start = (bf16[24,19712]{1,0:T(8,128)(2,1)}, bf16[24,19712]{1,0:T(8,128)(2,1)S(1)}, u32[]{:S(2)}) copy-start(bf16[24,19712]{1,0:T(8,128)(2,1)S(1)} %collective-permute-done.5.refs_8_.refs_6_) | copy-start | bytes 2838532
  70.9 9.8 %collective-permute-start.13 = (bf16[24,9856]{1,0:T(8,128)(2,1)S(1)}, bf16[24,9856]{1,0:T(8,128)(2,1)S(1)}, u32[]{:S(2)}, u32[]{:S(2)}) collective-permute-start(bf16[24,9856]{1,0:T(8,128)(2,1)S(1)} %slice.13), channel_id=1, source_target_pairs={{4,0},{8,4},{12,8},{14,12},{10,14},{6,10},{2,6},{0,2},{5,1},{9,5},... | collective-permute-start | bytes 1419272 | tf_op jit(solution)/shard_map/ppermute | solution.py:157
  72.5 9.5 %copy-start.1 = (bf16[24,19712]{1,0:T(8,128)(2,1)}, bf16[24,19712]{1,0:T(8,128)(2,1)S(1)}, u32[]{:S(2)}) copy-start(bf16[24,19712]{1,0:T(8,128)(2,1)S(1)} %collective-permute-done.4.refs_7_.refs_5_) | copy-start | bytes 2838532
  72.5 9.4 %collective-permute-start.6 = (bf16[24,9856]{1,0:T(8,128)(2,1)S(1)}, bf16[24,9856]{1,0:T(8,128)(2,1)S(1)}, u32[]{:S(2)}, u32[]{:S(2)}) collective-permute-start(bf16[24,9856]{1,0:T(8,128)(2,1)S(1)} %slice.12), channel_id=1, source_target_pairs={{0,4},{4,8},{8,12},{12,14},{14,10},{10,6},{6,2},{2,0},{1,5},{5,9},... | collective-permute-start | bytes 1419272 | tf_op jit(solution)/shard_map/ppermute | solution.py:154
  81.9 6.4 %collective-permute-start.14 = (bf16[128,6400]{1,0:T(8,128)(2,1)}, bf16[128,6400]{1,0:T(8,128)(2,1)}, u32[]{:S(2)}, u32[]{:S(2)}) collective-permute-start(bf16[128,6400]{1,0:T(8,128)(2,1)} %collective-permute-done.12.refs_14_), channel_id=1, source_target_pairs={{0,1},{1,0},{2,3},{3,2},{4,5},{5,4},{6,7},{7,6},{8,9},{9,8},{10,11... | collective-permute-start | bytes 4915208 | tf_op jit(solution)/shard_map/ppermute | solution.py:148
  82.0 6.3 %collective-permute-start.11 = (bf16[128,3584]{1,0:T(8,128)(2,1)}, bf16[128,3584]{1,0:T(8,128)(2,1)}, u32[]{:S(2)}, u32[]{:S(2)}) collective-permute-start(bf16[128,3584]{1,0:T(8,128)(2,1)} %collective-permute-done.10.refs_12_), channel_id=1, source_target_pairs={{0,1},{1,0},{2,3},{3,2},{4,5},{5,4},{6,7},{7,6},{8,9},{9,8},{10,11... | collective-permute-start | bytes 2752520 | tf_op jit(solution)/shard_map/ppermute | solution.py:148
  82.5 5.8 %collective-permute-start.9 = (bf16[128,3072]{1,0:T(8,128)(2,1)}, bf16[128,3072]{1,0:T(8,128)(2,1)}, u32[]{:S(2)}, u32[]{:S(2)}) collective-permute-start(bf16[128,3072]{1,0:T(8,128)(2,1)} %copy-done.6), channel_id=1, source_target_pairs={{0,1},{1,0},{2,3},{3,2},{4,5},{5,4},{6,7},{7,6},{8,9},{9,8},{10,11... | collective-permute-start | bytes 2359304 | tf_op jit(solution)/shard_map/ppermute | solution.py:148
  86.8 10.0 %collective-permute-start.16 = (f32[256,256]{1,0:T(8,128)S(1)}, f32[256,256]{1,0:T(8,128)S(1)}, u32[]{:S(2)}, u32[]{:S(2)}) collective-permute-start(f32[256,256]{1,0:T(8,128)S(1)} %get-tuple-element.30), channel_id=1, source_target_pairs={{0,16},{16,0},{1,17},{17,1},{2,18},{18,2},{3,19},{19,3},{4,20},{20... | collective-permute-start | bytes 786440 | tf_op jit(solution)/shard_map/ppermute | solution.py:151
  97.3 3.5 %collective-permute-start.17 = (f32[1,128]{1,0:T(1,128)S(1)}, f32[1,128]{1,0:T(1,128)S(1)}, u32[]{:S(2)}, u32[]{:S(2)}) collective-permute-start(f32[1,128]{1,0:T(1,128)S(1)} %get-tuple-element.32), channel_id=1, source_target_pairs={{0,16},{16,0},{1,17},{17,1},{2,18},{18,2},{3,19},{19,3},{4,20},{20... | collective-permute-start | bytes 1544 | tf_op jit(solution)/shard_map/ppermute | solution.py:151
  100.9 1.1 collective-permute-start.18
  102.1 3.6 %collective-permute-start.19 = (f32[2,1,128]{2,1,0:T(1,128)S(1)}, f32[2,1,128]{2,1,0:T(1,128)S(1)}, u32[]{:S(2)}, u32[]{:S(2)}) collective-permute-start(f32[2,1,128]{2,1,0:T(1,128)S(1)} %fusion.1), channel_id=1, source_target_pairs={{0,2},{1,3},{2,0},{3,1},{4,6},{5,7},{6,4},{7,5},{8,10},{9,11},{10,... | collective-permute-start | bytes 3080 | tf_op jit(solution)/shard_map/ppermute | solution.py:377
  105.7 3.6 %collective-permute-start.20 = (f32[2,1,128]{2,1,0:T(1,128)S(1)}, f32[2,1,128]{2,1,0:T(1,128)S(1)}, u32[]{:S(2)}, u32[]{:S(2)}) collective-permute-start(f32[2,1,128]{2,1,0:T(1,128)S(1)} %fusion.2), channel_id=1, source_target_pairs={{0,4},{1,5},{2,6},{3,7},{4,0},{5,1},{6,2},{7,3},{8,12},{9,13},{10,... | collective-permute-start | bytes 3080 | tf_op jit(solution)/shard_map/ppermute | solution.py:377
  109.3 4.5 %collective-permute-start.21 = (f32[2,1,128]{2,1,0:T(1,128)S(1)}, f32[2,1,128]{2,1,0:T(1,128)S(1)}, u32[]{:S(2)}, u32[]{:S(2)}) collective-permute-start(f32[2,1,128]{2,1,0:T(1,128)S(1)} %add.16), channel_id=1, source_target_pairs={{0,8},{1,9},{2,10},{3,11},{4,12},{5,13},{6,14},{7,15},{8,0},{9,1},... | collective-permute-start | bytes 3080 | tf_op jit(solution)/shard_map/ppermute | solution.py:377

commit v7 on v6

--- a/solution.py
+++ b/solution.py
@@ -179,7 +179,7 @@
                 ranges.append((in_source, layer, max(start - width, 0), stop - width))
             return ranges
 
-        edges = [0, width * 6 // 16, width * 13 // 16, packed]
+        edges = [0, width * 6 // 16, width * 12 // 16, packed]
 
         def away_part(k):
             return packing(1, 0, "other", edges[k], edges[k + 1])

time: 115 us -> 114 us (level)
    ppermute x4, waiting for transfers between devices: 31.9 us -> 34.8 us  [back_of(): return lax.ppermute(x, 'blk', backward)]
    ppermute x5, waiting for transfers between devices: 30.2 us -> 27.5 us  [swap_grp(): return lax.ppermute(x, 'grp', [(0, 1), (1, 0)])]
where the time goes in v7:
time: 114 us
  waiting for transfers between devices  71.9 us (63%)
  starting transfers between devices  22.5 us (20%)
  Pallas kernels  17.9 us (16%)
    ppermute x4, waiting for transfers between devices, back_of(): return lax.ppermute(x, 'blk', backward)  34.8 us
    ppermute x5, waiting for transfers between devices, swap_grp(): return lax.ppermute(x, 'grp', [(0, 1), (1, 0)])  27.5 us
    pallas_call x1, Pallas kernels, shards(): pl.pallas_call(main_kernel, out_shape=[proj] * 2, in_specs=[ANYWHERE] * c...  8.04 us
    ppermute x5, starting transfers between devices, swap_grp(): return lax.ppermute(x, 'grp', [(0, 1), (1, 0)])  7.71 us
    ppermute x4, waiting for transfers between devices, shards(): lax.ppermute(value, 'blk', [(i, i ^ bit) for i in range(blk)])  7.66 us
    ppermute x4, starting transfers between devices, back_of(): return lax.ppermute(x, 'blk', backward)  6.02 us
    pallas_call x2, Pallas kernels, move(): pl.pallas_call(kernel, out_shape=shapes, in_specs=[ANYWHERE] * (count + l...  5.87 us
    ppermute x4, starting transfers between devices, shards(): lax.ppermute(value, 'blk', [(i, i ^ bit) for i in range(blk)])  5.08 us
  transfers between devices with their start and end apart: 22, of which 13 were waited for; matrix products, arithmetic and copies ran while one was open for 0% of the time, Pallas kernels for 13%

profile of v7, /device:TPU:0, one launch (start us, length us, event | category | flops | bytes accessed | tf_op | source)
XLA Modules:
  0.0 114.0 jit_solution(5532273690111573123)
XLA Ops:
  0.0 2.7 %shard_map.55 = (bf16[24,19712]{1,0:T(8,128)(2,1)}, bf16[128,3072]{1,0:T(8,128)(2,1)}) custom-call(bf16[2,128,8192]{2,1,0:T(8,128)(2,1)} %refs_16_.1, bf16[2,128,8192]{2,1,0:T(8,128)(2,1)} %refs_8_.1, bf16[2,24,8192]{2,1,0:T(8,128)(2,1)} %refs_2_.1, bf16[2,24,8192]{2,1,0:T(8,128)(2,1)} %refs_3_.1), custom_call_target="tpu_custom_call" | custom-call | bytes 6930432 | tf_op jit(solution)/shard_map/pallas_call | solution.py:63
  2.7 3.0 %collective-permute-start.8 = (bf16[128,3072]{1,0:T(8,128)(2,1)}, bf16[128,3072]{1,0:T(8,128)(2,1)S(1)}, u32[]{:S(2)}, u32[]{:S(2)}) collective-permute-start(bf16[128,3072]{1,0:T(8,128)(2,1)} %get-tuple-element.20), channel_id=1, source_target_pairs={{0,16},{16,0},{1,17},{17,1},{2,18},{18,2},{3,19},{19,3},{4,20},{20... | collective-permute-start | bytes 2359304 | tf_op jit(solution)/shard_map/ppermute | solution.py:151
  5.8 1.5 %collective-permute-start.1 = (bf16[24,19712]{1,0:T(8,128)(2,1)}, bf16[24,19712]{1,0:T(8,128)(2,1)S(1)}, u32[]{:S(2)}, u32[]{:S(2)}) collective-permute-start(bf16[24,19712]{1,0:T(8,128)(2,1)} %get-tuple-element.19.refs_2_.refs_0_), channel_id=1, source_target_pairs={{4,0},{8,4},{12,8},{14,12},{10,14},{6,10},{2,6},{0,2},{5,1},{9,5},... | collective-permute-start | bytes 2838536 | tf_op jit(solution)/shard_map/ppermute | solution.py:157
  7.3 0.5 collective-permute-start
  7.8 0.0 collective-permute-start.15
  7.8 3.1 %shard_map.56 = (bf16[128,3072]{1,0:T(8,128)(2,1)}, bf16[128,6912]{1,0:T(8,128)(2,1)}) custom-call(bf16[2,128,8192]{2,1,0:T(8,128)(2,1)} %refs_16_.1, bf16[2,128,8192]{2,1,0:T(8,128)(2,1)} %refs_8_.1, bf16[24,19712]{1,0:T(8,128)(2,1)} %get-tuple-element.19.refs_2_.refs_0_), custom_call_target="tpu_custom_call" | custom-call | bytes 10223616 | tf_op jit(solution)/shard_map/pallas_call | solution.py:63
  11.0 12.6 %collective-permute-done.8.refs_10_ = bf16[128,3072]{1,0:T(8,128)(2,1)S(1)} collective-permute-done((bf16[128,3072]{1,0:T(8,128)(2,1)}, bf16[128,3072]{1,0:T(8,128)(2,1)S(1)}, u32[]{:S(2)}, u32[]{:S(2)}) %collective-permute-start.8) | collective-permute-done | bytes 786464 | tf_op jit(solution)/shard_map/ppermute | solution.py:151
  23.5 0.0 copy-start.6
  23.5 1.7 %collective-permute-start.10 = (bf16[128,3072]{1,0:T(8,128)(2,1)}, bf16[128,3072]{1,0:T(8,128)(2,1)}, u32[]{:S(2)}, u32[]{:S(2)}) collective-permute-start(bf16[128,3072]{1,0:T(8,128)(2,1)} %get-tuple-element.22), channel_id=1, source_target_pairs={{0,16},{16,0},{1,17},{17,1},{2,18},{18,2},{3,19},{19,3},{4,20},{20... | collective-permute-start | bytes 2359304 | tf_op jit(solution)/shard_map/ppermute | solution.py:151
  25.3 0.0 collective-permute-start.7
  25.3 3.1 %collective-permute-done.1.refs_4_.refs_2_ = bf16[24,19712]{1,0:T(8,128)(2,1)S(1)} collective-permute-done((bf16[24,19712]{1,0:T(8,128)(2,1)}, bf16[24,19712]{1,0:T(8,128)(2,1)S(1)}, u32[]{:S(2)}, u32[]{:S(2)}) %collective-permute-start.1) | collective-permute-done | bytes 946208 | tf_op jit(solution)/shard_map/ppermute | solution.py:157
  28.4 0.0 copy-start.2
  28.4 1.5 %collective-permute-start.3 = (bf16[24,19712]{1,0:T(8,128)(2,1)S(1)}, bf16[24,19712]{1,0:T(8,128)(2,1)S(1)}, u32[]{:S(2)}, u32[]{:S(2)}) collective-permute-start(bf16[24,19712]{1,0:T(8,128)(2,1)S(1)} %collective-permute-done.1.refs_4_.refs_2_), channel_id=1, source_target_pairs={{4,0},{8,4},{12,8},{14,12},{10,14},{6,10},{2,6},{0,2},{5,1},{9,5},... | collective-permute-start | bytes 2838536 | tf_op jit(solution)/shard_map/ppermute | solution.py:157
  29.9 0.0 collective-permute-done.refs_3_.refs_1_
  29.9 0.0 copy-start.3
  29.9 0.5 collective-permute-start.2
  30.4 12.1 %collective-permute-done.10.refs_12_ = bf16[128,3072]{1,0:T(8,128)(2,1)} collective-permute-done((bf16[128,3072]{1,0:T(8,128)(2,1)}, bf16[128,3072]{1,0:T(8,128)(2,1)}, u32[]{:S(2)}, u32[]{:S(2)}) %collective-permute-start.10) | collective-permute-done | bytes 786464 | tf_op jit(solution)/shard_map/ppermute | solution.py:151
  42.6 1.4 %collective-permute-start.12 = (bf16[128,6912]{1,0:T(8,128)(2,1)}, bf16[128,6912]{1,0:T(8,128)(2,1)}, u32[]{:S(2)}, u32[]{:S(2)}) collective-permute-start(bf16[128,6912]{1,0:T(8,128)(2,1)} %get-tuple-element.24), channel_id=1, source_target_pairs={{0,16},{16,0},{1,17},{17,1},{2,18},{18,2},{3,19},{19,3},{4,20},{20... | collective-permute-start | bytes 5308424 | tf_op jit(solution)/shard_map/ppermute | solution.py:151
  44.0 0.0 copy-done.6
  44.0 5.9 %collective-permute-done.3.refs_6_.refs_4_ = bf16[24,19712]{1,0:T(8,128)(2,1)S(1)} collective-permute-done((bf16[24,19712]{1,0:T(8,128)(2,1)S(1)}, bf16[24,19712]{1,0:T(8,128)(2,1)S(1)}, u32[]{:S(2)}, u32[]{:S(2)}) %collective-permute-start.3) | collective-permute-done | bytes 946208 | tf_op jit(solution)/shard_map/ppermute | solution.py:157
  49.9 1.5 %collective-permute-start.5 = (bf16[24,19712]{1,0:T(8,128)(2,1)S(1)}, bf16[24,19712]{1,0:T(8,128)(2,1)S(1)}, u32[]{:S(2)}, u32[]{:S(2)}) collective-permute-start(bf16[24,19712]{1,0:T(8,128)(2,1)S(1)} %collective-permute-done.3.refs_6_.refs_4_), channel_id=1, source_target_pairs={{4,0},{8,4},{12,8},{14,12},{10,14},{6,10},{2,6},{0,2},{5,1},{9,5},... | collective-permute-start | bytes 2838536 | tf_op jit(solution)/shard_map/ppermute | solution.py:157
  51.4 0.0 collective-permute-done.2.refs_5_.refs_3_
  51.4 0.0 copy-done.4
  51.4 1.0 collective-permute-start.4
  52.4 18.4 %collective-permute-done.5.refs_8_.refs_6_ = bf16[24,19712]{1,0:T(8,128)(2,1)S(1)} collective-permute-done((bf16[24,19712]{1,0:T(8,128)(2,1)S(1)}, bf16[24,19712]{1,0:T(8,128)(2,1)S(1)}, u32[]{:S(2)}, u32[]{:S(2)}) %collective-permute-start.5) | collective-permute-done | bytes 946208 | tf_op jit(solution)/shard_map/ppermute | solution.py:157
  70.9 1.5 %collective-permute-start.13 = (bf16[24,9856]{1,0:T(8,128)(2,1)S(1)}, bf16[24,9856]{1,0:T(8,128)(2,1)S(1)}, u32[]{:S(2)}, u32[]{:S(2)}) collective-permute-start(bf16[24,9856]{1,0:T(8,128)(2,1)S(1)} %slice.13), channel_id=1, source_target_pairs={{4,0},{8,4},{12,8},{14,12},{10,14},{6,10},{2,6},{0,2},{5,1},{9,5},... | collective-permute-start | bytes 1419272 | tf_op jit(solution)/shard_map/ppermute | solution.py:157
  72.4 0.0 collective-permute-done.4.refs_7_.refs_5_
  72.4 0.0 copy-done.2
  72.4 0.0 copy-done.3
  72.4 0.0 copy-start.1
  72.5 1.0 collective-permute-start.6
  73.5 7.3 %collective-permute-done.13.refs_9_.refs_10_ = bf16[24,9856]{1,0:T(8,128)(2,1)S(1)} collective-permute-done((bf16[24,9856]{1,0:T(8,128)(2,1)S(1)}, bf16[24,9856]{1,0:T(8,128)(2,1)S(1)}, u32[]{:S(2)}, u32[]{:S(2)}) %collective-permute-start.13) | collective-permute-done | bytes 473120 | tf_op jit(solution)/shard_map/ppermute | solution.py:157
  80.8 1.3 %collective-permute-done.6.refs_7_ = bf16[24,9856]{1,0:T(8,128)(2,1)S(1)} collective-permute-done((bf16[24,9856]{1,0:T(8,128)(2,1)S(1)}, bf16[24,9856]{1,0:T(8,128)(2,1)S(1)}, u32[]{:S(2)}, u32[]{:S(2)}) %collective-permute-start.6) | collective-permute-done | bytes 473120 | tf_op jit(solution)/shard_map/ppermute | solution.py:154
  82.0 0.0 copy-done.1
  82.0 0.0 collective-permute-done.12.refs_14_
  82.0 0.0 copy-done.5
  82.0 0.1 collective-permute-start.14
  82.1 0.5 collective-permute-start.9
  82.6 0.1 collective-permute-start.11
  83.3 0.0 collective-permute-done.15.refs_1_.refs_17_
  83.4 0.0 copy-done
  83.4 3.5 %shard_map.57 = (f32[256,256]{1,0:T(8,128)S(1)}, f32[256,256]{1,0:T(8,128)S(1)}, bf16[24,3200]{1,0:T(8,128)(2,1)S(1)}) custom-call(bf16[2,128,8192]{2,1,0:T(8,128)(2,1)} %refs_16_.1, bf16[2,128,8192]{2,1,0:T(8,128)(2,1)} %collective-permute-done.15.refs_1_.refs_17_, bf16[24,19712]{1,0:T(8,128)(2,1)} %get-tuple-element.19.refs_2_.refs_0_, ...), custom_call_target="tpu_custom_call" | custom-call | flops 654311424 | bytes 10223616 | tf_op jit(solution)/shard_map/pallas_call | solution.py:273
  86.9 0.7 collective-permute-start.16
  87.6 0.0 collective-permute-done.9.refs_11_
  87.6 0.7 collective-permute-done.11.refs_13_
  88.4 0.0 collective-permute-done.7.refs_9_
  88.4 0.0 collective-permute-done.14.refs_15_
  88.4 8.0 %shard_map.58 = (f32[512,192]{1,0:T(8,128)S(1)}, f32[512,192]{1,0:T(8,128)S(1)}) custom-call(bf16[24,19712]{1,0:T(8,128)(2,1)} %get-tuple-element.19.refs_2_.refs_0_, bf16[24,19712]{1,0:T(8,128)(2,1)} %copy-done.3, bf16[24,19712]{1,0:T(8,128)(2,1)} %copy-done.2, bf16[24,19712]{1,0:T(8,128)(2,1)} %copy-done.5, bf16[24,19712]{1,0:T(8,128)(2,1)} %copy-done.4, ...), custom_call_target="tpu_custom_call" | custom-call | flops 2566914048 | bytes 40108032 | tf_op jit(solution)/shard_map/pallas_call | solution.py:317
  96.4 0.0 collective-permute-done.16.refs_3_
  96.4 0.5 shard_map.59
  96.9 0.8 collective-permute-start.17
  97.7 2.8 %collective-permute-done.17 = f32[1,128]{1,0:T(1,128)S(1)} collective-permute-done((f32[1,128]{1,0:T(1,128)S(1)}, f32[1,128]{1,0:T(1,128)S(1)}, u32[]{:S(2)}, u32[]{:S(2)}) %collective-permute-start.17) | collective-permute-done | bytes 544 | tf_op jit(solution)/shard_map/ppermute | solution.py:151
  100.5 0.1 fusion
  100.5 0.0 collective-permute-start.18
  100.5 1.1 collective-permute-done.18
  101.7 0.1 fusion.1
  101.8 1.6 %collective-permute-start.19 = (f32[2,1,128]{2,1,0:T(1,128)S(1)}, f32[2,1,128]{2,1,0:T(1,128)S(1)}, u32[]{:S(2)}, u32[]{:S(2)}) collective-permute-start(f32[2,1,128]{2,1,0:T(1,128)S(1)} %fusion.1), channel_id=1, source_target_pairs={{0,2},{1,3},{2,0},{3,1},{4,6},{5,7},{6,4},{7,5},{8,10},{9,11},{10,... | collective-permute-start | bytes 3080 | tf_op jit(solution)/shard_map/ppermute | solution.py:377
  103.3 2.0 %collective-permute-done.19 = f32[2,1,128]{2,1,0:T(1,128)S(1)} collective-permute-done((f32[2,1,128]{2,1,0:T(1,128)S(1)}, f32[2,1,128]{2,1,0:T(1,128)S(1)}, u32[]{:S(2)}, u32[]{:S(2)}) %collective-permute-start.19) | collective-permute-done | bytes 1056 | tf_op jit(solution)/shard_map/ppermute | solution.py:377
  105.3 0.1 fusion.2
  105.4 1.2 %collective-permute-start.20 = (f32[2,1,128]{2,1,0:T(1,128)S(1)}, f32[2,1,128]{2,1,0:T(1,128)S(1)}, u32[]{:S(2)}, u32[]{:S(2)}) collective-permute-start(f32[2,1,128]{2,1,0:T(1,128)S(1)} %fusion.2), channel_id=1, source_target_pairs={{0,4},{1,5},{2,6},{3,7},{4,0},{5,1},{6,2},{7,3},{8,12},{9,13},{10,... | collective-permute-start | bytes 3080 | tf_op jit(solution)/shard_map/ppermute | solution.py:377
  106.6 2.3 %collective-permute-done.20 = f32[2,1,128]{2,1,0:T(1,128)S(1)} collective-permute-done((f32[2,1,128]{2,1,0:T(1,128)S(1)}, f32[2,1,128]{2,1,0:T(1,128)S(1)}, u32[]{:S(2)}, u32[]{:S(2)}) %collective-permute-start.20) | collective-permute-done | bytes 1056 | tf_op jit(solution)/shard_map/ppermute | solution.py:377
  109.0 2.3 %collective-permute-start.21 = (f32[2,1,128]{2,1,0:T(1,128)S(1)}, f32[2,1,128]{2,1,0:T(1,128)S(1)}, u32[]{:S(2)}, u32[]{:S(2)}) collective-permute-start(f32[2,1,128]{2,1,0:T(1,128)S(1)} %add.16), channel_id=1, source_target_pairs={{0,8},{1,9},{2,10},{3,11},{4,12},{5,13},{6,14},{7,15},{8,0},{9,1},... | collective-permute-start | bytes 3080 | tf_op jit(solution)/shard_map/ppermute | solution.py:377
  111.2 2.2 %collective-permute-done.21 = f32[2,1,128]{2,1,0:T(1,128)S(1)} collective-permute-done((f32[2,1,128]{2,1,0:T(1,128)S(1)}, f32[2,1,128]{2,1,0:T(1,128)S(1)}, u32[]{:S(2)}, u32[]{:S(2)}) %collective-permute-start.21) | collective-permute-done | bytes 1056 | tf_op jit(solution)/shard_map/ppermute | solution.py:377
  113.4 0.6 slice_add_fusion
  (7 shorter events, 0.1 us)
Async XLA Ops:
  2.7 20.8 %collective-permute-start.8 = (bf16[128,3072]{1,0:T(8,128)(2,1)}, bf16[128,3072]{1,0:T(8,128)(2,1)S(1)}, u32[]{:S(2)}, u32[]{:S(2)}) collective-permute-start(bf16[128,3072]{1,0:T(8,128)(2,1)} %get-tuple-element.20), channel_id=1, source_target_pairs={{0,16},{16,0},{1,17},{17,1},{2,18},{18,2},{3,19},{19,3},{4,20},{20... | collective-permute-start | bytes 2359304 | tf_op jit(solution)/shard_map/ppermute | solution.py:151
  5.8 22.6 %collective-permute-start.1 = (bf16[24,19712]{1,0:T(8,128)(2,1)}, bf16[24,19712]{1,0:T(8,128)(2,1)S(1)}, u32[]{:S(2)}, u32[]{:S(2)}) collective-permute-start(bf16[24,19712]{1,0:T(8,128)(2,1)} %get-tuple-element.19.refs_2_.refs_0_), channel_id=1, source_target_pairs={{4,0},{8,4},{12,8},{14,12},{10,14},{6,10},{2,6},{0,2},{5,1},{9,5},... | collective-permute-start | bytes 2838536 | tf_op jit(solution)/shard_map/ppermute | solution.py:157
  7.3 22.6 %collective-permute-start = (bf16[24,19712]{1,0:T(8,128)(2,1)}, bf16[24,19712]{1,0:T(8,128)(2,1)S(1)}, u32[]{:S(2)}, u32[]{:S(2)}) collective-permute-start(bf16[24,19712]{1,0:T(8,128)(2,1)} %get-tuple-element.19.refs_2_.refs_0_), channel_id=1, source_target_pairs={{0,4},{4,8},{8,12},{12,14},{14,10},{10,6},{6,2},{2,0},{1,5},{5,9},... | collective-permute-start | bytes 2838536 | tf_op jit(solution)/shard_map/ppermute | solution.py:154
  7.8 75.6 %collective-permute-start.15 = (bf16[2,128,8192]{2,1,0:T(8,128)(2,1)}, bf16[2,128,8192]{2,1,0:T(8,128)(2,1)}, u32[]{:S(2)}, u32[]{:S(2)}) collective-permute-start(bf16[2,128,8192]{2,1,0:T(8,128)(2,1)} %refs_16_.1), channel_id=1, source_target_pairs={{0,1},{1,0},{2,3},{3,2},{4,5},{5,4},{6,7},{7,6},{8,9},{9,8},{10,11... | collective-permute-start | bytes 12582920 | tf_op jit(solution)/shard_map/ppermute | solution.py:148
  23.5 20.5 %copy-start.6 = (bf16[128,3072]{1,0:T(8,128)(2,1)}, bf16[128,3072]{1,0:T(8,128)(2,1)S(1)}, u32[]{:S(2)}) copy-start(bf16[128,3072]{1,0:T(8,128)(2,1)S(1)} %collective-permute-done.8.refs_10_) | copy-start | bytes 2359300
  23.5 19.0 %collective-permute-start.10 = (bf16[128,3072]{1,0:T(8,128)(2,1)}, bf16[128,3072]{1,0:T(8,128)(2,1)}, u32[]{:S(2)}, u32[]{:S(2)}) collective-permute-start(bf16[128,3072]{1,0:T(8,128)(2,1)} %get-tuple-element.22), channel_id=1, source_target_pairs={{0,16},{16,0},{1,17},{17,1},{2,18},{18,2},{3,19},{19,3},{4,20},{20... | collective-permute-start | bytes 2359304 | tf_op jit(solution)/shard_map/ppermute | solution.py:151
  25.3 63.1 %collective-permute-start.7 = (bf16[2,128,8192]{2,1,0:T(8,128)(2,1)}, bf16[2,128,8192]{2,1,0:T(8,128)(2,1)}, u32[]{:S(2)}, u32[]{:S(2)}) collective-permute-start(bf16[2,128,8192]{2,1,0:T(8,128)(2,1)} %refs_8_.1), channel_id=1, source_target_pairs={{0,1},{1,0},{2,3},{3,2},{4,5},{5,4},{6,7},{7,6},{8,9},{9,8},{10,11... | collective-permute-start | bytes 12582920 | tf_op jit(solution)/shard_map/ppermute | solution.py:148
  28.4 44.0 %copy-start.2 = (bf16[24,19712]{1,0:T(8,128)(2,1)}, bf16[24,19712]{1,0:T(8,128)(2,1)S(1)}, u32[]{:S(2)}) copy-start(bf16[24,19712]{1,0:T(8,128)(2,1)S(1)} %collective-permute-done.1.refs_4_.refs_2_) | copy-start | bytes 2838532
  28.4 21.5 %collective-permute-start.3 = (bf16[24,19712]{1,0:T(8,128)(2,1)S(1)}, bf16[24,19712]{1,0:T(8,128)(2,1)S(1)}, u32[]{:S(2)}, u32[]{:S(2)}) collective-permute-start(bf16[24,19712]{1,0:T(8,128)(2,1)S(1)} %collective-permute-done.1.refs_4_.refs_2_), channel_id=1, source_target_pairs={{4,0},{8,4},{12,8},{14,12},{10,14},{6,10},{2,6},{0,2},{5,1},{9,5},... | collective-permute-start | bytes 2838536 | tf_op jit(solution)/shard_map/ppermute | solution.py:157
  29.9 42.5 %copy-start.3 = (bf16[24,19712]{1,0:T(8,128)(2,1)}, bf16[24,19712]{1,0:T(8,128)(2,1)S(1)}, u32[]{:S(2)}) copy-start(bf16[24,19712]{1,0:T(8,128)(2,1)S(1)} %collective-permute-done.refs_3_.refs_1_) | copy-start | bytes 2838532
  29.9 21.5 %collective-permute-start.2 = (bf16[24,19712]{1,0:T(8,128)(2,1)S(1)}, bf16[24,19712]{1,0:T(8,128)(2,1)S(1)}, u32[]{:S(2)}, u32[]{:S(2)}) collective-permute-start(bf16[24,19712]{1,0:T(8,128)(2,1)S(1)} %collective-permute-done.refs_3_.refs_1_), channel_id=1, source_target_pairs={{0,4},{4,8},{8,12},{12,14},{14,10},{10,6},{6,2},{2,0},{1,5},{5,9},... | collective-permute-start | bytes 2838536 | tf_op jit(solution)/shard_map/ppermute | solution.py:154
  42.6 39.5 %collective-permute-start.12 = (bf16[128,6912]{1,0:T(8,128)(2,1)}, bf16[128,6912]{1,0:T(8,128)(2,1)}, u32[]{:S(2)}, u32[]{:S(2)}) collective-permute-start(bf16[128,6912]{1,0:T(8,128)(2,1)} %get-tuple-element.24), channel_id=1, source_target_pairs={{0,16},{16,0},{1,17},{17,1},{2,18},{18,2},{3,19},{19,3},{4,20},{20... | collective-permute-start | bytes 5308424 | tf_op jit(solution)/shard_map/ppermute | solution.py:151
  49.9 1.5 %copy-start.4 = (bf16[24,19712]{1,0:T(8,128)(2,1)}, bf16[24,19712]{1,0:T(8,128)(2,1)S(1)}, u32[]{:S(2)}) copy-start(bf16[24,19712]{1,0:T(8,128)(2,1)S(1)} %collective-permute-done.3.refs_6_.refs_4_) | copy-start | bytes 2838532
  49.9 20.9 %collective-permute-start.5 = (bf16[24,19712]{1,0:T(8,128)(2,1)S(1)}, bf16[24,19712]{1,0:T(8,128)(2,1)S(1)}, u32[]{:S(2)}, u32[]{:S(2)}) collective-permute-start(bf16[24,19712]{1,0:T(8,128)(2,1)S(1)} %collective-permute-done.3.refs_6_.refs_4_), channel_id=1, source_target_pairs={{4,0},{8,4},{12,8},{14,12},{10,14},{6,10},{2,6},{0,2},{5,1},{9,5},... | collective-permute-start | bytes 2838536 | tf_op jit(solution)/shard_map/ppermute | solution.py:157
  51.4 30.6 %copy-start.5 = (bf16[24,19712]{1,0:T(8,128)(2,1)}, bf16[24,19712]{1,0:T(8,128)(2,1)S(1)}, u32[]{:S(2)}) copy-start(bf16[24,19712]{1,0:T(8,128)(2,1)S(1)} %collective-permute-done.2.refs_5_.refs_3_) | copy-start | bytes 2838532
  51.4 21.0 %collective-permute-start.4 = (bf16[24,19712]{1,0:T(8,128)(2,1)S(1)}, bf16[24,19712]{1,0:T(8,128)(2,1)S(1)}, u32[]{:S(2)}, u32[]{:S(2)}) collective-permute-start(bf16[24,19712]{1,0:T(8,128)(2,1)S(1)} %collective-permute-done.2.refs_5_.refs_3_), channel_id=1, source_target_pairs={{0,4},{4,8},{8,12},{12,14},{14,10},{10,6},{6,2},{2,0},{1,5},{5,9},... | collective-permute-start | bytes 2838536 | tf_op jit(solution)/shard_map/ppermute | solution.py:154
  70.9 12.5 %copy-start = (bf16[24,19712]{1,0:T(8,128)(2,1)}, bf16[24,19712]{1,0:T(8,128)(2,1)S(1)}, u32[]{:S(2)}) copy-start(bf16[24,19712]{1,0:T(8,128)(2,1)S(1)} %collective-permute-done.5.refs_8_.refs_6_) | copy-start | bytes 2838532
  70.9 9.9 %collective-permute-start.13 = (bf16[24,9856]{1,0:T(8,128)(2,1)S(1)}, bf16[24,9856]{1,0:T(8,128)(2,1)S(1)}, u32[]{:S(2)}, u32[]{:S(2)}) collective-permute-start(bf16[24,9856]{1,0:T(8,128)(2,1)S(1)} %slice.13), channel_id=1, source_target_pairs={{4,0},{8,4},{12,8},{14,12},{10,14},{6,10},{2,6},{0,2},{5,1},{9,5},... | collective-permute-start | bytes 1419272 | tf_op jit(solution)/shard_map/ppermute | solution.py:157
  72.4 9.6 %copy-start.1 = (bf16[24,19712]{1,0:T(8,128)(2,1)}, bf16[24,19712]{1,0:T(8,128)(2,1)S(1)}, u32[]{:S(2)}) copy-start(bf16[24,19712]{1,0:T(8,128)(2,1)S(1)} %collective-permute-done.4.refs_7_.refs_5_) | copy-start | bytes 2838532
  72.5 9.5 %collective-permute-start.6 = (bf16[24,9856]{1,0:T(8,128)(2,1)S(1)}, bf16[24,9856]{1,0:T(8,128)(2,1)S(1)}, u32[]{:S(2)}, u32[]{:S(2)}) collective-permute-start(bf16[24,9856]{1,0:T(8,128)(2,1)S(1)} %slice.12), channel_id=1, source_target_pairs={{0,4},{4,8},{8,12},{12,14},{14,10},{10,6},{6,2},{2,0},{1,5},{5,9},... | collective-permute-start | bytes 1419272 | tf_op jit(solution)/shard_map/ppermute | solution.py:154
  82.0 6.4 %collective-permute-start.14 = (bf16[128,6912]{1,0:T(8,128)(2,1)}, bf16[128,6912]{1,0:T(8,128)(2,1)}, u32[]{:S(2)}, u32[]{:S(2)}) collective-permute-start(bf16[128,6912]{1,0:T(8,128)(2,1)} %collective-permute-done.12.refs_14_), channel_id=1, source_target_pairs={{0,1},{1,0},{2,3},{3,2},{4,5},{5,4},{6,7},{7,6},{8,9},{9,8},{10,11... | collective-permute-start | bytes 5308424 | tf_op jit(solution)/shard_map/ppermute | solution.py:148
  82.1 5.5 %collective-permute-start.9 = (bf16[128,3072]{1,0:T(8,128)(2,1)}, bf16[128,3072]{1,0:T(8,128)(2,1)}, u32[]{:S(2)}, u32[]{:S(2)}) collective-permute-start(bf16[128,3072]{1,0:T(8,128)(2,1)} %copy-done.6), channel_id=1, source_target_pairs={{0,1},{1,0},{2,3},{3,2},{4,5},{5,4},{6,7},{7,6},{8,9},{9,8},{10,11... | collective-permute-start | bytes 2359304 | tf_op jit(solution)/shard_map/ppermute | solution.py:148
  82.6 5.8 %collective-permute-start.11 = (bf16[128,3072]{1,0:T(8,128)(2,1)}, bf16[128,3072]{1,0:T(8,128)(2,1)}, u32[]{:S(2)}, u32[]{:S(2)}) collective-permute-start(bf16[128,3072]{1,0:T(8,128)(2,1)} %collective-permute-done.10.refs_12_), channel_id=1, source_target_pairs={{0,1},{1,0},{2,3},{3,2},{4,5},{5,4},{6,7},{7,6},{8,9},{9,8},{10,11... | collective-permute-start | bytes 2359304 | tf_op jit(solution)/shard_map/ppermute | solution.py:148
  86.9 9.6 %collective-permute-start.16 = (f32[256,256]{1,0:T(8,128)S(1)}, f32[256,256]{1,0:T(8,128)S(1)}, u32[]{:S(2)}, u32[]{:S(2)}) collective-permute-start(f32[256,256]{1,0:T(8,128)S(1)} %get-tuple-element.30), channel_id=1, source_target_pairs={{0,16},{16,0},{1,17},{17,1},{2,18},{18,2},{3,19},{19,3},{4,20},{20... | collective-permute-start | bytes 786440 | tf_op jit(solution)/shard_map/ppermute | solution.py:151
  96.9 3.5 %collective-permute-start.17 = (f32[1,128]{1,0:T(1,128)S(1)}, f32[1,128]{1,0:T(1,128)S(1)}, u32[]{:S(2)}, u32[]{:S(2)}) collective-permute-start(f32[1,128]{1,0:T(1,128)S(1)} %get-tuple-element.32), channel_id=1, source_target_pairs={{0,16},{16,0},{1,17},{17,1},{2,18},{18,2},{3,19},{19,3},{4,20},{20... | collective-permute-start | bytes 1544 | tf_op jit(solution)/shard_map/ppermute | solution.py:151
  100.5 1.1 %collective-permute-start.18 = (f32[2,1,128]{2,1,0:T(1,128)S(1)}, f32[2,1,128]{2,1,0:T(1,128)S(1)}, u32[]{:S(2)}, u32[]{:S(2)}) collective-permute-start(f32[2,1,128]{2,1,0:T(1,128)S(1)} %fusion), channel_id=1, source_target_pairs={{0,1},{1,0},{2,3},{3,2},{4,5},{5,4},{6,7},{7,6},{8,9},{9,8},{10,11... | collective-permute-start | bytes 3080 | tf_op jit(solution)/shard_map/ppermute | solution.py:377
  101.8 3.6 %collective-permute-start.19 = (f32[2,1,128]{2,1,0:T(1,128)S(1)}, f32[2,1,128]{2,1,0:T(1,128)S(1)}, u32[]{:S(2)}, u32[]{:S(2)}) collective-permute-start(f32[2,1,128]{2,1,0:T(1,128)S(1)} %fusion.1), channel_id=1, source_target_pairs={{0,2},{1,3},{2,0},{3,1},{4,6},{5,7},{6,4},{7,5},{8,10},{9,11},{10,... | collective-permute-start | bytes 3080 | tf_op jit(solution)/shard_map/ppermute | solution.py:377
  105.4 3.6 %collective-permute-start.20 = (f32[2,1,128]{2,1,0:T(1,128)S(1)}, f32[2,1,128]{2,1,0:T(1,128)S(1)}, u32[]{:S(2)}, u32[]{:S(2)}) collective-permute-start(f32[2,1,128]{2,1,0:T(1,128)S(1)} %fusion.2), channel_id=1, source_target_pairs={{0,4},{1,5},{2,6},{3,7},{4,0},{5,1},{6,2},{7,3},{8,12},{9,13},{10,... | collective-permute-start | bytes 3080 | tf_op jit(solution)/shard_map/ppermute | solution.py:377
  109.0 4.5 %collective-permute-start.21 = (f32[2,1,128]{2,1,0:T(1,128)S(1)}, f32[2,1,128]{2,1,0:T(1,128)S(1)}, u32[]{:S(2)}, u32[]{:S(2)}) collective-permute-start(f32[2,1,128]{2,1,0:T(1,128)S(1)} %add.16), channel_id=1, source_target_pairs={{0,8},{1,9},{2,10},{3,11},{4,12},{5,13},{6,14},{7,15},{8,0},{9,1},... | collective-permute-start | bytes 3080 | tf_op jit(solution)/shard_map/ppermute | solution.py:377

commit v8 on v7

--- a/solution.py
+++ b/solution.py
@@ -163,7 +163,7 @@
         tokens_here = activations.shape[1]
         width = backprops.shape[2]
         depth = activations.shape[2]
-        cut = depth * 19 // 32
+        cut = depth * 37 // 64
         packed = width + cut
         beyond = depth - cut
         columns = out_factors.shape[1]
@@ -209,7 +209,7 @@
             got += [ahead, back]
         away_sib = [swap_core(x) for x in away[:2]]
         total = packed + 2 * beyond
-        middle = total // 2
+        middle = total // 256 * 128 - 128
         chip_tokens = 2 * tokens_here
         shard_rows = chips * columns
         if chips > 8:

time: 114 us -> 117 us (1.026)
  waiting for transfers between devices: 71.9 us -> 75.6 us
    ppermute x5, waiting for transfers between devices: 27.5 us -> 37.5 us  [swap_grp(): return lax.ppermute(x, 'grp', [(0, 1), (1, 0)])]
    ppermute x4, waiting for transfers between devices: 34.8 us -> 25.7 us  [back_of(): return lax.ppermute(x, 'blk', backward)]
    ppermute x4, waiting for transfers between devices: 1.27 us -> 3.48 us  [ahead_of(): return lax.ppermute(x, 'blk', forward)]
    ppermute x5, starting transfers between devices: 7.71 us -> 5.77 us  [swap_grp(): return lax.ppermute(x, 'grp', [(0, 1), (1, 0)])]
    ppermute x4, starting transfers between devices: 6.02 us -> 7.49 us  [back_of(): return lax.ppermute(x, 'blk', backward)]
  transfers between devices with their start and end apart: 22 -> 22, of which waited for: 13 -> 14; matrix products, arithmetic and copies ran while one was open for 0% -> 0% of each run, Pallas kernels for 13% -> 13%
where the time goes in v8:
time: 117 us
  waiting for transfers between devices  75.6 us (65%)
  starting transfers between devices  21.4 us (18%)
  Pallas kernels  18 us (15%)
    ppermute x5, waiting for transfers between devices, swap_grp(): return lax.ppermute(x, 'grp', [(0, 1), (1, 0)])  37.5 us
    ppermute x4, waiting for transfers between devices, back_of(): return lax.ppermute(x, 'blk', backward)  25.7 us
    pallas_call x1, Pallas kernels, shards(): pl.pallas_call(main_kernel, out_shape=[proj] * 2, in_specs=[ANYWHERE] * c...  7.99 us
    ppermute x4, waiting for transfers between devices, shards(): lax.ppermute(value, 'blk', [(i, i ^ bit) for i in range(blk)])  7.75 us
    ppermute x4, starting transfers between devices, back_of(): return lax.ppermute(x, 'blk', backward)  7.49 us
    pallas_call x2, Pallas kernels, move(): pl.pallas_call(kernel, out_shape=shapes, in_specs=[ANYWHERE] * (count + l...  5.84 us
    ppermute x5, starting transfers between devices, swap_grp(): return lax.ppermute(x, 'grp', [(0, 1), (1, 0)])  5.77 us
    ppermute x4, starting transfers between devices, shards(): lax.ppermute(value, 'blk', [(i, i ^ bit) for i in range(blk)])  5 us
  transfers between devices with their start and end apart: 22, of which 14 were waited for; matrix products, arithmetic and copies ran while one was open for 0% of the time, Pallas kernels for 13%

profile of v8, /device:TPU:0, one launch (start us, length us, event | category | flops | bytes accessed | tf_op | source)
XLA Modules:
  0.0 116.6 jit_solution(2402657075113705035)
XLA Ops:
  0.0 2.7 %shard_map.55 = (bf16[24,19840]{1,0:T(8,128)(2,1)}, bf16[128,3072]{1,0:T(8,128)(2,1)}) custom-call(bf16[2,128,8192]{2,1,0:T(8,128)(2,1)} %refs_16_.1, bf16[2,128,8192]{2,1,0:T(8,128)(2,1)} %refs_8_.1, bf16[2,24,8192]{2,1,0:T(8,128)(2,1)} %refs_2_.1, bf16[2,24,8192]{2,1,0:T(8,128)(2,1)} %refs_3_.1), custom_call_target="tpu_custom_call" | custom-call | bytes 6955008 | tf_op jit(solution)/shard_map/pallas_call | solution.py:63
  2.7 3.0 %collective-permute-start.1 = (bf16[24,19840]{1,0:T(8,128)(2,1)}, bf16[24,19840]{1,0:T(8,128)(2,1)S(1)}, u32[]{:S(2)}, u32[]{:S(2)}) collective-permute-start(bf16[24,19840]{1,0:T(8,128)(2,1)} %get-tuple-element.19.refs_2_.refs_0_), channel_id=1, source_target_pairs={{4,0},{8,4},{12,8},{14,12},{10,14},{6,10},{2,6},{0,2},{5,1},{9,5},... | collective-permute-start | bytes 2856968 | tf_op jit(solution)/shard_map/ppermute | solution.py:157
  5.7 0.1 collective-permute-start
  5.9 1.9 %collective-permute-start.8 = (bf16[128,3072]{1,0:T(8,128)(2,1)}, bf16[128,3072]{1,0:T(8,128)(2,1)S(1)}, u32[]{:S(2)}, u32[]{:S(2)}) collective-permute-start(bf16[128,3072]{1,0:T(8,128)(2,1)} %get-tuple-element.20), channel_id=1, source_target_pairs={{0,16},{16,0},{1,17},{17,1},{2,18},{18,2},{3,19},{19,3},{4,20},{20... | collective-permute-start | bytes 2359304 | tf_op jit(solution)/shard_map/ppermute | solution.py:151
  7.8 0.0 collective-permute-start.15
  7.8 3.1 %shard_map.56 = (bf16[128,3072]{1,0:T(8,128)(2,1)}, bf16[128,6784]{1,0:T(8,128)(2,1)}) custom-call(bf16[2,128,8192]{2,1,0:T(8,128)(2,1)} %refs_16_.1, bf16[2,128,8192]{2,1,0:T(8,128)(2,1)} %refs_8_.1, bf16[24,19840]{1,0:T(8,128)(2,1)} %get-tuple-element.19.refs_2_.refs_0_), custom_call_target="tpu_custom_call" | custom-call | bytes 10092544 | tf_op jit(solution)/shard_map/pallas_call | solution.py:63
  10.9 14.2 %collective-permute-done.8.refs_10_ = bf16[128,3072]{1,0:T(8,128)(2,1)S(1)} collective-permute-done((bf16[128,3072]{1,0:T(8,128)(2,1)}, bf16[128,3072]{1,0:T(8,128)(2,1)S(1)}, u32[]{:S(2)}, u32[]{:S(2)}) %collective-permute-start.8) | collective-permute-done | bytes 786464 | tf_op jit(solution)/shard_map/ppermute | solution.py:151
  25.1 0.0 copy-start.6
  25.1 1.6 %collective-permute-start.10 = (bf16[128,3072]{1,0:T(8,128)(2,1)}, bf16[128,3072]{1,0:T(8,128)(2,1)}, u32[]{:S(2)}, u32[]{:S(2)}) collective-permute-start(bf16[128,3072]{1,0:T(8,128)(2,1)} %get-tuple-element.22), channel_id=1, source_target_pairs={{0,16},{16,0},{1,17},{17,1},{2,18},{18,2},{3,19},{19,3},{4,20},{20... | collective-permute-start | bytes 2359304 | tf_op jit(solution)/shard_map/ppermute | solution.py:151
  26.7 0.0 collective-permute-start.7
  26.7 0.4 collective-permute-done.1.refs_4_.refs_2_
  27.1 0.0 copy-start.2
  27.1 1.7 %collective-permute-start.3 = (bf16[24,19840]{1,0:T(8,128)(2,1)S(1)}, bf16[24,19840]{1,0:T(8,128)(2,1)S(1)}, u32[]{:S(2)}, u32[]{:S(2)}) collective-permute-start(bf16[24,19840]{1,0:T(8,128)(2,1)S(1)} %collective-permute-done.1.refs_4_.refs_2_), channel_id=1, source_target_pairs={{4,0},{8,4},{12,8},{14,12},{10,14},{6,10},{2,6},{0,2},{5,1},{9,5},... | collective-permute-start | bytes 2856968 | tf_op jit(solution)/shard_map/ppermute | solution.py:157
  28.8 0.0 collective-permute-done.refs_3_.refs_1_
  28.8 0.0 copy-start.3
  28.8 0.4 collective-permute-start.2
  29.1 14.3 %collective-permute-done.10.refs_12_ = bf16[128,3072]{1,0:T(8,128)(2,1)} collective-permute-done((bf16[128,3072]{1,0:T(8,128)(2,1)}, bf16[128,3072]{1,0:T(8,128)(2,1)}, u32[]{:S(2)}, u32[]{:S(2)}) %collective-permute-start.10) | collective-permute-done | bytes 786464 | tf_op jit(solution)/shard_map/ppermute | solution.py:151
  43.5 1.3 %collective-permute-start.12 = (bf16[128,6784]{1,0:T(8,128)(2,1)}, bf16[128,6784]{1,0:T(8,128)(2,1)}, u32[]{:S(2)}, u32[]{:S(2)}) collective-permute-start(bf16[128,6784]{1,0:T(8,128)(2,1)} %get-tuple-element.24), channel_id=1, source_target_pairs={{0,16},{16,0},{1,17},{17,1},{2,18},{18,2},{3,19},{19,3},{4,20},{20... | collective-permute-start | bytes 5210120 | tf_op jit(solution)/shard_map/ppermute | solution.py:151
  44.8 0.0 copy-done.6
  44.8 5.4 %collective-permute-done.3.refs_6_.refs_4_ = bf16[24,19840]{1,0:T(8,128)(2,1)S(1)} collective-permute-done((bf16[24,19840]{1,0:T(8,128)(2,1)S(1)}, bf16[24,19840]{1,0:T(8,128)(2,1)S(1)}, u32[]{:S(2)}, u32[]{:S(2)}) %collective-permute-start.3) | collective-permute-done | bytes 952352 | tf_op jit(solution)/shard_map/ppermute | solution.py:157
  50.2 1.5 %collective-permute-start.5 = (bf16[24,19840]{1,0:T(8,128)(2,1)S(1)}, bf16[24,19840]{1,0:T(8,128)(2,1)S(1)}, u32[]{:S(2)}, u32[]{:S(2)}) collective-permute-start(bf16[24,19840]{1,0:T(8,128)(2,1)S(1)} %collective-permute-done.3.refs_6_.refs_4_), channel_id=1, source_target_pairs={{4,0},{8,4},{12,8},{14,12},{10,14},{6,10},{2,6},{0,2},{5,1},{9,5},... | collective-permute-start | bytes 2856968 | tf_op jit(solution)/shard_map/ppermute | solution.py:157
  51.7 0.0 collective-permute-done.2.refs_5_.refs_3_
  51.7 0.0 copy-done.4
  51.7 1.0 collective-permute-start.4
  52.7 19.9 %collective-permute-done.5.refs_8_.refs_6_ = bf16[24,19840]{1,0:T(8,128)(2,1)S(1)} collective-permute-done((bf16[24,19840]{1,0:T(8,128)(2,1)S(1)}, bf16[24,19840]{1,0:T(8,128)(2,1)S(1)}, u32[]{:S(2)}, u32[]{:S(2)}) %collective-permute-start.5) | collective-permute-done | bytes 952352 | tf_op jit(solution)/shard_map/ppermute | solution.py:157
  72.6 1.4 %collective-permute-start.13 = (bf16[24,10112]{1,0:T(8,128)(2,1)S(1)}, bf16[24,10112]{1,0:T(8,128)(2,1)S(1)}, u32[]{:S(2)}, u32[]{:S(2)}) collective-permute-start(bf16[24,10112]{1,0:T(8,128)(2,1)S(1)} %slice.13), channel_id=1, source_target_pairs={{4,0},{8,4},{12,8},{14,12},{10,14},{6,10},{2,6},{0,2},{5,1},{9,5},... | collective-permute-start | bytes 1456136 | tf_op jit(solution)/shard_map/ppermute | solution.py:157
  74.0 0.0 collective-permute-done.4.refs_7_.refs_5_
  74.0 0.0 copy-done.2
  74.0 0.0 copy-done.3
  74.0 0.0 copy-start.1
  74.1 1.0 collective-permute-start.6
  75.0 6.3 %collective-permute-done.12.refs_14_ = bf16[128,6784]{1,0:T(8,128)(2,1)} collective-permute-done((bf16[128,6784]{1,0:T(8,128)(2,1)}, bf16[128,6784]{1,0:T(8,128)(2,1)}, u32[]{:S(2)}, u32[]{:S(2)}) %collective-permute-start.12) | collective-permute-done | bytes 1736736 | tf_op jit(solution)/shard_map/ppermute | solution.py:151
  81.3 3.5 %collective-permute-done.6.refs_7_ = bf16[24,9728]{1,0:T(8,128)(2,1)S(1)} collective-permute-done((bf16[24,9728]{1,0:T(8,128)(2,1)S(1)}, bf16[24,9728]{1,0:T(8,128)(2,1)S(1)}, u32[]{:S(2)}, u32[]{:S(2)}) %collective-permute-start.6) | collective-permute-done | bytes 466976 | tf_op jit(solution)/shard_map/ppermute | solution.py:154
  84.8 0.0 collective-permute-done.13.refs_9_.refs_10_
  84.8 0.0 copy-done.1
  84.8 0.0 collective-permute-start.14
  84.8 0.0 copy-done.5
  84.8 0.5 collective-permute-start.9
  85.3 0.1 collective-permute-start.11
  86.1 0.0 collective-permute-done.15.refs_1_.refs_17_
  86.1 0.0 copy-done
  86.1 3.7 %shard_map.57 = (f32[256,256]{1,0:T(8,128)S(1)}, f32[256,256]{1,0:T(8,128)S(1)}, bf16[24,3200]{1,0:T(8,128)(2,1)S(1)}) custom-call(bf16[2,128,8192]{2,1,0:T(8,128)(2,1)} %refs_16_.1, bf16[2,128,8192]{2,1,0:T(8,128)(2,1)} %collective-permute-done.15.refs_1_.refs_17_, bf16[24,19840]{1,0:T(8,128)(2,1)} %get-tuple-element.19.refs_2_.refs_0_, ...), custom_call_target="tpu_custom_call" | custom-call | flops 679477248 | bytes 10616832 | tf_op jit(solution)/shard_map/pallas_call | solution.py:273
  89.8 0.1 collective-permute-start.16
  89.9 0.1 collective-permute-done.9.refs_11_
  89.9 1.1 collective-permute-done.11.refs_13_
  91.1 0.0 collective-permute-done.7.refs_9_
  91.1 0.0 collective-permute-done.14.refs_15_
  91.1 8.0 %shard_map.58 = (f32[512,192]{1,0:T(8,128)S(1)}, f32[512,192]{1,0:T(8,128)S(1)}) custom-call(bf16[24,19840]{1,0:T(8,128)(2,1)} %get-tuple-element.19.refs_2_.refs_0_, bf16[24,19840]{1,0:T(8,128)(2,1)} %copy-done.3, bf16[24,19840]{1,0:T(8,128)(2,1)} %copy-done.2, bf16[24,19840]{1,0:T(8,128)(2,1)} %copy-done.5, bf16[24,19840]{1,0:T(8,128)(2,1)} %copy-done.4, ...), custom_call_target="tpu_custom_call" | custom-call | flops 2541748224 | bytes 39714816 | tf_op jit(solution)/shard_map/pallas_call | solution.py:317
  99.1 0.0 collective-permute-done.16.refs_3_
  99.1 0.5 shard_map.59
  99.5 0.8 collective-permute-start.17
  100.4 2.7 %collective-permute-done.17 = f32[1,128]{1,0:T(1,128)S(1)} collective-permute-done((f32[1,128]{1,0:T(1,128)S(1)}, f32[1,128]{1,0:T(1,128)S(1)}, u32[]{:S(2)}, u32[]{:S(2)}) %collective-permute-start.17) | collective-permute-done | bytes 544 | tf_op jit(solution)/shard_map/ppermute | solution.py:151
  103.1 0.1 fusion
  103.2 0.0 collective-permute-start.18
  103.2 1.1 collective-permute-done.18
  104.3 0.1 fusion.1
  104.4 1.6 %collective-permute-start.19 = (f32[2,1,128]{2,1,0:T(1,128)S(1)}, f32[2,1,128]{2,1,0:T(1,128)S(1)}, u32[]{:S(2)}, u32[]{:S(2)}) collective-permute-start(f32[2,1,128]{2,1,0:T(1,128)S(1)} %fusion.1), channel_id=1, source_target_pairs={{0,2},{1,3},{2,0},{3,1},{4,6},{5,7},{6,4},{7,5},{8,10},{9,11},{10,... | collective-permute-start | bytes 3080 | tf_op jit(solution)/shard_map/ppermute | solution.py:377
  106.0 2.0 %collective-permute-done.19 = f32[2,1,128]{2,1,0:T(1,128)S(1)} collective-permute-done((f32[2,1,128]{2,1,0:T(1,128)S(1)}, f32[2,1,128]{2,1,0:T(1,128)S(1)}, u32[]{:S(2)}, u32[]{:S(2)}) %collective-permute-start.19) | collective-permute-done | bytes 1056 | tf_op jit(solution)/shard_map/ppermute | solution.py:377
  107.9 0.1 fusion.2
  108.0 1.2 %collective-permute-start.20 = (f32[2,1,128]{2,1,0:T(1,128)S(1)}, f32[2,1,128]{2,1,0:T(1,128)S(1)}, u32[]{:S(2)}, u32[]{:S(2)}) collective-permute-start(f32[2,1,128]{2,1,0:T(1,128)S(1)} %fusion.2), channel_id=1, source_target_pairs={{0,4},{1,5},{2,6},{3,7},{4,0},{5,1},{6,2},{7,3},{8,12},{9,13},{10,... | collective-permute-start | bytes 3080 | tf_op jit(solution)/shard_map/ppermute | solution.py:377
  109.2 2.4 %collective-permute-done.20 = f32[2,1,128]{2,1,0:T(1,128)S(1)} collective-permute-done((f32[2,1,128]{2,1,0:T(1,128)S(1)}, f32[2,1,128]{2,1,0:T(1,128)S(1)}, u32[]{:S(2)}, u32[]{:S(2)}) %collective-permute-start.20) | collective-permute-done | bytes 1056 | tf_op jit(solution)/shard_map/ppermute | solution.py:377
  111.6 2.2 %collective-permute-start.21 = (f32[2,1,128]{2,1,0:T(1,128)S(1)}, f32[2,1,128]{2,1,0:T(1,128)S(1)}, u32[]{:S(2)}, u32[]{:S(2)}) collective-permute-start(f32[2,1,128]{2,1,0:T(1,128)S(1)} %add.16), channel_id=1, source_target_pairs={{0,8},{1,9},{2,10},{3,11},{4,12},{5,13},{6,14},{7,15},{8,0},{9,1},... | collective-permute-start | bytes 3080 | tf_op jit(solution)/shard_map/ppermute | solution.py:377
  113.8 2.3 %collective-permute-done.21 = f32[2,1,128]{2,1,0:T(1,128)S(1)} collective-permute-done((f32[2,1,128]{2,1,0:T(1,128)S(1)}, f32[2,1,128]{2,1,0:T(1,128)S(1)}, u32[]{:S(2)}, u32[]{:S(2)}) %collective-permute-start.21) | collective-permute-done | bytes 1056 | tf_op jit(solution)/shard_map/ppermute | solution.py:377
  116.1 0.6 slice_add_fusion
  (7 shorter events, 0.1 us)
Async XLA Ops:
  2.7 24.4 %collective-permute-start.1 = (bf16[24,19840]{1,0:T(8,128)(2,1)}, bf16[24,19840]{1,0:T(8,128)(2,1)S(1)}, u32[]{:S(2)}, u32[]{:S(2)}) collective-permute-start(bf16[24,19840]{1,0:T(8,128)(2,1)} %get-tuple-element.19.refs_2_.refs_0_), channel_id=1, source_target_pairs={{4,0},{8,4},{12,8},{14,12},{10,14},{6,10},{2,6},{0,2},{5,1},{9,5},... | collective-permute-start | bytes 2856968 | tf_op jit(solution)/shard_map/ppermute | solution.py:157
  5.7 23.1 %collective-permute-start = (bf16[24,19840]{1,0:T(8,128)(2,1)}, bf16[24,19840]{1,0:T(8,128)(2,1)S(1)}, u32[]{:S(2)}, u32[]{:S(2)}) collective-permute-start(bf16[24,19840]{1,0:T(8,128)(2,1)} %get-tuple-element.19.refs_2_.refs_0_), channel_id=1, source_target_pairs={{0,4},{4,8},{8,12},{12,14},{14,10},{10,6},{6,2},{2,0},{1,5},{5,9},... | collective-permute-start | bytes 2856968 | tf_op jit(solution)/shard_map/ppermute | solution.py:154
  5.9 19.2 %collective-permute-start.8 = (bf16[128,3072]{1,0:T(8,128)(2,1)}, bf16[128,3072]{1,0:T(8,128)(2,1)S(1)}, u32[]{:S(2)}, u32[]{:S(2)}) collective-permute-start(bf16[128,3072]{1,0:T(8,128)(2,1)} %get-tuple-element.20), channel_id=1, source_target_pairs={{0,16},{16,0},{1,17},{17,1},{2,18},{18,2},{3,19},{19,3},{4,20},{20... | collective-permute-start | bytes 2359304 | tf_op jit(solution)/shard_map/ppermute | solution.py:151
  7.8 78.3 %collective-permute-start.15 = (bf16[2,128,8192]{2,1,0:T(8,128)(2,1)}, bf16[2,128,8192]{2,1,0:T(8,128)(2,1)}, u32[]{:S(2)}, u32[]{:S(2)}) collective-permute-start(bf16[2,128,8192]{2,1,0:T(8,128)(2,1)} %refs_16_.1), channel_id=1, source_target_pairs={{0,1},{1,0},{2,3},{3,2},{4,5},{5,4},{6,7},{7,6},{8,9},{9,8},{10,11... | collective-permute-start | bytes 12582920 | tf_op jit(solution)/shard_map/ppermute | solution.py:148
  25.1 19.7 %copy-start.6 = (bf16[128,3072]{1,0:T(8,128)(2,1)}, bf16[128,3072]{1,0:T(8,128)(2,1)S(1)}, u32[]{:S(2)}) copy-start(bf16[128,3072]{1,0:T(8,128)(2,1)S(1)} %collective-permute-done.8.refs_10_) | copy-start | bytes 2359300
  25.1 18.4 %collective-permute-start.10 = (bf16[128,3072]{1,0:T(8,128)(2,1)}, bf16[128,3072]{1,0:T(8,128)(2,1)}, u32[]{:S(2)}, u32[]{:S(2)}) collective-permute-start(bf16[128,3072]{1,0:T(8,128)(2,1)} %get-tuple-element.22), channel_id=1, source_target_pairs={{0,16},{16,0},{1,17},{17,1},{2,18},{18,2},{3,19},{19,3},{4,20},{20... | collective-permute-start | bytes 2359304 | tf_op jit(solution)/shard_map/ppermute | solution.py:151
  26.7 64.4 %collective-permute-start.7 = (bf16[2,128,8192]{2,1,0:T(8,128)(2,1)}, bf16[2,128,8192]{2,1,0:T(8,128)(2,1)}, u32[]{:S(2)}, u32[]{:S(2)}) collective-permute-start(bf16[2,128,8192]{2,1,0:T(8,128)(2,1)} %refs_8_.1), channel_id=1, source_target_pairs={{0,1},{1,0},{2,3},{3,2},{4,5},{5,4},{6,7},{7,6},{8,9},{9,8},{10,11... | collective-permute-start | bytes 12582920 | tf_op jit(solution)/shard_map/ppermute | solution.py:148
  27.1 46.9 %copy-start.2 = (bf16[24,19840]{1,0:T(8,128)(2,1)}, bf16[24,19840]{1,0:T(8,128)(2,1)S(1)}, u32[]{:S(2)}) copy-start(bf16[24,19840]{1,0:T(8,128)(2,1)S(1)} %collective-permute-done.1.refs_4_.refs_2_) | copy-start | bytes 2856964
  27.1 23.1 %collective-permute-start.3 = (bf16[24,19840]{1,0:T(8,128)(2,1)S(1)}, bf16[24,19840]{1,0:T(8,128)(2,1)S(1)}, u32[]{:S(2)}, u32[]{:S(2)}) collective-permute-start(bf16[24,19840]{1,0:T(8,128)(2,1)S(1)} %collective-permute-done.1.refs_4_.refs_2_), channel_id=1, source_target_pairs={{4,0},{8,4},{12,8},{14,12},{10,14},{6,10},{2,6},{0,2},{5,1},{9,5},... | collective-permute-start | bytes 2856968 | tf_op jit(solution)/shard_map/ppermute | solution.py:157
  28.8 45.2 %copy-start.3 = (bf16[24,19840]{1,0:T(8,128)(2,1)}, bf16[24,19840]{1,0:T(8,128)(2,1)S(1)}, u32[]{:S(2)}) copy-start(bf16[24,19840]{1,0:T(8,128)(2,1)S(1)} %collective-permute-done.refs_3_.refs_1_) | copy-start | bytes 2856964
  28.8 22.9 %collective-permute-start.2 = (bf16[24,19840]{1,0:T(8,128)(2,1)S(1)}, bf16[24,19840]{1,0:T(8,128)(2,1)S(1)}, u32[]{:S(2)}, u32[]{:S(2)}) collective-permute-start(bf16[24,19840]{1,0:T(8,128)(2,1)S(1)} %collective-permute-done.refs_3_.refs_1_), channel_id=1, source_target_pairs={{0,4},{4,8},{8,12},{12,14},{14,10},{10,6},{6,2},{2,0},{1,5},{5,9},... | collective-permute-start | bytes 2856968 | tf_op jit(solution)/shard_map/ppermute | solution.py:154
  43.5 37.9 %collective-permute-start.12 = (bf16[128,6784]{1,0:T(8,128)(2,1)}, bf16[128,6784]{1,0:T(8,128)(2,1)}, u32[]{:S(2)}, u32[]{:S(2)}) collective-permute-start(bf16[128,6784]{1,0:T(8,128)(2,1)} %get-tuple-element.24), channel_id=1, source_target_pairs={{0,16},{16,0},{1,17},{17,1},{2,18},{18,2},{3,19},{19,3},{4,20},{20... | collective-permute-start | bytes 5210120 | tf_op jit(solution)/shard_map/ppermute | solution.py:151
  50.2 1.5 %copy-start.4 = (bf16[24,19840]{1,0:T(8,128)(2,1)}, bf16[24,19840]{1,0:T(8,128)(2,1)S(1)}, u32[]{:S(2)}) copy-start(bf16[24,19840]{1,0:T(8,128)(2,1)S(1)} %collective-permute-done.3.refs_6_.refs_4_) | copy-start | bytes 2856964
  50.2 22.4 %collective-permute-start.5 = (bf16[24,19840]{1,0:T(8,128)(2,1)S(1)}, bf16[24,19840]{1,0:T(8,128)(2,1)S(1)}, u32[]{:S(2)}, u32[]{:S(2)}) collective-permute-start(bf16[24,19840]{1,0:T(8,128)(2,1)S(1)} %collective-permute-done.3.refs_6_.refs_4_), channel_id=1, source_target_pairs={{4,0},{8,4},{12,8},{14,12},{10,14},{6,10},{2,6},{0,2},{5,1},{9,5},... | collective-permute-start | bytes 2856968 | tf_op jit(solution)/shard_map/ppermute | solution.py:157
  51.7 33.1 %copy-start.5 = (bf16[24,19840]{1,0:T(8,128)(2,1)}, bf16[24,19840]{1,0:T(8,128)(2,1)S(1)}, u32[]{:S(2)}) copy-start(bf16[24,19840]{1,0:T(8,128)(2,1)S(1)} %collective-permute-done.2.refs_5_.refs_3_) | copy-start | bytes 2856964
  51.7 22.3 %collective-permute-start.4 = (bf16[24,19840]{1,0:T(8,128)(2,1)S(1)}, bf16[24,19840]{1,0:T(8,128)(2,1)S(1)}, u32[]{:S(2)}, u32[]{:S(2)}) collective-permute-start(bf16[24,19840]{1,0:T(8,128)(2,1)S(1)} %collective-permute-done.2.refs_5_.refs_3_), channel_id=1, source_target_pairs={{0,4},{4,8},{8,12},{12,14},{14,10},{10,6},{6,2},{2,0},{1,5},{5,9},... | collective-permute-start | bytes 2856968 | tf_op jit(solution)/shard_map/ppermute | solution.py:154
  72.6 13.5 %copy-start = (bf16[24,19840]{1,0:T(8,128)(2,1)}, bf16[24,19840]{1,0:T(8,128)(2,1)S(1)}, u32[]{:S(2)}) copy-start(bf16[24,19840]{1,0:T(8,128)(2,1)S(1)} %collective-permute-done.5.refs_8_.refs_6_) | copy-start | bytes 2856964
  72.6 12.2 %collective-permute-start.13 = (bf16[24,10112]{1,0:T(8,128)(2,1)S(1)}, bf16[24,10112]{1,0:T(8,128)(2,1)S(1)}, u32[]{:S(2)}, u32[]{:S(2)}) collective-permute-start(bf16[24,10112]{1,0:T(8,128)(2,1)S(1)} %slice.13), channel_id=1, source_target_pairs={{4,0},{8,4},{12,8},{14,12},{10,14},{6,10},{2,6},{0,2},{5,1},{9,5},... | collective-permute-start | bytes 1456136 | tf_op jit(solution)/shard_map/ppermute | solution.py:157
  74.0 10.8 %copy-start.1 = (bf16[24,19840]{1,0:T(8,128)(2,1)}, bf16[24,19840]{1,0:T(8,128)(2,1)S(1)}, u32[]{:S(2)}) copy-start(bf16[24,19840]{1,0:T(8,128)(2,1)S(1)} %collective-permute-done.4.refs_7_.refs_5_) | copy-start | bytes 2856964
  74.1 10.7 %collective-permute-start.6 = (bf16[24,9728]{1,0:T(8,128)(2,1)S(1)}, bf16[24,9728]{1,0:T(8,128)(2,1)S(1)}, u32[]{:S(2)}, u32[]{:S(2)}) collective-permute-start(bf16[24,9728]{1,0:T(8,128)(2,1)S(1)} %slice.12), channel_id=1, source_target_pairs={{0,4},{4,8},{8,12},{12,14},{14,10},{10,6},{6,2},{2,0},{1,5},{5,9},... | collective-permute-start | bytes 1400840 | tf_op jit(solution)/shard_map/ppermute | solution.py:154
  84.8 6.2 %collective-permute-start.14 = (bf16[128,6784]{1,0:T(8,128)(2,1)}, bf16[128,6784]{1,0:T(8,128)(2,1)}, u32[]{:S(2)}, u32[]{:S(2)}) collective-permute-start(bf16[128,6784]{1,0:T(8,128)(2,1)} %collective-permute-done.12.refs_14_), channel_id=1, source_target_pairs={{0,1},{1,0},{2,3},{3,2},{4,5},{5,4},{6,7},{7,6},{8,9},{9,8},{10,11... | collective-permute-start | bytes 5210120 | tf_op jit(solution)/shard_map/ppermute | solution.py:148
  84.8 5.1 %collective-permute-start.9 = (bf16[128,3072]{1,0:T(8,128)(2,1)}, bf16[128,3072]{1,0:T(8,128)(2,1)}, u32[]{:S(2)}, u32[]{:S(2)}) collective-permute-start(bf16[128,3072]{1,0:T(8,128)(2,1)} %copy-done.6), channel_id=1, source_target_pairs={{0,1},{1,0},{2,3},{3,2},{4,5},{5,4},{6,7},{7,6},{8,9},{9,8},{10,11... | collective-permute-start | bytes 2359304 | tf_op jit(solution)/shard_map/ppermute | solution.py:148
  85.3 5.7 %collective-permute-start.11 = (bf16[128,3072]{1,0:T(8,128)(2,1)}, bf16[128,3072]{1,0:T(8,128)(2,1)}, u32[]{:S(2)}, u32[]{:S(2)}) collective-permute-start(bf16[128,3072]{1,0:T(8,128)(2,1)} %collective-permute-done.10.refs_12_), channel_id=1, source_target_pairs={{0,1},{1,0},{2,3},{3,2},{4,5},{5,4},{6,7},{7,6},{8,9},{9,8},{10,11... | collective-permute-start | bytes 2359304 | tf_op jit(solution)/shard_map/ppermute | solution.py:148
  89.8 9.3 %collective-permute-start.16 = (f32[256,256]{1,0:T(8,128)S(1)}, f32[256,256]{1,0:T(8,128)S(1)}, u32[]{:S(2)}, u32[]{:S(2)}) collective-permute-start(f32[256,256]{1,0:T(8,128)S(1)} %get-tuple-element.30), channel_id=1, source_target_pairs={{0,16},{16,0},{1,17},{17,1},{2,18},{18,2},{3,19},{19,3},{4,20},{20... | collective-permute-start | bytes 786440 | tf_op jit(solution)/shard_map/ppermute | solution.py:151
  99.5 3.5 %collective-permute-start.17 = (f32[1,128]{1,0:T(1,128)S(1)}, f32[1,128]{1,0:T(1,128)S(1)}, u32[]{:S(2)}, u32[]{:S(2)}) collective-permute-start(f32[1,128]{1,0:T(1,128)S(1)} %get-tuple-element.32), channel_id=1, source_target_pairs={{0,16},{16,0},{1,17},{17,1},{2,18},{18,2},{3,19},{19,3},{4,20},{20... | collective-permute-start | bytes 1544 | tf_op jit(solution)/shard_map/ppermute | solution.py:151
  103.2 1.1 collective-permute-start.18
  104.4 3.6 %collective-permute-start.19 = (f32[2,1,128]{2,1,0:T(1,128)S(1)}, f32[2,1,128]{2,1,0:T(1,128)S(1)}, u32[]{:S(2)}, u32[]{:S(2)}) collective-permute-start(f32[2,1,128]{2,1,0:T(1,128)S(1)} %fusion.1), channel_id=1, source_target_pairs={{0,2},{1,3},{2,0},{3,1},{4,6},{5,7},{6,4},{7,5},{8,10},{9,11},{10,... | collective-permute-start | bytes 3080 | tf_op jit(solution)/shard_map/ppermute | solution.py:377
  108.0 3.6 %collective-permute-start.20 = (f32[2,1,128]{2,1,0:T(1,128)S(1)}, f32[2,1,128]{2,1,0:T(1,128)S(1)}, u32[]{:S(2)}, u32[]{:S(2)}) collective-permute-start(f32[2,1,128]{2,1,0:T(1,128)S(1)} %fusion.2), channel_id=1, source_target_pairs={{0,4},{1,5},{2,6},{3,7},{4,0},{5,1},{6,2},{7,3},{8,12},{9,13},{10,... | collective-permute-start | bytes 3080 | tf_op jit(solution)/shard_map/ppermute | solution.py:377
  111.6 4.5 %collective-permute-start.21 = (f32[2,1,128]{2,1,0:T(1,128)S(1)}, f32[2,1,128]{2,1,0:T(1,128)S(1)}, u32[]{:S(2)}, u32[]{:S(2)}) collective-permute-start(f32[2,1,128]{2,1,0:T(1,128)S(1)} %add.16), channel_id=1, source_target_pairs={{0,8},{1,9},{2,10},{3,11},{4,12},{5,13},{6,14},{7,15},{8,0},{9,1},... | collective-permute-start | bytes 3080 | tf_op jit(solution)/shard_map/ppermute | solution.py:377
